TPU v7x, 32 devices: a whole 2x2x4 slice. The times are simulated.
32 devices in a mesh: tok: 4 (over z), scol: 4 (over y, x), tcol: 2 (over core).
Axes of the slice: x: 2, y: 2, z: 4, core: 2. Of those that a mesh axis runs over, the one named last changes fastest.
Arguments:
- student: float32 [2048, 4096], P('tok', 'scol'), may hold values from -6 to 6
- teacher: float32 [2048, 4096], P('tok', 'tcol'), may hold values from -6 to 6
- teacher_norm: float32 [1], replicated, may hold values from 65536 to 262144
Outputs:
- student_grad: float32 [2048, 4096], P(('tok', 'tcol'), 'scol')
All inputs are finite; a program needn't handle non-finite values.
Results may differ from a plain program's by a relative error of at most 0.000073.
Values sent between devices are 32-bit elements; how exact they have to be, the bound alone decides.
No kernel may reach another device: no remote copies, remote signals or barrier semaphores. Data moves between devices by JAX's collectives and lax.ppermute only.
A program may use at most 128 MiB of HBM per device.

v0:
```python
import jax
import jax.numpy as jnp
from jax import lax
from jax.sharding import PartitionSpec as P

DS = 4096


def token_contract(left, right):
    return lax.dot_general(
        left,
        right,
        (((0,), (0,)), ((), ())),
        precision=lax.Precision.HIGHEST,
        preferred_element_type=jnp.float32,
    )


def feature_contract(left, right):
    return lax.dot_general(
        left,
        right,
        (((1,), (1,)), ((), ())),
        precision=lax.Precision.HIGHEST,
        preferred_element_type=jnp.float32,
    )


def body(student, teacher, teacher_norm):
    col_index = lax.axis_index("tcol")
    tcol_count = lax.axis_size("tcol")
    tok_rows = student.shape[0]
    local_width = student.shape[1]
    part_width = local_width // tcol_count
    own_slice = lax.dynamic_slice_in_dim(student, col_index * part_width, part_width, 1)
    partner = lax.all_gather(own_slice, "scol", axis=1, tiled=True)
    cov_block = token_contract(student, teacher)
    gram_block = token_contract(student, partner)
    cov_block, gram_block = lax.psum((cov_block, gram_block), "tok")
    local_stats = jnp.stack([jnp.sum(cov_block * cov_block), jnp.sum(gram_block * gram_block)])
    gathered = lax.all_gather(local_stats, ("scol", "tcol"), axis=0, tiled=True)
    totals = jnp.sum(gathered.reshape(-1, 2), axis=0)
    tokens_all = tok_rows * lax.axis_size("tok")
    factor = -2.0 * tokens_all * DS / (jnp.sqrt(totals[1]) * teacher_norm[0])
    gram_ratio = totals[0] / totals[1]
    result = feature_contract(teacher, cov_block) - gram_ratio * feature_contract(
        partner, gram_block
    )
    return lax.psum_scatter(factor * result, "tcol", scatter_dimension=0, tiled=True)


def solution(mesh):
    return jax.shard_map(
        body,
        mesh=mesh,
        in_specs=(P("tok", "scol"), P("tok", "tcol"), P()),
        out_specs=P(("tok", "tcol"), "scol"),
        check_vma=False,
    )
```

profile of v0, /device:TPU:0, one launch (start us, length us, event | category | flops | bytes accessed | tf_op | source)
XLA Modules:
  0.0 722.7 jit_solution(12614459821742080665)
XLA Ops:
  6.5 0.0 copy-start
  6.5 0.0 all-gather.2.cloned.1.call-start
  6.5 1.6 copy-done
  8.1 1.1 constant_dynamic-slice_fusion
  9.2 0.0 all-gather.2.cloned.1.call-update
  9.2 0.0 all-reduce.4.cloned.1.call-start
  9.3 17.1 %fusion.2 = f32[1024,2048]{1,0:T(8,128)} fusion(f32[512,1024]{1,0:T(8,128)S(1)} %copy-done, f32[512,2048]{1,0:T(8,128)} %param.4), kind=kOutput, calls=%fused_computation.8 | convolution fusion | flops 12884901888 | bytes 14680064 | tf_op jit(solution)/shard_map/dot_general | solution.py:10
  26.4 38.4 %all-gather.2.cloned.1.call-done = f32[512,2048]{1,0:T(8,128)} async-done(((f32[512,512]{1,0:T(8,128)}), f32[512,2048]{1,0:T(8,128)}) %all-gather.2.cloned.1.call-update) | async-done | bytes 4194320 | tf_op jit(solution)/shard_map/all_gather | solution.py:36
  64.8 17.1 %convolution_bitcast_fusion = f32[1024,2048]{0,1:T(8,128)} fusion(f32[512,2048]{1,0:T(8,128)} %all-gather.2.cloned.1.call-done, f32[512,1024]{1,0:T(8,128)S(1)} %copy-done), kind=kOutput, calls=%fused_computation.2 | convolution fusion | flops 12884901888 | bytes 14680064 | tf_op jit(solution)/shard_map/dot_general | solution.py:10
  81.9 0.0 copy-start.3
  81.9 0.0 all-reduce.4.cloned.1.call-update
  81.9 0.0 reduce-scatter.2.cloned.1.call-start
  82.0 0.6 copy-done.3
  82.6 0.6 dynamic-slice
  83.8 561.5 %all-reduce.4.cloned.1.call-done = (f32[1024,2048]{0,1:T(8,128)}, f32[1024,2048]{1,0:T(8,128)}) async-done(((f32[1024,2048]{0,1:T(8,128)}, f32[1024,2048]{1,0:T(8,128)}), (f32[1024,2048]{0,1:T(8,128)}, f32[1024,2048]{1,0:T(8,128)})) %all-reduce.4.cloned.1.call-update) | async-done | bytes 16777232 | tf_op jit(solution)/shard_map/psum | solution.py:39
  645.3 0.0 copy-start.1
  645.3 6.4 multiply_reduce_fusion.1
  651.7 0.0 copy-done.1
  651.7 2.7 multiply_reduce_fusion
  654.5 1.4 maximum_dynamic-update-slice_fusion
  656.5 13.6 %all-reduce = f32[16]{0:T(128)S(1)} all-reduce(f32[16]{0:T(128)S(1)} %maximum_dynamic-update-slice_fusion), channel_id=1, replica_groups=mesh['tok'=4,'scol'=4,'tcol'=2] {'scol','tcol'}, use_global_device_ids=true, to_apply=%add | all-reduce | flops 16 | bytes 128
  670.2 0.1 reshape.8
  670.3 0.6 fusion.1
  672.9 0.0 copy-start.2
  672.9 16.5 %fusion.3 = f32[512,1024]{0,1:T(8,128)S(1)} fusion(f32[512,2048]{1,0:T(8,128)} %all-gather.2.cloned.1.call-done, f32[1024,2048]{0,1:T(8,128)} %get-tuple-element.5), kind=kOutput, calls=%fused_computation.9 | convolution fusion | flops 12884901888 | bytes 14680064 | tf_op jit(solution)/shard_map/dot_general | solution.py:20
  689.4 0.0 copy-done.2
  689.4 17.3 %fusion = f32[512,1024]{0,1:T(8,128)} fusion(f32[512,1024]{0,1:T(8,128)S(1)} %fusion.3, f32[1024,2048]{1,0:T(8,128)} %get-tuple-element.6, f32[512,2048]{1,0:T(8,128)S(1)} %copy-done.2, f32[]{:T(128)} %bitcast.6, f32[]{:T(128)} %bitcast.4), kind=kOutput, calls=%fused_computation.4 | convolution fusion | flops 12886474752 | bytes 16777224 | tf_op jit(solution)/shard_map/dot_general | solution.py:20
  706.7 0.0 reduce-scatter.2.cloned.1.call-update
  706.7 6.9 reduce-scatter.2.cloned.1.call-done
  713.6 2.5 copy.7
  (2 shorter events, 0.0 us)
Async XLA Ops:
  6.5 1.6 copy-start
  6.5 58.2 %all-gather.2.cloned.1.call-start = ((), (), s32[]{:S(2)}) async-start(), calls=%async_computation.1 | async-start | bytes 5242880 | tf_op jit(solution)/shard_map/all_gather | solution.py:36
  9.2 636.1 %all-reduce.4.cloned.1.call-start = ((), (), s32[]{:S(2)}) async-start(), calls=%async_computation.3 | async-start | bytes 33554432 | tf_op jit(solution)/shard_map/psum | solution.py:39
  81.9 0.7 copy-start.3
  81.9 631.7 %reduce-scatter.2.cloned.1.call-start = ((), (), s32[]{:S(2)}) async-start(), calls=%async_computation.2 | async-start | bytes 3145728 | tf_op jit(solution)/shard_map/reduce_scatter | solution.py:49
  645.3 6.4 copy-start.1
  672.9 16.5 %copy-start.2 = (f32[512,2048]{1,0:T(8,128)S(1)}, f32[512,2048]{1,0:T(8,128)}, u32[]{:S(2)}) copy-start(f32[512,2048]{1,0:T(8,128)} %param.4) | copy-start | bytes 12582916
Sparse Core Ops, SparseCore 0:
  9.3 55.3 all-gather.1
  82.0 563.2 all-reduce.3
  706.9 6.7 reduce-scatter.1
where the time goes:
time: 723 us
  waiting for transfers between devices  607 us (84%)
  matrix products  68.1 us (9%)
  between operations  16.4 us (2%)
  blocking collectives  13.6 us (2%)
  other arithmetic  10.6 us (1%)
    psum x1, waiting for transfers between devices, body(): cov_block, gram_block = lax.psum((cov_block, gram_block), 'tok')  562 us
    all_gather x1, waiting for transfers between devices, body(): partner = lax.all_gather(own_slice, 'scol', axis=1, tiled=True)  38.4 us
    dot_general x2, matrix products, token_contract(): lax.dot_general(left, right, (((0,), (0,)), ((), ())), precision=lax.Prec...  34.3 us
    dot_general x2, matrix products, feature_contract(): lax.dot_general(left, right, (((1,), (1,)), ((), ())), precision=lax.Prec...  33.8 us
  transfers between devices with their start and end apart: 3, of which 3 were waited for; matrix products, arithmetic and copies ran while one was open for 2% of the time, Pallas kernels for 0%

commit v1 on v0

--- a/solution.py
+++ b/solution.py
@@ -1,9 +1,14 @@
+import math
+
 import jax
 import jax.numpy as jnp
 from jax import lax
+from jax.experimental import pallas as pl
+from jax.experimental.pallas import tpu as pltpu
 from jax.sharding import PartitionSpec as P
 
-DS = 4096
+LIGHT = pl.CostEstimate(flops=0, bytes_accessed=0, transcendentals=0)
+PLANE = ("tok", "scol", "tcol")
 
 
 def token_contract(left, right):
@@ -26,11 +31,12 @@
     )
 
 
-def body(student, teacher, teacher_norm):
+def feature_form(student, teacher, teacher_norm):
     col_index = lax.axis_index("tcol")
     tcol_count = lax.axis_size("tcol")
     tok_rows = student.shape[0]
     local_width = student.shape[1]
+    features = local_width * lax.axis_size("scol")
     part_width = local_width // tcol_count
     own_slice = lax.dynamic_slice_in_dim(student, col_index * part_width, part_width, 1)
     partner = lax.all_gather(own_slice, "scol", axis=1, tiled=True)
@@ -41,7 +47,7 @@
     gathered = lax.all_gather(local_stats, ("scol", "tcol"), axis=0, tiled=True)
     totals = jnp.sum(gathered.reshape(-1, 2), axis=0)
     tokens_all = tok_rows * lax.axis_size("tok")
-    factor = -2.0 * tokens_all * DS / (jnp.sqrt(totals[1]) * teacher_norm[0])
+    factor = -2.0 * tokens_all * features / (jnp.sqrt(totals[1]) * teacher_norm[0])
     gram_ratio = totals[0] / totals[1]
     result = feature_contract(teacher, cov_block) - gram_ratio * feature_contract(
         partner, gram_block
@@ -49,7 +55,396 @@
     return lax.psum_scatter(factor * result, "tcol", scatter_dimension=0, tiled=True)
 
 
+PAIRS = [(0, 1), (1, 0), (2, 3), (3, 2)]
+MIDDLE = [(1, 2), (2, 1)]
+OUTWARD = [(1, 0), (2, 3)]
+INWARD = [(0, 1), (3, 2)]
+FAR = [(2, 0), (1, 3)]
+CORES = [(0, 1), (1, 0)]
+
+
+def chip_shift(shift):
+    return [(c, c ^ shift) for c in range(4)]
+
+
+def device_id(z, y, x, k):
+    return ((z * 2 + y) * 2 + x) * 2 + k
+
+
+def piece_shift(hi, lo):
+    perm = []
+    for z in range(4):
+        for y in range(2):
+            for x in range(2):
+                for k in range(2):
+                    if z in (0, 3):
+                        perm.append((device_id(z, k, x ^ lo, y ^ hi), device_id(z, y, x, k)))
+                    elif hi or lo:
+                        perm.append((device_id(z, y ^ hi, x ^ lo, k), device_id(z, y, x, k)))
+    return perm
+
+
+def split(x):
+    high = x.astype(jnp.bfloat16)
+    return high, (x - high.astype(jnp.float32)).astype(jnp.bfloat16)
+
+
+def dot(left, right, dims):
+    return lax.dot_general(left, right, (dims, ((), ())), preferred_element_type=jnp.float32)
+
+
+def dot_split(left, right, dims):
+    (lh, ll), (rh, rl) = left, right
+    return dot(lh, rh, dims) + dot(lh, rl, dims) + dot(ll, rh, dims)
+
+
+ROWS = ((1,), (1,))
+COLS = ((1,), (0,))
+FLAGS = pl.BlockSpec(memory_space=pltpu.SMEM)
+
+
+def room(args, outs, scratch=0):
+    total = sum(math.prod(a.shape) * a.dtype.itemsize for a in (*args, *outs)) + scratch
+    return pltpu.CompilerParams(vmem_limit_bytes=total + total // 4 + (6 << 20))
+
+
+def call(kernel, flags, args, outs):
+    outs = [jax.ShapeDtypeStruct(o, jnp.float32) for o in outs]
+    whole = pl.BlockSpec(memory_space=pltpu.VMEM)
+    return pl.pallas_call(
+        kernel,
+        out_shape=outs,
+        in_specs=[FLAGS] + [whole] * len(args),
+        out_specs=[whole] * len(outs),
+        compiler_params=room(args, outs),
+        cost_estimate=LIGHT,
+    )(flags, *args)
+
+
+def gram_part(flags, own, pair):
+    half = own.shape[0]
+
+    def kernel(flags_ref, own_ref, first_ref, second_ref, *outs):
+        left = split(own_ref[...])
+        for ref, out_ref in zip((first_ref, second_ref), outs):
+            out_ref[...] = dot_split(left, split(ref[...]), ROWS)
+
+    return call(kernel, flags, [own, *pair], [(half, half)] * 2)
+
+
+def summed(refs, side):
+    return refs[2 * side][...] + refs[2 * side + 1][...]
+
+
+def teacher_parts(flags, teacher, others, keep_split=False):
+    rows, width = teacher[0].shape
+    half = rows // 2
+    flat = [array for other in others for array in (other if isinstance(other, tuple) else (other,))]
+    n = sum((other[0] if isinstance(other, tuple) else other).shape[0] for other in others)
+    step = width // 4
+
+    def kernel(flags_ref, *refs):
+        teacher_refs, other_refs = refs[: len(teacher)], refs[len(teacher) :][: len(flat)]
+        outs = refs[len(teacher) + len(flat) :]
+        edge = flags_ref[1] == 1
+        for i in range(4):
+            at = slice(i * step, (i + 1) * step)
+            taken = iter(other_refs)
+            right = []
+            for other in others:
+                value = next(taken)[:, at]
+                if isinstance(other, tuple):
+                    value = jnp.where(edge, value, next(taken)[:, at])
+                right.append(value)
+            high, low = split(right[0] if len(right) == 1 else jnp.concatenate(right, 0))
+            both = jnp.concatenate([high, low], 0)
+            for out_ref, which in ((outs[1], 1 - flags_ref[0]), (outs[0], flags_ref[0])):
+                mine = pl.ds(pl.multiple_of(which * half, half), half)
+                if len(teacher) == 1:
+                    th, tl = split(teacher_refs[0][mine, at])
+                    if keep_split:
+                        outs[2][mine, at], outs[3][mine, at] = th, tl
+                else:
+                    th, tl = (ref[mine, at] for ref in teacher_refs)
+                part = dot(th, both, ROWS)
+                part = part[:, :n] + part[:, n:] + dot(tl, high, ROWS)
+                if i == 0:
+                    out_ref[...] = part
+                else:
+                    out_ref[...] += part
+
+    whole = pl.BlockSpec(memory_space=pltpu.VMEM)
+    outs = [jax.ShapeDtypeStruct((half, n), jnp.float32)] * 2
+    if keep_split:
+        outs += [jax.ShapeDtypeStruct((rows, width), jnp.bfloat16)] * 2
+    return pl.pallas_call(
+        kernel,
+        out_shape=outs,
+        in_specs=[FLAGS] + [whole] * (len(teacher) + len(flat)),
+        out_specs=[whole] * len(outs),
+        compiler_params=room([*teacher, *flat], outs),
+        cost_estimate=LIGHT,
+    )(flags, *teacher, *flat)
+
+
+def ordered(flags_ref, pieces):
+    lo, hi = flags_ref[2] == 1, flags_ref[3] == 1
+    g00, g01, g10, g11 = pieces
+    a0, a1 = jnp.where(lo, g01, g00), jnp.where(lo, g00, g01)
+    b0, b1 = jnp.where(lo, g11, g10), jnp.where(lo, g10, g11)
+    low, high = jnp.concatenate([a0, a1], 1), jnp.concatenate([b0, b1], 1)
+    return jnp.where(hi, high, low), jnp.where(hi, low, high)
+
+
+def pick(flags_ref, first, second):
+    return jnp.where(flags_ref[1] == 1, first, second)
+
+
+def spread(sum_ref, hsic, gram):
+    row = lax.broadcasted_iota(jnp.int32, sum_ref.shape, 0)
+    return jnp.where(row < 4, hsic, gram)
+
+
+def products_call(kernel, flags, args, out, scratch):
+    outs = [jax.ShapeDtypeStruct(shape, jnp.float32) for shape in (out, (8, 128))]
+    whole = pl.BlockSpec(memory_space=pltpu.VMEM)
+    return pl.pallas_call(
+        kernel,
+        out_shape=outs,
+        in_specs=[FLAGS] + [whole] * len(args),
+        out_specs=[whole] * 2,
+        scratch_shapes=[pltpu.VMEM(scratch, jnp.bfloat16)] * 2,
+        compiler_params=room(args, outs, 4 * math.prod(scratch)),
+        cost_estimate=LIGHT,
+    )(flags, *args)
+
+
+def first_products(flags, ks, s):
+    half, width = s[0].shape
+    chunk = width // 4
+
+    def kernel(flags_ref, *refs):
+        ks_refs, s_refs = refs[:12], refs[12:18]
+        out_ref, sum_ref, high, low = refs[18:]
+        gram = jnp.zeros((1, 1), jnp.float32)
+        for g in range(3):
+            for side in range(2):
+                at = slice((2 * g + side) * half, (2 * g + side + 1) * half)
+                bottom = summed(ks_refs[4 * g : 4 * g + 4], side)
+                high[:, at], low[:, at] = split(bottom)
+                gram = gram + jnp.sum(bottom * bottom, keepdims=True)
+        sum_ref[...] = spread(sum_ref, 0.0, gram)
+        for j in range(4):
+            cols = slice(j * chunk, (j + 1) * chunk)
+            total = 0.0
+            for i in range(6):
+                at = slice(i * half, (i + 1) * half)
+                total = total + dot_split((high[:, at], low[:, at]), split(s_refs[i][:, cols]), COLS)
+            out_ref[:, cols] = total
+
+    args = [part for quad in ks for part in quad] + list(s)
+    return products_call(kernel, flags, args, [half, width], [half, 6 * half])
+
+
+def second_products(flags, own, first, ks, s, products, sums):
+    half, width = s[0].shape
+    chunk = width // 4
+
+    def kernel(flags_ref, *refs):
+        own_refs, first_refs, refs = refs[:4], refs[4:9], refs[9:]
+        ks_refs, s_refs, (prod_ref, before_ref) = refs[:16], refs[16:24], refs[24:26]
+        edge = flags_ref[1] == 1
+        tops = [ordered(flags_ref, [ref[...] for ref in own_refs])]
+        for g in range(2):
+            at = slice(g * half // 2, (g + 1) * half // 2)
+            pieces = [ref[:, at] for ref in first_refs]
+            left, right = ordered(flags_ref, [jnp.where(edge, pieces[4], pieces[0]), *pieces[1:4]])
+            tops.append((jnp.where(edge, left.T, left), jnp.where(edge, right.T, right)))
+        out_ref, sum_ref, high, low = refs[26:]
+        hsic = gram = jnp.zeros((1, 1), jnp.float32)
+        for side in range(2):
+            own, a, b, c = (summed(ks_refs[4 * g : 4 * g + 4], side) for g in range(4))
+            for g, bottom in enumerate((own, a, pick(flags_ref, b, c))):
+                at = slice((2 * g + side) * half, (2 * g + side + 1) * half)
+                top = tops[g][side]
+                high[:, at], low[:, at] = split(top)
+                hsic = hsic + jnp.sum(top * bottom, keepdims=True)
+            at = slice((6 + side) * half, (7 + side) * half)
+            high[:, at], low[:, at] = split(c)
+            gram = gram + jnp.sum(c * c, keepdims=True)
+        sum_ref[...] = before_ref[...] + spread(sum_ref, hsic, gram)
+        for j in range(4):
+            cols = slice(j * chunk, (j + 1) * chunk)
+            upper, lower = 0.0, prod_ref[:, cols]
+            for side in range(2):
+                own, a, b, c = (s_refs[2 * g + side][:, cols] for g in range(4))
+                for g, part in enumerate((own, a, pick(flags_ref, b, c), c)):
+                    at = slice((2 * g + side) * half, (2 * g + side + 1) * half)
+                    part = dot_split((high[:, at], low[:, at]), split(part), COLS)
+                    if g < 3:
+                        upper = upper + part
+                    else:
+                        lower = lower + part
+            out_ref[:half, cols] = upper
+            out_ref[half:, cols] = lower
+
+    args = [*own, *first, *[part for quad in ks for part in quad], *s, products, sums]
+    return products_call(kernel, flags, args, [2 * half, width], [half, 8 * half])
+
+
+def last_sums(flags, pieces, ks_b, ks_c, sums):
+    half = pieces[0].shape[0]
+
+    def kernel(flags_ref, p0, p1, p2, p3, *refs):
+        b_refs, c_refs, (sum_ref, left_ref, right_ref, out_ref) = refs[:4], refs[4:8], refs[8:]
+        tops = ordered(flags_ref, [p[...] for p in (p0, p1, p2, p3)])
+        left_ref[...], right_ref[...] = tops
+        hsic = jnp.zeros((1, 1), jnp.float32)
+        for side in range(2):
+            bottom = pick(flags_ref, summed(c_refs, side), summed(b_refs, side))
+            hsic = hsic + jnp.sum(tops[side] * bottom, keepdims=True)
+        out_ref[...] = sum_ref[...] + spread(out_ref, hsic, 0.0)
+
+    return call(kernel, flags, [*pieces, *ks_b, *ks_c, sums], [(half, half)] * 2 + [(8, 128)])
+
+
+def last_products(flags, kt, s, products):
+    half, width = s[0].shape
+    chunk = width // 4
+
+    def kernel(flags_ref, l_ref, r_ref, bl, br, cl, cr, prod_ref, out_ref):
+        left, right = split(l_ref[...]), split(r_ref[...])
+        for j in range(4):
+            cols = slice(j * chunk, (j + 1) * chunk)
+            total = prod_ref[:half, cols]
+            total = total + dot_split(left, split(pick(flags_ref, cl[:, cols], bl[:, cols])), COLS)
+            total = total + dot_split(right, split(pick(flags_ref, cr[:, cols], br[:, cols])), COLS)
+            out_ref[:, cols] = total
+
+    return call(kernel, flags, [*kt, *s, products], [(half, width)])[0]
+
+
+def finish(flags, upper, products, sums, norm, scale):
+    half, width = upper.shape
+
+    def kernel(flags_ref, up_ref, prod_ref, norm_ref, *refs):
+        total = sum(ref[...] for ref in refs[:-1])
+        hsic, gram = total[0:1, 0:1], total[4:5, 0:1]
+        factor = scale / (jnp.sqrt(gram) * norm_ref[0:1, 0:1])
+        refs[-1][...] = factor * (up_ref[...] - (hsic / gram) * prod_ref[half:, :])
+
+    return call(kernel, flags, [upper, products, norm, *sums], [(half, width)])[0]
+
+
+def token_form(student, teacher, teacher_norm):
+    z = lax.axis_index("tok")
+    c = lax.axis_index("scol")
+    k = lax.axis_index("tcol")
+    rows = student.shape[0]
+    half = rows // 2
+    quarter = rows // 4
+    tokens_all = rows * lax.axis_size("tok")
+    features = student.shape[1] * lax.axis_size("scol")
+    edge = jnp.logical_or(z == 0, z == 3)
+    flags = jnp.stack([k, edge.astype(jnp.int32), c % 2, (c // 2 != k).astype(jnp.int32)])
+    step = lax.optimization_barrier
+
+    def send(x, perm):
+        return lax.ppermute(x, "tok", perm)
+
+    def both_halves(mine):
+        return mine, lax.ppermute(mine, "tcol", CORES)
+
+    def sum_x_y(left, right):
+        left = left + lax.ppermute(left, "scol", chip_shift(1))
+        right = right + lax.ppermute(right, "scol", chip_shift(2))
+        return left, right
+
+    def terms_y_x(left, right):
+        return [
+            left,
+            lax.ppermute(left, "scol", chip_shift(2)),
+            right,
+            lax.ppermute(right, "scol", chip_shift(1)),
+        ]
+
+    def chip_sum(parts):
+        return terms_y_x(*sum_x_y(*parts))
+
+    def swap_rows(kept, away):
+        return kept + lax.ppermute(away, "tcol", CORES)
+
+    def same_plane(piece):
+        return [piece] + [lax.ppermute(piece, "scol", chip_shift(s)) for s in (1, 2, 3)]
+
+    def mixed(piece):
+        return [piece] + [
+            lax.ppermute(piece, PLANE, piece_shift(hi, lo)) for hi, lo in ((0, 1), (1, 0), (1, 1), (0, 0))
+        ]
+
+    s_half = lax.dynamic_slice_in_dim(student, k * half, half, 0)
+    near, mid = send(s_half, PAIRS), send(s_half, MIDDLE)
+    s_own = (s_half, lax.dynamic_slice_in_dim(student, (1 - k) * half, half, 0))
+    ks_own = chip_sum(gram_part(flags, s_half, s_own))
+    t_quarter = lax.dynamic_slice_in_dim(teacher, c * quarter, quarter, 0)
+    kept, away, *t_split = teacher_parts(flags, [teacher], [t_quarter], True)
+    own = swap_rows(kept, away)
+    near, mid, t_quarter, ks_own, own, t_split = step((near, mid, t_quarter, ks_own, own, t_split))
+
+    far_edge, far_mid = send(mid, OUTWARD), send(near, MIDDLE)
+    t_in = send(t_quarter, INWARD)
+    pieces_own = same_plane(own)
+    s_a = both_halves(near)
+    ks_a = chip_sum(gram_part(flags, s_half, s_a))
+    far_edge, far_mid, t_in, mid, t_quarter, s_a, ks_a, pieces_own = step(
+        (far_edge, far_mid, t_in, mid, t_quarter, s_a, ks_a, pieces_own)
+    )
+
+    last_edge, t_cross = send(far_mid, OUTWARD), send(t_in, MIDDLE)
+    s_b = both_halves(jnp.where(edge, far_edge, mid))
+    first = swap_rows(*teacher_parts(flags, t_split, [t_in]))
+    back_in = send(first, OUTWARD)
+    ks_b = chip_sum(gram_part(flags, s_half, s_b))
+    last_edge, t_cross, far_mid, t_quarter, s_b, first, ks_b = step(
+        (last_edge, t_cross, far_mid, t_quarter, s_b, first, ks_b)
+    )
+
+    part = quarter // 2
+    edge_1, mid_1 = send(t_cross[:part], OUTWARD), send(t_quarter[:part], MIDDLE)
+    cross = swap_rows(*teacher_parts(flags, t_split, [t_cross]))
+    back_cross = send(cross, FAR)
+    s_c = both_halves(jnp.where(edge, last_edge, far_mid))
+    part_c = sum_x_y(*gram_part(flags, s_half, s_c))
+    products, sums = first_products(flags, [ks_own, ks_a, ks_b], [*s_own, *s_a, *s_b])
+    edge_1, mid_1, t_cross, t_quarter, back_in, part_c, cross, products, sums = step(
+        (edge_1, mid_1, t_cross, t_quarter, back_in, part_c, cross, products, sums)
+    )
+    edge_2, mid_2 = send(t_cross[part:], OUTWARD), send(t_quarter[part:], MIDDLE)
+    ks_c = terms_y_x(*part_c)
+    pieces_first = mixed(jnp.concatenate([jnp.where(edge, back_in, first), jnp.where(edge, back_cross, cross)], 1))
+    edge_2, mid_2, pieces_first = step((edge_2, mid_2, pieces_first))
+
+    pieces = same_plane(swap_rows(*teacher_parts(flags, t_split, [(edge_1, mid_1), (edge_2, mid_2)])))
+    s_all, ks_all = [*s_own, *s_a, *s_b, *s_c], [ks_own, ks_a, ks_b, ks_c]
+    products, sums = second_products(flags, pieces_own, pieces_first, ks_all, s_all, products, sums)
+    left, right, sums = last_sums(flags, pieces, ks_b, ks_c, sums)
+    sums = sums + lax.ppermute(sums, "tcol", CORES)
+    planes = [sums] + [lax.ppermute(sums, "tok", [(i, (i + s) % 4) for i in range(4)]) for s in (1, 2, 3)]
+    upper = last_products(flags, (left, right), [*s_b, *s_c], products)
+    scale = -2.0 * tokens_all * features
+    return finish(flags, upper, products, planes, teacher_norm.reshape(1, 1), scale)
+
+
 def solution(mesh):
+    sizes = (mesh.shape["tok"], mesh.shape["scol"], mesh.shape["tcol"])
+
+    def body(student, teacher, teacher_norm):
+        tokens_all = student.shape[0] * sizes[0]
+        features = student.shape[1] * sizes[1]
+        if sizes == (4, 4, 2) and tokens_all <= features:
+            return token_form(student, teacher, teacher_norm)
+        return feature_form(student, teacher, teacher_norm)
+
     return jax.shard_map(
         body,
         mesh=mesh,

time: 723 us -> 162 us (0.22)
  waiting for transfers between devices: 607 us -> 59.6 us
  matrix products: 68.1 us -> 0 us
  starting transfers between devices: 0.09 us -> 65.7 us
  Pallas kernels: 0 us -> 26.8 us
  between operations: 16.4 us -> 1.12 us
  blocking collectives: 13.6 us -> 0 us
  other arithmetic: 10.6 us -> 2.77 us
    psum x1 -> x0, waiting for transfers between devices: 562 us -> none  [body(): cov_block, gram_block = lax.psum((cov_block, gram_block), 'tok')]
    dot_general x4 -> x0, matrix products: 68.1 us -> none  [the longest x2 34.3 us: token_contract(): lax.dot_general(left, right, (((0,), (0,)), ((), ())), precision=lax.Prec...]
    ppermute x0 -> x50, starting transfers between devices: none -> 65.7 us  [the longest x13 23.8 us: send(): return lax.ppermute(x, 'tok', perm)]
    ppermute x0 -> x50, waiting for transfers between devices: none -> 59.6 us  [the longest x13 19.5 us: send(): return lax.ppermute(x, 'tok', perm)]
    all_gather x1 -> x0, waiting for transfers between devices: 38.4 us -> none  [body(): partner = lax.all_gather(own_slice, 'scol', axis=1, tiled=True)]
    pallas_call x0 -> x13, Pallas kernels: none -> 26.8 us  [the longest x7 11.3 us: call(): pl.pallas_call(kernel, out_shape=outs, in_specs=[FLAGS] + [whole] * len(a...]
    unnamed x1 -> x0, blocking collectives: 13.6 us -> none
    reduce_sum x3 -> x0, other arithmetic: 9.14 us -> none  [the longest x1 6.37 us: body(): jnp.sum(cov_block * cov_block)]
  transfers between devices with their start and end apart: 3 -> 50, of which waited for: 3 -> 22; matrix products, arithmetic and copies ran while one was open for 2% -> 2% of each run, Pallas kernels for 0% -> 15%
where the time goes in v1:
time: 162 us; the launch traced here: 161 us
  starting transfers between devices  65.7 us (41%)
  waiting for transfers between devices  59.6 us (37%)
  Pallas kernels  26.8 us (17%)
  local copies, waits for them, and re-layouts  5.31 us (3%)
  other arithmetic  2.77 us (2%)
    ppermute x13, starting transfers between devices, send(): return lax.ppermute(x, 'tok', perm)  23.8 us
    ppermute x13, waiting for transfers between devices, send(): return lax.ppermute(x, 'tok', perm)  19.5 us
    ppermute x4, waiting for transfers between devices, sum_x_y(): left = left + lax.ppermute(left, 'scol', chip_shift(1))  14.5 us
    pallas_call x7, Pallas kernels, call(): pl.pallas_call(kernel, out_shape=outs, in_specs=[FLAGS] + [whole] * len(a...  11.3 us
    ppermute x6, starting transfers between devices, same_plane(): lax.ppermute(piece, 'scol', chip_shift(s))  9.59 us
    ppermute x4, waiting for transfers between devices, mixed(): lax.ppermute(piece, PLANE, piece_shift(hi, lo))  8.21 us
    pallas_call x2, Pallas kernels, products_call(): pl.pallas_call(kernel, out_shape=outs, in_specs=[FLAGS] + [whole] * len(a...  7.83 us
    pallas_call x4, Pallas kernels, teacher_parts(): pl.pallas_call(kernel, out_shape=outs, in_specs=[FLAGS] + [whole] * (len(...  7.71 us
  transfers between devices with their start and end apart: 50, of which 22 were waited for; matrix products, arithmetic and copies ran while one was open for 2% of the time, Pallas kernels for 15%

profile of v1, /device:TPU:0, one launch (start us, length us, event | category | flops | bytes accessed | tf_op | source)
XLA Modules:
  0.0 161.4 jit_solution(3426071484613172679)
XLA Ops:
  0.0 1.7 %constant_dynamic-slice_fusion = (f32[256,1024]{1,0:T(8,128)S(1)}, f32[256,1024]{1,0:T(8,128)S(1)}) fusion(f32[512,1024]{1,0:T(8,128)} %param.3, s32[]{:T(128)S(6)} %select_n.48, s32[]{:T(128)S(6)} %select_n.46), kind=kLoop, calls=%fused_computation.5 | loop fusion | bytes 4194312 | tf_op jit(solution)/shard_map/dynamic_slice | solution.py:387
  1.7 3.1 %collective-permute-start = (f32[256,1024]{1,0:T(8,128)S(1)}, f32[256,1024]{1,0:T(8,128)S(1)}, u32[]{:S(2)}, u32[]{:S(2)}) collective-permute-start(f32[256,1024]{1,0:T(8,128)S(1)} %get-tuple-element.162.own_ref.first_ref.refs_12_.refs_25_), channel_id=1, source_target_pairs={{0,8},{8,0},{16,24},{24,16},{1,9},{9,1},{17,25},{25,17},{2,10},{10... | collective-permute-start | bytes 3145736 | tf_op jit(solution)/shard_map/ppermute | solution.py:353
  4.8 1.7 %collective-permute-start.1 = (f32[256,1024]{1,0:T(8,128)S(1)}, f32[256,1024]{1,0:T(8,128)}, u32[]{:S(2)}, u32[]{:S(2)}) collective-permute-start(f32[256,1024]{1,0:T(8,128)S(1)} %get-tuple-element.162.own_ref.first_ref.refs_12_.refs_25_), channel_id=1, source_target_pairs={{8,16},{16,8},{9,17},{17,9},{10,18},{18,10},{11,19},{19,11},{12,20... | collective-permute-start | bytes 3145736 | tf_op jit(solution)/shard_map/ppermute | solution.py:353
  6.5 2.3 %shard_map.37 = (f32[256,256]{1,0:T(8,128)}, f32[256,256]{1,0:T(8,128)S(1)}) custom-call(s32[4]{0:T(128)S(1)} %pad_add_fusion.flags_ref, f32[256,1024]{1,0:T(8,128)S(1)} %get-tuple-element.162.own_ref.first_ref.refs_12_.refs_25_, f32[256,1024]{1,0:T(8,128)S(1)} %get-tuple-element.162.own_ref.first_ref.refs_12_.refs_25_, ...), custom_call_target="tpu_custom_call" | custom-call | tf_op jit(solution)/shard_map/pallas_call | solution.py:114
  11.8 5.1 %collective-permute-done.2 = f32[256,256]{1,0:T(8,128)} collective-permute-done((f32[256,256]{1,0:T(8,128)}, f32[256,256]{1,0:T(8,128)}, u32[]{:S(2)}, u32[]{:S(2)}) %collective-permute-start.2) | collective-permute-done | bytes 262176 | tf_op jit(solution)/shard_map/ppermute | solution.py:359
  23.4 2.2 %copy-done = f32[512,2048]{1,0:T(8,128)S(1)} copy-done((f32[512,2048]{1,0:T(8,128)S(1)}, f32[512,2048]{1,0:T(8,128)}, u32[]{:S(2)}) %copy-start) | copy-done | bytes 4194328
  25.6 2.2 %shard_map.38 = (f32[256,128]{1,0:T(8,128)S(1)}, f32[256,128]{1,0:T(8,128)S(1)}, bf16[512,2048]{1,0:T(8,128)(2,1)S(1)}, bf16[512,2048]{1,0:T(8,128)(2,1)S(1)}) custom-call(s32[4]{0:T(128)S(1)} %pad_add_fusion.flags_ref, f32[512,2048]{1,0:T(8,128)S(1)} %copy-done, f32[128,2048]{1,0:T(8,128)S(1)} %constant_dynamic-slice_fusion.1.refs_1_), custom_call_target="tpu_custom_call" | custom-call | tf_op jit(solution)/shard_map/pallas_call | solution.py:180
  31.5 8.2 %collective-permute-start.9 = (f32[128,2048]{1,0:T(8,128)S(1)}, f32[128,2048]{1,0:T(8,128)S(1)}, u32[]{:S(2)}, u32[]{:S(2)}) collective-permute-start(f32[128,2048]{1,0:T(8,128)S(1)} %constant_dynamic-slice_fusion.1.refs_1_), channel_id=1, source_target_pairs={{0,8},{24,16},{1,9},{25,17},{2,10},{26,18},{3,11},{27,19},{4,12},{... | collective-permute-start | bytes 3145736 | tf_op jit(solution)/shard_map/ppermute | solution.py:353
  43.5 1.7 %collective-permute-done.15.refs_1_ = f32[256,128]{1,0:T(8,128)S(1)} collective-permute-done((f32[256,128]{1,0:T(8,128)S(1)}, f32[256,128]{1,0:T(8,128)S(1)}, u32[]{:S(2)}, u32[]{:S(2)}) %collective-permute-start.15) | collective-permute-done | bytes 131104 | tf_op jit(solution)/shard_map/ppermute | solution.py:378
  46.7 4.1 %collective-permute-done.11 = f32[256,256]{1,0:T(8,128)S(1)} collective-permute-done((f32[256,256]{1,0:T(8,128)S(1)}, f32[256,256]{1,0:T(8,128)S(1)}, u32[]{:S(2)}, u32[]{:S(2)}) %collective-permute-start.11) | collective-permute-done | bytes 262176 | tf_op jit(solution)/shard_map/ppermute | solution.py:359
  52.7 2.3 %collective-permute-start.17 = (f32[256,128]{1,0:T(8,128)S(1)}, f32[256,128]{1,0:T(8,128)S(1)}, u32[]{:S(2)}, u32[]{:S(2)}) collective-permute-start(f32[256,128]{1,0:T(8,128)S(1)} %add.59.refs_0_), channel_id=1, source_target_pairs={{0,6},{2,4},{4,2},{6,0},{1,7},{3,5},{5,3},{7,1},{8,14},{10,12},{12... | collective-permute-start | bytes 393224 | tf_op jit(solution)/shard_map/ppermute | solution.py:378
  55.0 4.0 %collective-permute-done.16.refs_2_ = f32[256,128]{1,0:T(8,128)S(1)} collective-permute-done((f32[256,128]{1,0:T(8,128)S(1)}, f32[256,128]{1,0:T(8,128)S(1)}, u32[]{:S(2)}, u32[]{:S(2)}) %collective-permute-start.16) | collective-permute-done | bytes 131104 | tf_op jit(solution)/shard_map/ppermute | solution.py:378
  62.5 2.9 %collective-permute-done.12.refs_5_.refs_14_ = f32[256,256]{1,0:T(8,128)S(1)} collective-permute-done((f32[256,256]{1,0:T(8,128)S(1)}, f32[256,256]{1,0:T(8,128)S(1)}, u32[]{:S(2)}, u32[]{:S(2)}) %collective-permute-start.12) | collective-permute-done | bytes 262176 | tf_op jit(solution)/shard_map/ppermute | solution.py:366
  71.1 2.0 %collective-permute-start.24 = (f32[256,256]{1,0:T(8,128)S(1)}, f32[256,256]{1,0:T(8,128)S(1)}, u32[]{:S(2)}, u32[]{:S(2)}) collective-permute-start(f32[256,256]{1,0:T(8,128)S(1)} %get-tuple-element.105), channel_id=1, source_target_pairs={{0,4},{2,6},{4,0},{6,2},{1,5},{3,7},{5,1},{7,3},{8,12},{10,14},{12... | collective-permute-start | bytes 786440 | tf_op jit(solution)/shard_map/ppermute | solution.py:360
  73.0 5.3 %collective-permute-done.22 = f32[256,256]{1,0:T(8,128)S(1)} collective-permute-done((f32[256,256]{1,0:T(8,128)S(1)}, f32[256,256]{1,0:T(8,128)S(1)}, u32[]{:S(2)}, u32[]{:S(2)}) %collective-permute-start.22) | collective-permute-done | bytes 262176 | tf_op jit(solution)/shard_map/ppermute | solution.py:359
  78.3 2.1 %collective-permute-start.23 = (f32[256,256]{1,0:T(8,128)S(1)}, f32[256,256]{1,0:T(8,128)S(1)}, u32[]{:S(2)}, u32[]{:S(2)}) collective-permute-start(f32[256,256]{1,0:T(8,128)S(1)} %add.63.refs_8_.refs_17_.refs_0_), channel_id=1, source_target_pairs={{0,4},{2,6},{4,0},{6,2},{1,5},{3,7},{5,1},{7,3},{8,12},{10,14},{12... | collective-permute-start | bytes 786440 | tf_op jit(solution)/shard_map/ppermute | solution.py:366
  81.6 1.8 %shard_map.40 = (f32[256,128]{1,0:T(8,128)S(1)}, f32[256,128]{1,0:T(8,128)S(1)}) custom-call(s32[4]{0:T(128)S(1)} %pad_add_fusion.flags_ref, bf16[512,2048]{1,0:T(8,128)(2,1)S(1)} %get-tuple-element.89.refs_0_, bf16[512,2048]{1,0:T(8,128)(2,1)S(1)} %get-tuple-element.90.refs_1_, f32[128,2048]{1,0:T(8,128)S(1)} %collective-permute-done.9.refs_2_), custom_call_target="tpu_custom_call" | custom-call | tf_op jit(solution)/shard_map/pallas_call | solution.py:180
  84.9 8.3 %collective-permute-done.18 = f32[256,1024]{1,0:T(8,128)S(1)} collective-permute-done((f32[256,1024]{1,0:T(8,128)S(1)}, f32[256,1024]{1,0:T(8,128)S(1)}, u32[]{:S(2)}, u32[]{:S(2)}) %collective-permute-start.18) | collective-permute-done | bytes 1048608 | tf_op jit(solution)/shard_map/ppermute | solution.py:353
  95.5 1.8 %shard_map.43 = (f32[256,128]{1,0:T(8,128)S(1)}, f32[256,128]{1,0:T(8,128)S(1)}) custom-call(s32[4]{0:T(128)S(1)} %pad_add_fusion.flags_ref, bf16[512,2048]{1,0:T(8,128)(2,1)S(1)} %get-tuple-element.89.refs_0_, bf16[512,2048]{1,0:T(8,128)(2,1)S(1)} %get-tuple-element.90.refs_1_, f32[128,2048]{1,0:T(8,128)S(1)} %collective-permute-done.19.refs_2_), custom_call_target="tpu_custom_call" | custom-call | tf_op jit(solution)/shard_map/pallas_call | solution.py:180
  100.1 2.0 %collective-permute-start.31 = (f32[256,256]{1,0:T(8,128)S(1)}, f32[256,256]{1,0:T(8,128)S(1)}, u32[]{:S(2)}, u32[]{:S(2)}) collective-permute-start(f32[256,256]{1,0:T(8,128)S(1)} %get-tuple-element.111), channel_id=1, source_target_pairs={{0,4},{2,6},{4,0},{6,2},{1,5},{3,7},{5,1},{7,3},{8,12},{10,14},{12... | collective-permute-start | bytes 786440 | tf_op jit(solution)/shard_map/ppermute | solution.py:360
  104.8 3.2 %shard_map.44 = (f32[256,1024]{1,0:T(8,128)S(1)}, f32[8,128]{1,0:T(8,128)S(1)}) custom-call(s32[4]{0:T(128)S(1)} %pad_add_fusion.flags_ref, f32[256,256]{1,0:T(8,128)S(1)} %add.57.refs_0_.refs_9_, f32[256,256]{1,0:T(8,128)S(1)} %collective-permute-done.3.refs_1_.refs_10_, f32[256,256]{1,0:T(8,128)S(1)} %add.58.refs_2_.refs_11_, ...), custom_call_target="tpu_custom_call" | custom-call | tf_op jit(solution)/shard_map/pallas_call | solution.py:211
  109.5 4.3 %collective-permute-done.28 = f32[256,128]{1,0:T(8,128)S(1)} collective-permute-done((f32[256,128]{1,0:T(8,128)S(1)}, f32[256,128]{1,0:T(8,128)S(1)}, u32[]{:S(2)}, u32[]{:S(2)}) %collective-permute-start.28) | collective-permute-done | bytes 131104 | tf_op jit(solution)/shard_map/ppermute | solution.py:353
  115.2 4.5 %collective-permute-done.35 = f32[256,128]{1,0:T(8,128)S(1)} collective-permute-done((f32[256,128]{1,0:T(8,128)S(1)}, f32[256,128]{1,0:T(8,128)S(1)}, u32[]{:S(2)}, u32[]{:S(2)}) %collective-permute-start.35) | collective-permute-done | bytes 131104 | tf_op jit(solution)/shard_map/ppermute | solution.py:353
  122.8 6.2 %collective-permute-done.36.refs_5_ = f32[256,256]{1,0:T(8,128)S(1)} collective-permute-done((f32[256,256]{1,0:T(8,128)S(1)}, f32[256,256]{1,0:T(8,128)S(1)}, u32[]{:S(2)}, u32[]{:S(2)}) %collective-permute-start.36) | collective-permute-done | bytes 262176 | tf_op jit(solution)/shard_map/ppermute | solution.py:382
  131.2 2.0 %collective-permute-done.38.refs_7_ = f32[256,256]{1,0:T(8,128)S(1)} collective-permute-done((f32[256,256]{1,0:T(8,128)S(1)}, f32[256,256]{1,0:T(8,128)S(1)}, u32[]{:S(2)}, u32[]{:S(2)}) %collective-permute-start.38) | collective-permute-done | bytes 262176 | tf_op jit(solution)/shard_map/ppermute | solution.py:382
  134.4 1.8 %shard_map.45 = (f32[256,128]{1,0:T(8,128)S(1)}, f32[256,128]{1,0:T(8,128)S(1)}) custom-call(s32[4]{0:T(128)S(1)} %pad_add_fusion.flags_ref, bf16[512,2048]{1,0:T(8,128)(2,1)S(1)} %get-tuple-element.89.refs_0_, bf16[512,2048]{1,0:T(8,128)(2,1)S(1)} %get-tuple-element.90.refs_1_, f32[64,2048]{1,0:T(8,128)S(1)} %collective-permute-done.26.refs_2_, ...), custom_call_target="tpu_custom_call" | custom-call | tf_op jit(solution)/shard_map/pallas_call | solution.py:180
  136.3 3.5 %collective-permute-start.40 = (f32[256,128]{1,0:T(8,128)S(1)}, f32[256,128]{1,0:T(8,128)S(1)}, u32[]{:S(2)}, u32[]{:S(2)}) collective-permute-start(f32[256,128]{1,0:T(8,128)S(1)} %get-tuple-element.142), channel_id=1, source_target_pairs={{0,1},{1,0},{2,3},{3,2},{4,5},{5,4},{6,7},{7,6},{8,9},{9,8},{10,11... | collective-permute-start | bytes 393224 | tf_op jit(solution)/shard_map/ppermute | solution.py:375
  142.0 2.7 %collective-permute-start.42 = (f32[256,128]{1,0:T(8,128)S(1)}, f32[256,128]{1,0:T(8,128)S(1)}, u32[]{:S(2)}, u32[]{:S(2)}) collective-permute-start(f32[256,128]{1,0:T(8,128)S(1)} %add.68.p0), channel_id=1, source_target_pairs={{0,4},{2,6},{4,0},{6,2},{1,5},{3,7},{5,1},{7,3},{8,12},{10,14},{12... | collective-permute-start | bytes 393224 | tf_op jit(solution)/shard_map/ppermute | solution.py:378
  145.0 4.6 %shard_map.46 = (f32[512,1024]{1,0:T(8,128)S(1)}, f32[8,128]{1,0:T(8,128)S(1)}) custom-call(s32[4]{0:T(128)S(1)} %pad_add_fusion.flags_ref, f32[256,128]{1,0:T(8,128)S(1)} %add.59.refs_0_, f32[256,128]{1,0:T(8,128)S(1)} %collective-permute-done.15.refs_1_, f32[256,128]{1,0:T(8,128)S(1)} %collective-permute-done.16.refs_2_, ...), custom_call_target="tpu_custom_call" | custom-call | tf_op jit(solution)/shard_map/pallas_call | solution.py:211
  153.5 1.8 %collective-permute-start.48 = (f32[8,128]{1,0:T(8,128)S(1)}, f32[8,128]{1,0:T(8,128)S(1)}, u32[]{:S(2)}, u32[]{:S(2)}) collective-permute-start(f32[8,128]{1,0:T(8,128)S(1)} %add.69.refs_0_), channel_id=1, source_target_pairs={{0,16},{8,24},{16,0},{24,8},{1,17},{9,25},{17,1},{25,9},{2,18},{10... | collective-permute-start | bytes 12296 | tf_op jit(solution)/shard_map/ppermute | solution.py:432
  155.2 2.0 %collective-permute-start.49 = (f32[8,128]{1,0:T(8,128)S(1)}, f32[8,128]{1,0:T(8,128)S(1)}, u32[]{:S(2)}, u32[]{:S(2)}) collective-permute-start(f32[8,128]{1,0:T(8,128)S(1)} %add.69.refs_0_), channel_id=1, source_target_pairs={{0,24},{8,0},{16,8},{24,16},{1,25},{9,1},{17,9},{25,17},{2,26},{10... | collective-permute-start | bytes 12296 | tf_op jit(solution)/shard_map/ppermute | solution.py:432
  159.6 1.8 %shard_map.49 = f32[256,1024]{1,0:T(8,128)} custom-call(s32[4]{0:T(128)S(1)} %pad_add_fusion.flags_ref, f32[256,1024]{1,0:T(8,128)S(1)} %shard_map.48.up_ref, f32[512,1024]{1,0:T(8,128)S(1)} %get-tuple-element.159.prod_ref, f32[1,1]{1,0:T(1,128)} %bitcast.5.norm_ref, f32[8,128]{1,0:T(8,128)S(1)} %add.69.refs_0_, ...), custom_call_target="tpu_custom_call" | custom-call | tf_op jit(solution)/shard_map/pallas_call | solution.py:114
  (108 shorter events, 57.1 us)
Async XLA Ops:
  1.7 27.6 %collective-permute-start = (f32[256,1024]{1,0:T(8,128)S(1)}, f32[256,1024]{1,0:T(8,128)S(1)}, u32[]{:S(2)}, u32[]{:S(2)}) collective-permute-start(f32[256,1024]{1,0:T(8,128)S(1)} %get-tuple-element.162.own_ref.first_ref.refs_12_.refs_25_), channel_id=1, source_target_pairs={{0,8},{8,0},{16,24},{24,16},{1,9},{9,1},{17,25},{25,17},{2,10},{10... | collective-permute-start | bytes 3145736 | tf_op jit(solution)/shard_map/ppermute | solution.py:353
  4.8 24.5 %collective-permute-start.1 = (f32[256,1024]{1,0:T(8,128)S(1)}, f32[256,1024]{1,0:T(8,128)}, u32[]{:S(2)}, u32[]{:S(2)}) collective-permute-start(f32[256,1024]{1,0:T(8,128)S(1)} %get-tuple-element.162.own_ref.first_ref.refs_12_.refs_25_), channel_id=1, source_target_pairs={{8,16},{16,8},{9,17},{17,9},{10,18},{18,10},{11,19},{19,11},{12,20... | collective-permute-start | bytes 3145736 | tf_op jit(solution)/shard_map/ppermute | solution.py:353
  8.8 8.1 %collective-permute-start.2 = (f32[256,256]{1,0:T(8,128)}, f32[256,256]{1,0:T(8,128)}, u32[]{:S(2)}, u32[]{:S(2)}) collective-permute-start(f32[256,256]{1,0:T(8,128)} %get-tuple-element.83), channel_id=1, source_target_pairs={{0,2},{2,0},{4,6},{6,4},{1,3},{3,1},{5,7},{7,5},{8,10},{10,8},{12,... | collective-permute-start | bytes 786440 | tf_op jit(solution)/shard_map/ppermute | solution.py:359
  10.3 9.2 %collective-permute-start.4 = (f32[256,256]{1,0:T(8,128)S(1)}, f32[256,256]{1,0:T(8,128)}, u32[]{:S(2)}, u32[]{:S(2)}) collective-permute-start(f32[256,256]{1,0:T(8,128)S(1)} %get-tuple-element.84), channel_id=1, source_target_pairs={{0,4},{2,6},{4,0},{6,2},{1,5},{3,7},{5,1},{7,3},{8,12},{10,14},{12... | collective-permute-start | bytes 786440 | tf_op jit(solution)/shard_map/ppermute | solution.py:360
  17.9 11.3 %collective-permute-start.3 = (f32[256,256]{1,0:T(8,128)S(1)}, f32[256,256]{1,0:T(8,128)S(1)}, u32[]{:S(2)}, u32[]{:S(2)}) collective-permute-start(f32[256,256]{1,0:T(8,128)S(1)} %add.57.refs_0_.refs_9_), channel_id=1, source_target_pairs={{0,4},{2,6},{4,0},{6,2},{1,5},{3,7},{5,1},{7,3},{8,12},{10,14},{12... | collective-permute-start | bytes 786440 | tf_op jit(solution)/shard_map/ppermute | solution.py:366
  20.5 8.7 %collective-permute-start.5 = (f32[256,256]{1,0:T(8,128)S(1)}, f32[256,256]{1,0:T(8,128)S(1)}, u32[]{:S(2)}, u32[]{:S(2)}) collective-permute-start(f32[256,256]{1,0:T(8,128)S(1)} %add.58.refs_2_.refs_11_), channel_id=1, source_target_pairs={{0,2},{2,0},{4,6},{6,4},{1,3},{3,1},{5,7},{7,5},{8,10},{10,8},{12,... | collective-permute-start | bytes 786440 | tf_op jit(solution)/shard_map/ppermute | solution.py:368
  29.3 12.0 %collective-permute-start.10 = (f32[256,1024]{1,0:T(8,128)S(1)}, f32[256,1024]{1,0:T(8,128)S(1)}, u32[]{:S(2)}, u32[]{:S(2)}) collective-permute-start(f32[256,1024]{1,0:T(8,128)S(1)} %collective-permute-done.first_ref.refs_14_.refs_27_), channel_id=1, source_target_pairs={{0,1},{1,0},{2,3},{3,2},{4,5},{5,4},{6,7},{7,6},{8,9},{9,8},{10,11... | collective-permute-start | bytes 3145736 | tf_op jit(solution)/shard_map/ppermute | solution.py:356
  29.5 32.0 %collective-permute-start.8 = (f32[256,1024]{1,0:T(8,128)S(1)}, f32[256,1024]{1,0:T(8,128)S(1)}, u32[]{:S(2)}, u32[]{:S(2)}) collective-permute-start(f32[256,1024]{1,0:T(8,128)S(1)} %collective-permute-done.first_ref.refs_14_.refs_27_), channel_id=1, source_target_pairs={{8,16},{16,8},{9,17},{17,9},{10,18},{18,10},{11,19},{19,11},{12,20... | collective-permute-start | bytes 3145736 | tf_op jit(solution)/shard_map/ppermute | solution.py:353
  30.2 31.2 %collective-permute-start.7 = (f32[256,1024]{1,0:T(8,128)}, f32[256,1024]{1,0:T(8,128)S(1)}, u32[]{:S(2)}, u32[]{:S(2)}) collective-permute-start(f32[256,1024]{1,0:T(8,128)} %collective-permute-done.1), channel_id=1, source_target_pairs={{8,0},{16,24},{9,1},{17,25},{10,2},{18,26},{11,3},{19,27},{12,4},{... | collective-permute-start | bytes 3145736 | tf_op jit(solution)/shard_map/ppermute | solution.py:353
  31.5 31.0 %collective-permute-start.9 = (f32[128,2048]{1,0:T(8,128)S(1)}, f32[128,2048]{1,0:T(8,128)S(1)}, u32[]{:S(2)}, u32[]{:S(2)}) collective-permute-start(f32[128,2048]{1,0:T(8,128)S(1)} %constant_dynamic-slice_fusion.1.refs_1_), channel_id=1, source_target_pairs={{0,8},{24,16},{1,9},{25,17},{2,10},{26,18},{3,11},{27,19},{4,12},{... | collective-permute-start | bytes 3145736 | tf_op jit(solution)/shard_map/ppermute | solution.py:353
  50.9 8.2 %collective-permute-start.16 = (f32[256,128]{1,0:T(8,128)S(1)}, f32[256,128]{1,0:T(8,128)S(1)}, u32[]{:S(2)}, u32[]{:S(2)}) collective-permute-start(f32[256,128]{1,0:T(8,128)S(1)} %add.59.refs_0_), channel_id=1, source_target_pairs={{0,4},{2,6},{4,0},{6,2},{1,5},{3,7},{5,1},{7,3},{8,12},{10,14},{12... | collective-permute-start | bytes 393224 | tf_op jit(solution)/shard_map/ppermute | solution.py:378
  65.7 27.4 %collective-permute-start.18 = (f32[256,1024]{1,0:T(8,128)S(1)}, f32[256,1024]{1,0:T(8,128)S(1)}, u32[]{:S(2)}, u32[]{:S(2)}) collective-permute-start(f32[256,1024]{1,0:T(8,128)S(1)} %collective-permute-done.8), channel_id=1, source_target_pairs={{8,0},{16,24},{9,1},{17,25},{10,2},{18,26},{11,3},{19,27},{12,4},{... | collective-permute-start | bytes 3145736 | tf_op jit(solution)/shard_map/ppermute | solution.py:353
  67.0 26.1 %collective-permute-start.19 = (f32[128,2048]{1,0:T(8,128)S(1)}, f32[128,2048]{1,0:T(8,128)S(1)}, u32[]{:S(2)}, u32[]{:S(2)}) collective-permute-start(f32[128,2048]{1,0:T(8,128)S(1)} %collective-permute-done.9.refs_2_), channel_id=1, source_target_pairs={{8,16},{16,8},{9,17},{17,9},{10,18},{18,10},{11,19},{19,11},{12,20... | collective-permute-start | bytes 3145736 | tf_op jit(solution)/shard_map/ppermute | solution.py:353
  69.9 8.4 %collective-permute-start.22 = (f32[256,256]{1,0:T(8,128)S(1)}, f32[256,256]{1,0:T(8,128)S(1)}, u32[]{:S(2)}, u32[]{:S(2)}) collective-permute-start(f32[256,256]{1,0:T(8,128)S(1)} %get-tuple-element.104), channel_id=1, source_target_pairs={{0,2},{2,0},{4,6},{6,4},{1,3},{3,1},{5,7},{7,5},{8,10},{10,8},{12,... | collective-permute-start | bytes 786440 | tf_op jit(solution)/shard_map/ppermute | solution.py:359
  71.1 9.4 %collective-permute-start.24 = (f32[256,256]{1,0:T(8,128)S(1)}, f32[256,256]{1,0:T(8,128)S(1)}, u32[]{:S(2)}, u32[]{:S(2)}) collective-permute-start(f32[256,256]{1,0:T(8,128)S(1)} %get-tuple-element.105), channel_id=1, source_target_pairs={{0,4},{2,6},{4,0},{6,2},{1,5},{3,7},{5,1},{7,3},{8,12},{10,14},{12... | collective-permute-start | bytes 786440 | tf_op jit(solution)/shard_map/ppermute | solution.py:360
  78.3 14.8 %collective-permute-start.23 = (f32[256,256]{1,0:T(8,128)S(1)}, f32[256,256]{1,0:T(8,128)S(1)}, u32[]{:S(2)}, u32[]{:S(2)}) collective-permute-start(f32[256,256]{1,0:T(8,128)S(1)} %add.63.refs_8_.refs_17_.refs_0_), channel_id=1, source_target_pairs={{0,4},{2,6},{4,0},{6,2},{1,5},{3,7},{5,1},{7,3},{8,12},{10,14},{12... | collective-permute-start | bytes 786440 | tf_op jit(solution)/shard_map/ppermute | solution.py:366
  80.5 12.7 %collective-permute-start.25 = (f32[256,256]{1,0:T(8,128)S(1)}, f32[256,256]{1,0:T(8,128)S(1)}, u32[]{:S(2)}, u32[]{:S(2)}) collective-permute-start(f32[256,256]{1,0:T(8,128)S(1)} %add.64.refs_10_.refs_19_.refs_2_), channel_id=1, source_target_pairs={{0,2},{2,0},{4,6},{6,4},{1,3},{3,1},{5,7},{7,5},{8,10},{10,8},{12,... | collective-permute-start | bytes 786440 | tf_op jit(solution)/shard_map/ppermute | solution.py:368
  93.4 20.4 %collective-permute-start.26 = (f32[64,2048]{1,0:T(8,128)S(1)}, f32[64,2048]{1,0:T(8,128)S(1)}, u32[]{:S(2)}, u32[]{:S(2)}) collective-permute-start(f32[64,2048]{1,0:T(8,128)S(1)} %slice.12), channel_id=1, source_target_pairs={{8,0},{16,24},{9,1},{17,25},{10,2},{18,26},{11,3},{19,27},{12,4},{... | collective-permute-start | bytes 1572872 | tf_op jit(solution)/shard_map/ppermute | solution.py:353
  94.8 19.0 %collective-permute-start.27 = (f32[64,2048]{1,0:T(8,128)S(1)}, f32[64,2048]{1,0:T(8,128)S(1)}, u32[]{:S(2)}, u32[]{:S(2)}) collective-permute-start(f32[64,2048]{1,0:T(8,128)S(1)} %slice.13), channel_id=1, source_target_pairs={{8,16},{16,8},{9,17},{17,9},{10,18},{18,10},{11,19},{19,11},{12,20... | collective-permute-start | bytes 1572872 | tf_op jit(solution)/shard_map/ppermute | solution.py:353
  98.9 9.2 %collective-permute-start.30 = (f32[256,256]{1,0:T(8,128)S(1)}, f32[256,256]{1,0:T(8,128)S(1)}, u32[]{:S(2)}, u32[]{:S(2)}) collective-permute-start(f32[256,256]{1,0:T(8,128)S(1)} %get-tuple-element.110), channel_id=1, source_target_pairs={{0,2},{2,0},{4,6},{6,4},{1,3},{3,1},{5,7},{7,5},{8,10},{10,8},{12,... | collective-permute-start | bytes 786440 | tf_op jit(solution)/shard_map/ppermute | solution.py:359
  100.1 9.4 %collective-permute-start.31 = (f32[256,256]{1,0:T(8,128)S(1)}, f32[256,256]{1,0:T(8,128)S(1)}, u32[]{:S(2)}, u32[]{:S(2)}) collective-permute-start(f32[256,256]{1,0:T(8,128)S(1)} %get-tuple-element.111), channel_id=1, source_target_pairs={{0,4},{2,6},{4,0},{6,2},{1,5},{3,7},{5,1},{7,3},{8,12},{10,14},{12... | collective-permute-start | bytes 786440 | tf_op jit(solution)/shard_map/ppermute | solution.py:360
  103.4 10.4 %collective-permute-start.28 = (f32[256,128]{1,0:T(8,128)S(1)}, f32[256,128]{1,0:T(8,128)S(1)}, u32[]{:S(2)}, u32[]{:S(2)}) collective-permute-start(f32[256,128]{1,0:T(8,128)S(1)} %add.62), channel_id=1, source_target_pairs={{8,0},{16,24},{9,1},{17,25},{10,2},{18,26},{11,3},{19,27},{12,4},{... | collective-permute-start | bytes 393224 | tf_op jit(solution)/shard_map/ppermute | solution.py:353
  108.1 11.6 %collective-permute-start.35 = (f32[256,128]{1,0:T(8,128)S(1)}, f32[256,128]{1,0:T(8,128)S(1)}, u32[]{:S(2)}, u32[]{:S(2)}) collective-permute-start(f32[256,128]{1,0:T(8,128)S(1)} %add.67), channel_id=1, source_target_pairs={{16,0},{8,24},{17,1},{9,25},{18,2},{10,26},{19,3},{11,27},{20,4},{... | collective-permute-start | bytes 393224 | tf_op jit(solution)/shard_map/ppermute | solution.py:353
  113.9 20.5 %collective-permute-start.33 = (f32[64,2048]{1,0:T(8,128)S(1)}, f32[64,2048]{1,0:T(8,128)S(1)}, u32[]{:S(2)}, u32[]{:S(2)}) collective-permute-start(f32[64,2048]{1,0:T(8,128)S(1)} %slice.14), channel_id=1, source_target_pairs={{8,0},{16,24},{9,1},{17,25},{10,2},{18,26},{11,3},{19,27},{12,4},{... | collective-permute-start | bytes 1572872 | tf_op jit(solution)/shard_map/ppermute | solution.py:353
  119.8 9.2 %collective-permute-start.36 = (f32[256,256]{1,0:T(8,128)S(1)}, f32[256,256]{1,0:T(8,128)S(1)}, u32[]{:S(2)}, u32[]{:S(2)}) collective-permute-start(f32[256,256]{1,0:T(8,128)S(1)} %pad_maximum_fusion.refs_4_), channel_id=1, source_target_pairs={{2,0},{6,1},{0,2},{4,3},{3,4},{7,5},{1,6},{5,7},{10,8},{11,9},{8,1... | collective-permute-start | bytes 786440 | tf_op jit(solution)/shard_map/ppermute | solution.py:382
  120.8 13.6 %collective-permute-start.34 = (f32[64,2048]{1,0:T(8,128)S(1)}, f32[64,2048]{1,0:T(8,128)S(1)}, u32[]{:S(2)}, u32[]{:S(2)}) collective-permute-start(f32[64,2048]{1,0:T(8,128)S(1)} %slice.15), channel_id=1, source_target_pairs={{8,16},{16,8},{9,17},{17,9},{10,18},{18,10},{11,19},{19,11},{12,20... | collective-permute-start | bytes 1572872 | tf_op jit(solution)/shard_map/ppermute | solution.py:353
  121.5 8.1 %collective-permute-start.37 = (f32[256,256]{1,0:T(8,128)S(1)}, f32[256,256]{1,0:T(8,128)S(1)}, u32[]{:S(2)}, u32[]{:S(2)}) collective-permute-start(f32[256,256]{1,0:T(8,128)S(1)} %pad_maximum_fusion.refs_4_), channel_id=1, source_target_pairs={{1,0},{5,1},{3,2},{7,3},{0,4},{4,5},{2,6},{6,7},{12,8},{13,9},{14,... | collective-permute-start | bytes 786440 | tf_op jit(solution)/shard_map/ppermute | solution.py:382
  122.2 11.0 %collective-permute-start.38 = (f32[256,256]{1,0:T(8,128)S(1)}, f32[256,256]{1,0:T(8,128)S(1)}, u32[]{:S(2)}, u32[]{:S(2)}) collective-permute-start(f32[256,256]{1,0:T(8,128)S(1)} %pad_maximum_fusion.refs_4_), channel_id=1, source_target_pairs={{3,0},{7,1},{1,2},{5,3},{2,4},{6,5},{0,6},{4,7},{14,8},{15,9},{12,... | collective-permute-start | bytes 786440 | tf_op jit(solution)/shard_map/ppermute | solution.py:382
  129.7 15.3 %collective-permute-start.44 = (f32[256,256]{1,0:T(8,128)S(1)}, f32[256,256]{1,0:T(8,128)S(1)}, u32[]{:S(2)}, u32[]{:S(2)}) collective-permute-start(f32[256,256]{1,0:T(8,128)S(1)} %add.65.refs_21_.refs_4_), channel_id=1, source_target_pairs={{0,4},{2,6},{4,0},{6,2},{1,5},{3,7},{5,1},{7,3},{8,12},{10,14},{12... | collective-permute-start | bytes 786440 | tf_op jit(solution)/shard_map/ppermute | solution.py:366
  133.2 11.8 %collective-permute-start.45 = (f32[256,256]{1,0:T(8,128)S(1)}, f32[256,256]{1,0:T(8,128)S(1)}, u32[]{:S(2)}, u32[]{:S(2)}) collective-permute-start(f32[256,256]{1,0:T(8,128)S(1)} %add.66.refs_23_.refs_6_), channel_id=1, source_target_pairs={{0,2},{2,0},{4,6},{6,4},{1,3},{3,1},{5,7},{7,5},{8,10},{10,8},{12,... | collective-permute-start | bytes 786440 | tf_op jit(solution)/shard_map/ppermute | solution.py:368
  140.7 8.9 %collective-permute-start.41 = (f32[256,128]{1,0:T(8,128)S(1)}, f32[256,128]{1,0:T(8,128)S(1)}, u32[]{:S(2)}, u32[]{:S(2)}) collective-permute-start(f32[256,128]{1,0:T(8,128)S(1)} %add.68.p0), channel_id=1, source_target_pairs={{0,2},{2,0},{4,6},{6,4},{1,3},{3,1},{5,7},{7,5},{8,10},{10,8},{12,... | collective-permute-start | bytes 393224 | tf_op jit(solution)/shard_map/ppermute | solution.py:378
  142.0 8.3 %collective-permute-start.42 = (f32[256,128]{1,0:T(8,128)S(1)}, f32[256,128]{1,0:T(8,128)S(1)}, u32[]{:S(2)}, u32[]{:S(2)}) collective-permute-start(f32[256,128]{1,0:T(8,128)S(1)} %add.68.p0), channel_id=1, source_target_pairs={{0,4},{2,6},{4,0},{6,2},{1,5},{3,7},{5,1},{7,3},{8,12},{10,14},{12... | collective-permute-start | bytes 393224 | tf_op jit(solution)/shard_map/ppermute | solution.py:378
  (19 other events, 87.5 us)

commit v2 on v1

--- a/solution.py
+++ b/solution.py
@@ -119,6 +119,23 @@
         compiler_params=room(args, outs),
         cost_estimate=LIGHT,
     )(flags, *args)
+
+
+def mine(flags_ref, side, half):
+    k = flags_ref[0]
+    return pl.ds(pl.multiple_of((k if side == 0 else 1 - k) * half, half), half)
+
+
+def own_gram(flags, student):
+    half = student.shape[0] // 2
+
+    def kernel(flags_ref, student_ref, *outs):
+        left = split(student_ref[mine(flags_ref, 0, half), :])
+        right = split(student_ref[mine(flags_ref, 1, half), :])
+        outs[0][...] = dot_split(left, left, ROWS)
+        outs[1][...] = dot_split(left, right, ROWS)
+
+    return call(kernel, flags, [student], [(half, half)] * 2)
 
 
 def gram_part(flags, own, pair):
@@ -196,8 +213,10 @@
     return jnp.where(hi, high, low), jnp.where(hi, low, high)
 
 
-def pick(flags_ref, first, second):
-    return jnp.where(flags_ref[1] == 1, first, second)
+def returned(flags_ref, pieces):
+    edge = flags_ref[1] == 1
+    left, right = ordered(flags_ref, [jnp.where(edge, pieces[4], pieces[0]), *pieces[1:4]])
+    return jnp.where(edge, left.T, left), jnp.where(edge, right.T, right)
 
 
 def spread(sum_ref, hsic, gram):
@@ -219,106 +238,111 @@
     )(flags, *args)
 
 
-def first_products(flags, ks, s):
+def first_products(flags, pieces, ks, student, s_a):
+    half, width = s_a[0].shape
+    chunk = width // 4
+
+    def kernel(flags_ref, *refs):
+        tops = ordered(flags_ref, [ref[...] for ref in refs[:4]])
+        ks_refs, (student_ref, left_ref, right_ref) = (refs[4:8], refs[8:12]), refs[12:15]
+        out_ref, sum_ref, high, low = refs[15:]
+        hsic = gram = jnp.zeros((1, 1), jnp.float32)
+        for g in range(2):
+            for side in range(2):
+                at = slice((2 * g + side) * half, (2 * g + side + 1) * half)
+                bottom = summed(ks_refs[g], side)
+                high[half:, at], low[half:, at] = split(bottom)
+                gram = gram + jnp.sum(bottom * bottom, keepdims=True)
+                if g == 0:
+                    high[:half, at], low[:half, at] = split(tops[side])
+                    hsic = hsic + jnp.sum(tops[side] * bottom, keepdims=True)
+        sum_ref[...] = spread(sum_ref, hsic, gram)
+        for j in range(4):
+            cols = slice(j * chunk, (j + 1) * chunk)
+            both, lower = 0.0, 0.0
+            for side in range(2):
+                at = slice(side * half, (side + 1) * half)
+                own = split(student_ref[mine(flags_ref, side, half), cols])
+                both = both + dot_split((high[:, at], low[:, at]), own, COLS)
+                at = slice((2 + side) * half, (3 + side) * half)
+                a = split((left_ref, right_ref)[side][:, cols])
+                lower = lower + dot_split((high[half:, at], low[half:, at]), a, COLS)
+            out_ref[:half, cols] = both[:half]
+            out_ref[half:, cols] = both[half:] + lower
+
+    args = [*pieces, *[part for terms in ks for part in terms], student, *s_a]
+    return products_call(kernel, flags, args, [2 * half, width], [2 * half, 4 * half])
+
+
+def second_products(flags, pieces, ks, s, products, sums):
     half, width = s[0].shape
     chunk = width // 4
 
     def kernel(flags_ref, *refs):
-        ks_refs, s_refs = refs[:12], refs[12:18]
-        out_ref, sum_ref, high, low = refs[18:]
-        gram = jnp.zeros((1, 1), jnp.float32)
+        tops, refs = returned(flags_ref, [ref[...] for ref in refs[:5]]), refs[5:]
+        ks_refs, s_refs, (prod_ref, before_ref) = (refs[:4], refs[4:8], refs[8:12]), refs[12:18], refs[18:20]
+        out_ref, sum_ref, high, low = refs[20:]
+        hsic = gram = jnp.zeros((1, 1), jnp.float32)
         for g in range(3):
             for side in range(2):
                 at = slice((2 * g + side) * half, (2 * g + side + 1) * half)
-                bottom = summed(ks_refs[4 * g : 4 * g + 4], side)
-                high[:, at], low[:, at] = split(bottom)
-                gram = gram + jnp.sum(bottom * bottom, keepdims=True)
-        sum_ref[...] = spread(sum_ref, 0.0, gram)
-        for j in range(4):
-            cols = slice(j * chunk, (j + 1) * chunk)
-            total = 0.0
-            for i in range(6):
-                at = slice(i * half, (i + 1) * half)
-                total = total + dot_split((high[:, at], low[:, at]), split(s_refs[i][:, cols]), COLS)
-            out_ref[:, cols] = total
-
-    args = [part for quad in ks for part in quad] + list(s)
-    return products_call(kernel, flags, args, [half, width], [half, 6 * half])
-
-
-def second_products(flags, own, first, ks, s, products, sums):
-    half, width = s[0].shape
-    chunk = width // 4
-
-    def kernel(flags_ref, *refs):
-        own_refs, first_refs, refs = refs[:4], refs[4:9], refs[9:]
-        ks_refs, s_refs, (prod_ref, before_ref) = refs[:16], refs[16:24], refs[24:26]
-        edge = flags_ref[1] == 1
-        tops = [ordered(flags_ref, [ref[...] for ref in own_refs])]
-        for g in range(2):
-            at = slice(g * half // 2, (g + 1) * half // 2)
-            pieces = [ref[:, at] for ref in first_refs]
-            left, right = ordered(flags_ref, [jnp.where(edge, pieces[4], pieces[0]), *pieces[1:4]])
-            tops.append((jnp.where(edge, left.T, left), jnp.where(edge, right.T, right)))
-        out_ref, sum_ref, high, low = refs[26:]
-        hsic = gram = jnp.zeros((1, 1), jnp.float32)
-        for side in range(2):
-            own, a, b, c = (summed(ks_refs[4 * g : 4 * g + 4], side) for g in range(4))
-            for g, bottom in enumerate((own, a, pick(flags_ref, b, c))):
-                at = slice((2 * g + side) * half, (2 * g + side + 1) * half)
-                top = tops[g][side]
-                high[:, at], low[:, at] = split(top)
-                hsic = hsic + jnp.sum(top * bottom, keepdims=True)
-            at = slice((6 + side) * half, (7 + side) * half)
-            high[:, at], low[:, at] = split(c)
-            gram = gram + jnp.sum(c * c, keepdims=True)
+                bottom = summed(ks_refs[g], side)
+                if g == 0:
+                    high[:, at], low[:, at] = split(tops[side])
+                    hsic = hsic + jnp.sum(tops[side] * bottom, keepdims=True)
+                else:
+                    high[:, at], low[:, at] = split(bottom)
+                    gram = gram + jnp.sum(bottom * bottom, keepdims=True)
         sum_ref[...] = before_ref[...] + spread(sum_ref, hsic, gram)
         for j in range(4):
             cols = slice(j * chunk, (j + 1) * chunk)
-            upper, lower = 0.0, prod_ref[:, cols]
-            for side in range(2):
-                own, a, b, c = (s_refs[2 * g + side][:, cols] for g in range(4))
-                for g, part in enumerate((own, a, pick(flags_ref, b, c), c)):
-                    at = slice((2 * g + side) * half, (2 * g + side + 1) * half)
-                    part = dot_split((high[:, at], low[:, at]), split(part), COLS)
-                    if g < 3:
-                        upper = upper + part
-                    else:
-                        lower = lower + part
+            upper, lower = prod_ref[:half, cols], prod_ref[half:, cols]
+            for i, ref in enumerate(s_refs):
+                at = slice(i * half, (i + 1) * half)
+                part = dot_split((high[:, at], low[:, at]), split(ref[:, cols]), COLS)
+                if i < 2:
+                    upper = upper + part
+                else:
+                    lower = lower + part
             out_ref[:half, cols] = upper
             out_ref[half:, cols] = lower
 
-    args = [*own, *first, *[part for quad in ks for part in quad], *s, products, sums]
-    return products_call(kernel, flags, args, [2 * half, width], [half, 8 * half])
-
-
-def last_sums(flags, pieces, ks_b, ks_c, sums):
-    half = pieces[0].shape[0]
-
-    def kernel(flags_ref, p0, p1, p2, p3, *refs):
-        b_refs, c_refs, (sum_ref, left_ref, right_ref, out_ref) = refs[:4], refs[4:8], refs[8:]
-        tops = ordered(flags_ref, [p[...] for p in (p0, p1, p2, p3)])
-        left_ref[...], right_ref[...] = tops
+    args = [*pieces, *[part for terms in ks for part in terms], *s, products, sums]
+    return products_call(kernel, flags, args, [2 * half, width], [half, 6 * half])
+
+
+def last_sums(flags, second, third, ks_b, ks_c, sums):
+    half = third[0].shape[0]
+
+    def kernel(flags_ref, *refs):
+        edge = flags_ref[1] == 1
+        two = returned(flags_ref, [ref[...] for ref in refs[:5]])
+        three = ordered(flags_ref, [ref[...] for ref in refs[5:9]])
+        b_refs, c_refs, sum_ref, outs = refs[9:13], refs[13:17], refs[17], refs[18:]
         hsic = jnp.zeros((1, 1), jnp.float32)
         for side in range(2):
-            bottom = pick(flags_ref, summed(c_refs, side), summed(b_refs, side))
-            hsic = hsic + jnp.sum(tops[side] * bottom, keepdims=True)
-        out_ref[...] = sum_ref[...] + spread(out_ref, hsic, 0.0)
-
-    return call(kernel, flags, [*pieces, *ks_b, *ks_c, sums], [(half, half)] * 2 + [(8, 128)])
+            top_b = jnp.where(edge, two[side], three[side])
+            top_c = jnp.where(edge, three[side], two[side])
+            outs[side][...], outs[2 + side][...] = top_b, top_c
+            both = top_b * summed(b_refs, side) + top_c * summed(c_refs, side)
+            hsic = hsic + jnp.sum(both, keepdims=True)
+        outs[4][...] = sum_ref[...] + spread(outs[4], hsic, 0.0)
+
+    return call(kernel, flags, [*second, *third, *ks_b, *ks_c, sums], [(half, half)] * 4 + [(8, 128)])
 
 
 def last_products(flags, kt, s, products):
     half, width = s[0].shape
     chunk = width // 4
 
-    def kernel(flags_ref, l_ref, r_ref, bl, br, cl, cr, prod_ref, out_ref):
-        left, right = split(l_ref[...]), split(r_ref[...])
+    def kernel(flags_ref, *refs):
+        left = [split(ref[...]) for ref in refs[:4]]
+        s_refs, prod_ref, out_ref = refs[4:8], refs[8], refs[9]
         for j in range(4):
             cols = slice(j * chunk, (j + 1) * chunk)
             total = prod_ref[:half, cols]
-            total = total + dot_split(left, split(pick(flags_ref, cl[:, cols], bl[:, cols])), COLS)
-            total = total + dot_split(right, split(pick(flags_ref, cr[:, cols], br[:, cols])), COLS)
+            for part, ref in zip(left, s_refs):
+                total = total + dot_split(part, split(ref[:, cols]), COLS)
             out_ref[:, cols] = total
 
     return call(kernel, flags, [*kt, *s, products], [(half, width)])[0]
@@ -384,8 +408,7 @@
 
     s_half = lax.dynamic_slice_in_dim(student, k * half, half, 0)
     near, mid = send(s_half, PAIRS), send(s_half, MIDDLE)
-    s_own = (s_half, lax.dynamic_slice_in_dim(student, (1 - k) * half, half, 0))
-    ks_own = chip_sum(gram_part(flags, s_half, s_own))
+    ks_own = chip_sum(own_gram(flags, student))
     t_quarter = lax.dynamic_slice_in_dim(teacher, c * quarter, quarter, 0)
     kept, away, *t_split = teacher_parts(flags, [teacher], [t_quarter], True)
     own = swap_rows(kept, away)
@@ -395,42 +418,40 @@
     t_in = send(t_quarter, INWARD)
     pieces_own = same_plane(own)
     s_a = both_halves(near)
-    ks_a = chip_sum(gram_part(flags, s_half, s_a))
-    far_edge, far_mid, t_in, mid, t_quarter, s_a, ks_a, pieces_own = step(
-        (far_edge, far_mid, t_in, mid, t_quarter, s_a, ks_a, pieces_own)
+    part_a = sum_x_y(*gram_part(flags, s_half, s_a))
+    far_edge, far_mid, t_in, mid, t_quarter, s_a, part_a, pieces_own = step(
+        (far_edge, far_mid, t_in, mid, t_quarter, s_a, part_a, pieces_own)
     )
 
     last_edge, t_cross = send(far_mid, OUTWARD), send(t_in, MIDDLE)
+    ks_a = terms_y_x(*part_a)
     s_b = both_halves(jnp.where(edge, far_edge, mid))
     first = swap_rows(*teacher_parts(flags, t_split, [t_in]))
     back_in = send(first, OUTWARD)
     ks_b = chip_sum(gram_part(flags, s_half, s_b))
-    last_edge, t_cross, far_mid, t_quarter, s_b, first, ks_b = step(
-        (last_edge, t_cross, far_mid, t_quarter, s_b, first, ks_b)
-    )
-
-    part = quarter // 2
-    edge_1, mid_1 = send(t_cross[:part], OUTWARD), send(t_quarter[:part], MIDDLE)
+    products, sums = first_products(flags, pieces_own, [ks_own, ks_a], student, s_a)
+    t_cross, far_mid, t_quarter, s_b, first, back_in, ks_b, products, sums = step(
+        (t_cross, far_mid, t_quarter, s_b, first, back_in, ks_b, products, sums)
+    )
+
+    t_edge, t_mid = send(t_cross, OUTWARD), send(t_quarter, MIDDLE)
+    pieces_first = mixed(jnp.where(edge, back_in, first))
+    s_c = both_halves(jnp.where(edge, last_edge, far_mid))
+    part_c = sum_x_y(*gram_part(flags, s_half, s_c))
+    pieces_first, part_c, t_cross = step((pieces_first, part_c, t_cross))
     cross = swap_rows(*teacher_parts(flags, t_split, [t_cross]))
     back_cross = send(cross, FAR)
-    s_c = both_halves(jnp.where(edge, last_edge, far_mid))
-    part_c = sum_x_y(*gram_part(flags, s_half, s_c))
-    products, sums = first_products(flags, [ks_own, ks_a, ks_b], [*s_own, *s_a, *s_b])
-    edge_1, mid_1, t_cross, t_quarter, back_in, part_c, cross, products, sums = step(
-        (edge_1, mid_1, t_cross, t_quarter, back_in, part_c, cross, products, sums)
-    )
-    edge_2, mid_2 = send(t_cross[part:], OUTWARD), send(t_quarter[part:], MIDDLE)
     ks_c = terms_y_x(*part_c)
-    pieces_first = mixed(jnp.concatenate([jnp.where(edge, back_in, first), jnp.where(edge, back_cross, cross)], 1))
-    edge_2, mid_2, pieces_first = step((edge_2, mid_2, pieces_first))
-
-    pieces = same_plane(swap_rows(*teacher_parts(flags, t_split, [(edge_1, mid_1), (edge_2, mid_2)])))
-    s_all, ks_all = [*s_own, *s_a, *s_b, *s_c], [ks_own, ks_a, ks_b, ks_c]
-    products, sums = second_products(flags, pieces_own, pieces_first, ks_all, s_all, products, sums)
-    left, right, sums = last_sums(flags, pieces, ks_b, ks_c, sums)
+    t_edge, t_mid, cross = step((t_edge, t_mid, cross))
+
+    pieces_third = same_plane(swap_rows(*teacher_parts(flags, t_split, [(t_edge, t_mid)])))
+    pieces_second = mixed(jnp.where(edge, back_cross, cross))
+    s_abc = [*s_a, *s_b, *s_c]
+    products, sums = second_products(flags, pieces_first, [ks_a, ks_b, ks_c], s_abc, products, sums)
+    *kt_bc, sums = last_sums(flags, pieces_second, pieces_third, ks_b, ks_c, sums)
     sums = sums + lax.ppermute(sums, "tcol", CORES)
     planes = [sums] + [lax.ppermute(sums, "tok", [(i, (i + s) % 4) for i in range(4)]) for s in (1, 2, 3)]
-    upper = last_products(flags, (left, right), [*s_b, *s_c], products)
+    upper = last_products(flags, kt_bc, [*s_b, *s_c], products)
     scale = -2.0 * tokens_all * features
     return finish(flags, upper, products, planes, teacher_norm.reshape(1, 1), scale)
 

time: 162 us -> 160 us (0.988)
  waiting for transfers between devices: 59.6 us -> 56.5 us
  Pallas kernels: 26.8 us -> 28.8 us
    ppermute x4 -> x8, waiting for transfers between devices: 8.21 us -> 13.2 us  [mixed(): lax.ppermute(piece, PLANE, piece_shift(hi, lo))]
    ppermute x13 -> x11, waiting for transfers between devices: 19.5 us -> 14.7 us  [send(): return lax.ppermute(x, 'tok', perm)]
    ppermute x4 -> x8, starting transfers between devices: 2.91 us -> 5.96 us  [mixed(): lax.ppermute(piece, PLANE, piece_shift(hi, lo))]
    ppermute x13 -> x11, starting transfers between devices: 23.8 us -> 21.8 us  [send(): return lax.ppermute(x, 'tok', perm)]
    pallas_call x7, Pallas kernels: 11.3 us -> 13 us  [call(): pl.pallas_call(kernel, out_shape=outs, in_specs=[FLAGS] + [whole] * len(a...]
  transfers between devices with their start and end apart: 50 -> 52, of which waited for: 22 -> 22; matrix products, arithmetic and copies ran while one was open for 2% -> 2% of each run, Pallas kernels for 15% -> 16%
where the time goes in v2:
time: 160 us
  starting transfers between devices  65.7 us (41%)
  waiting for transfers between devices  56.5 us (35%)
  Pallas kernels  28.8 us (18%)
  local copies, waits for them, and re-layouts  4.94 us (3%)
  other arithmetic  2.76 us (2%)
    ppermute x11, starting transfers between devices, send(): return lax.ppermute(x, 'tok', perm)  21.8 us
    ppermute x11, waiting for transfers between devices, send(): return lax.ppermute(x, 'tok', perm)  14.7 us
    ppermute x8, waiting for transfers between devices, mixed(): lax.ppermute(piece, PLANE, piece_shift(hi, lo))  13.2 us
    pallas_call x7, Pallas kernels, call(): pl.pallas_call(kernel, out_shape=outs, in_specs=[FLAGS] + [whole] * len(a...  13 us
    ppermute x4, waiting for transfers between devices, sum_x_y(): left = left + lax.ppermute(left, 'scol', chip_shift(1))  12.9 us
    ppermute x6, starting transfers between devices, same_plane(): lax.ppermute(piece, 'scol', chip_shift(s))  9.45 us
    pallas_call x2, Pallas kernels, products_call(): pl.pallas_call(kernel, out_shape=outs, in_specs=[FLAGS] + [whole] * len(a...  8.17 us
    pallas_call x4, Pallas kernels, teacher_parts(): pl.pallas_call(kernel, out_shape=outs, in_specs=[FLAGS] + [whole] * (len(...  7.69 us
  transfers between devices with their start and end apart: 52, of which 22 were waited for; matrix products, arithmetic and copies ran while one was open for 2% of the time, Pallas kernels for 16%

profile of v2, /device:TPU:0, one launch (start us, length us, event | category | flops | bytes accessed | tf_op | source)
XLA Modules:
  0.0 159.8 jit_solution(9227635663287986244)
XLA Ops:
  1.4 3.1 %collective-permute-start = (f32[256,1024]{1,0:T(8,128)S(1)}, f32[256,1024]{1,0:T(8,128)}, u32[]{:S(2)}, u32[]{:S(2)}) collective-permute-start(f32[256,1024]{1,0:T(8,128)S(1)} %constant_dynamic-slice_fusion.1.own_ref), channel_id=1, source_target_pairs={{0,8},{8,0},{16,24},{24,16},{1,9},{9,1},{17,25},{25,17},{2,10},{10... | collective-permute-start | bytes 3145736 | tf_op jit(solution)/shard_map/ppermute | solution.py:377
  4.5 1.7 %collective-permute-start.1 = (f32[256,1024]{1,0:T(8,128)S(1)}, f32[256,1024]{1,0:T(8,128)}, u32[]{:S(2)}, u32[]{:S(2)}) collective-permute-start(f32[256,1024]{1,0:T(8,128)S(1)} %constant_dynamic-slice_fusion.1.own_ref), channel_id=1, source_target_pairs={{8,16},{16,8},{9,17},{17,9},{10,18},{18,10},{11,19},{19,11},{12,20... | collective-permute-start | bytes 3145736 | tf_op jit(solution)/shard_map/ppermute | solution.py:377
  6.3 2.3 %shard_map.37 = (f32[256,256]{1,0:T(8,128)}, f32[256,256]{1,0:T(8,128)S(1)}) custom-call(s32[4]{0:T(128)S(1)} %pad_add_fusion.flags_ref, f32[512,1024]{1,0:T(8,128)S(1)} %copy-done), custom_call_target="tpu_custom_call" | custom-call | tf_op jit(solution)/shard_map/pallas_call | solution.py:114
  11.6 5.1 %collective-permute-done.2 = f32[256,256]{1,0:T(8,128)} collective-permute-done((f32[256,256]{1,0:T(8,128)}, f32[256,256]{1,0:T(8,128)}, u32[]{:S(2)}, u32[]{:S(2)}) %collective-permute-start.2) | collective-permute-done | bytes 262176 | tf_op jit(solution)/shard_map/ppermute | solution.py:383
  17.7 1.6 collective-permute-start.3
  23.2 2.2 %copy-done.1 = f32[512,2048]{1,0:T(8,128)S(1)} copy-done((f32[512,2048]{1,0:T(8,128)S(1)}, f32[512,2048]{1,0:T(8,128)}, u32[]{:S(2)}) %copy-start.1) | copy-done | bytes 4194328
  25.3 2.2 %shard_map.38 = (f32[256,128]{1,0:T(8,128)S(1)}, f32[256,128]{1,0:T(8,128)S(1)}, bf16[512,2048]{1,0:T(8,128)(2,1)S(1)}, bf16[512,2048]{1,0:T(8,128)(2,1)S(1)}) custom-call(s32[4]{0:T(128)S(1)} %pad_add_fusion.flags_ref, f32[512,2048]{1,0:T(8,128)S(1)} %copy-done.1, f32[128,2048]{1,0:T(8,128)S(1)} %constant_dynamic-slice_fusion.refs_1_), custom_call_target="tpu_custom_call" | custom-call | tf_op jit(solution)/shard_map/pallas_call | solution.py:197
  31.3 8.3 %collective-permute-start.9 = (f32[128,2048]{1,0:T(8,128)S(1)}, f32[128,2048]{1,0:T(8,128)S(1)}, u32[]{:S(2)}, u32[]{:S(2)}) collective-permute-start(f32[128,2048]{1,0:T(8,128)S(1)} %constant_dynamic-slice_fusion.refs_1_), channel_id=1, source_target_pairs={{0,8},{24,16},{1,9},{25,17},{2,10},{26,18},{3,11},{27,19},{4,12},{... | collective-permute-start | bytes 3145736 | tf_op jit(solution)/shard_map/ppermute | solution.py:377
  41.1 2.3 %shard_map.39 = (f32[256,256]{1,0:T(8,128)S(1)}, f32[256,256]{1,0:T(8,128)S(1)}) custom-call(s32[4]{0:T(128)S(1)} %pad_add_fusion.flags_ref, f32[256,1024]{1,0:T(8,128)S(1)} %constant_dynamic-slice_fusion.1.own_ref, f32[256,1024]{1,0:T(8,128)} %collective-permute-done.first_ref.refs_13_.refs_17_, ...), custom_call_target="tpu_custom_call" | custom-call | tf_op jit(solution)/shard_map/pallas_call | solution.py:114
  46.5 4.9 %collective-permute-done.11 = f32[256,256]{1,0:T(8,128)S(1)} collective-permute-done((f32[256,256]{1,0:T(8,128)S(1)}, f32[256,256]{1,0:T(8,128)S(1)}, u32[]{:S(2)}, u32[]{:S(2)}) %collective-permute-start.11) | collective-permute-done | bytes 262176 | tf_op jit(solution)/shard_map/ppermute | solution.py:383
  52.9 1.9 %collective-permute-start.15 = (f32[256,128]{1,0:T(8,128)S(1)}, f32[256,128]{1,0:T(8,128)S(1)}, u32[]{:S(2)}, u32[]{:S(2)}) collective-permute-start(f32[256,128]{1,0:T(8,128)S(1)} %add.55.refs_0_), channel_id=1, source_target_pairs={{0,6},{2,4},{4,2},{6,0},{1,7},{3,5},{5,3},{7,1},{8,14},{10,12},{12... | collective-permute-start | bytes 393224 | tf_op jit(solution)/shard_map/ppermute | solution.py:402
  54.9 4.2 %collective-permute-done.14.refs_2_ = f32[256,128]{1,0:T(8,128)S(1)} collective-permute-done((f32[256,128]{1,0:T(8,128)S(1)}, f32[256,128]{1,0:T(8,128)S(1)}, u32[]{:S(2)}, u32[]{:S(2)}) %collective-permute-start.14) | collective-permute-done | bytes 131104 | tf_op jit(solution)/shard_map/ppermute | solution.py:402
  59.1 2.2 %collective-permute-done.7 = f32[256,1024]{1,0:T(8,128)S(1)} collective-permute-done((f32[256,1024]{1,0:T(8,128)}, f32[256,1024]{1,0:T(8,128)S(1)}, u32[]{:S(2)}, u32[]{:S(2)}) %collective-permute-start.7) | collective-permute-done | bytes 1048608 | tf_op jit(solution)/shard_map/ppermute | solution.py:377
  65.2 1.6 shard_map.41
  70.3 1.8 %shard_map.40 = (f32[256,128]{1,0:T(8,128)S(1)}, f32[256,128]{1,0:T(8,128)S(1)}) custom-call(s32[4]{0:T(128)S(1)} %pad_add_fusion.flags_ref, bf16[512,2048]{1,0:T(8,128)(2,1)S(1)} %get-tuple-element.85.refs_0_, bf16[512,2048]{1,0:T(8,128)(2,1)S(1)} %get-tuple-element.86.refs_1_, f32[128,2048]{1,0:T(8,128)S(1)} %collective-permute-done.9.refs_2_), custom_call_target="tpu_custom_call" | custom-call | tf_op jit(solution)/shard_map/pallas_call | solution.py:197
  72.2 3.0 %collective-permute-done.20 = f32[256,256]{1,0:T(8,128)S(1)} collective-permute-done((f32[256,256]{1,0:T(8,128)S(1)}, f32[256,256]{1,0:T(8,128)S(1)}, u32[]{:S(2)}, u32[]{:S(2)}) %collective-permute-start.20) | collective-permute-done | bytes 262176 | tf_op jit(solution)/shard_map/ppermute | solution.py:383
  80.4 2.0 %collective-permute-done.24.refs_9_.refs_6_ = f32[256,256]{1,0:T(8,128)S(1)} collective-permute-done((f32[256,256]{1,0:T(8,128)S(1)}, f32[256,256]{1,0:T(8,128)S(1)}, u32[]{:S(2)}, u32[]{:S(2)}) %collective-permute-start.24) | collective-permute-done | bytes 262176 | tf_op jit(solution)/shard_map/ppermute | solution.py:390
  84.2 3.9 %shard_map.42 = (f32[512,1024]{1,0:T(8,128)S(1)}, f32[8,128]{1,0:T(8,128)S(1)}) custom-call(s32[4]{0:T(128)S(1)} %pad_add_fusion.flags_ref, f32[256,128]{1,0:T(8,128)S(1)} %add.55.refs_0_, f32[256,128]{1,0:T(8,128)S(1)} %collective-permute-done.13.refs_1_, f32[256,128]{1,0:T(8,128)S(1)} %collective-permute-done.14.refs_2_, ...), custom_call_target="tpu_custom_call" | custom-call | tf_op jit(solution)/shard_map/pallas_call | solution.py:230
  88.1 7.9 %collective-permute-done.19 = f32[256,128]{1,0:T(8,128)S(1)} collective-permute-done((f32[256,128]{1,0:T(8,128)S(1)}, f32[256,128]{1,0:T(8,128)S(1)}, u32[]{:S(2)}, u32[]{:S(2)}) %collective-permute-start.19) | collective-permute-done | bytes 131104 | tf_op jit(solution)/shard_map/ppermute | solution.py:377
  104.2 7.5 %collective-permute-done.26.refs_1_ = f32[256,128]{1,0:T(8,128)S(1)} collective-permute-done((f32[256,128]{1,0:T(8,128)S(1)}, f32[256,128]{1,0:T(8,128)S(1)}, u32[]{:S(2)}, u32[]{:S(2)}) %collective-permute-start.26) | collective-permute-done | bytes 131104 | tf_op jit(solution)/shard_map/ppermute | solution.py:406
  115.1 2.9 %collective-permute-done.28.refs_3_ = f32[256,128]{1,0:T(8,128)S(1)} collective-permute-done((f32[256,128]{1,0:T(8,128)S(1)}, f32[256,128]{1,0:T(8,128)S(1)}, u32[]{:S(2)}, u32[]{:S(2)}) %collective-permute-start.28) | collective-permute-done | bytes 131104 | tf_op jit(solution)/shard_map/ppermute | solution.py:406
  118.0 1.8 %shard_map.44 = (f32[256,128]{1,0:T(8,128)S(1)}, f32[256,128]{1,0:T(8,128)S(1)}) custom-call(s32[4]{0:T(128)S(1)} %pad_add_fusion.flags_ref, bf16[512,2048]{1,0:T(8,128)(2,1)S(1)} %get-tuple-element.85.refs_0_, bf16[512,2048]{1,0:T(8,128)(2,1)S(1)} %get-tuple-element.86.refs_1_, f32[128,2048]{1,0:T(8,128)S(1)} %collective-permute-done.16.refs_2_), custom_call_target="tpu_custom_call" | custom-call | tf_op jit(solution)/shard_map/pallas_call | solution.py:197
  119.8 2.6 %collective-permute-start.34 = (f32[256,128]{1,0:T(8,128)S(1)}, f32[256,128]{1,0:T(8,128)S(1)}, u32[]{:S(2)}, u32[]{:S(2)}) collective-permute-start(f32[256,128]{1,0:T(8,128)S(1)} %get-tuple-element.124), channel_id=1, source_target_pairs={{0,1},{1,0},{2,3},{3,2},{4,5},{5,4},{6,7},{7,6},{8,9},{9,8},{10,11... | collective-permute-start | bytes 393224 | tf_op jit(solution)/shard_map/ppermute | solution.py:399
  127.1 1.8 %shard_map.45 = (f32[256,128]{1,0:T(8,128)S(1)}, f32[256,128]{1,0:T(8,128)S(1)}) custom-call(s32[4]{0:T(128)S(1)} %pad_add_fusion.flags_ref, bf16[512,2048]{1,0:T(8,128)(2,1)S(1)} %get-tuple-element.85.refs_0_, bf16[512,2048]{1,0:T(8,128)(2,1)S(1)} %get-tuple-element.86.refs_1_, f32[128,2048]{1,0:T(8,128)S(1)} %collective-permute-done.36.refs_2_, ...), custom_call_target="tpu_custom_call" | custom-call | tf_op jit(solution)/shard_map/pallas_call | solution.py:197
  129.0 3.6 %collective-permute-done.35 = f32[256,128]{1,0:T(8,128)S(1)} collective-permute-done((f32[256,128]{1,0:T(8,128)S(1)}, f32[256,128]{1,0:T(8,128)S(1)}, u32[]{:S(2)}, u32[]{:S(2)}) %collective-permute-start.35) | collective-permute-done | bytes 131104 | tf_op jit(solution)/shard_map/ppermute | solution.py:377
  137.1 1.9 %collective-permute-done.38.refs_1_ = f32[256,128]{1,0:T(8,128)S(1)} collective-permute-done((f32[256,128]{1,0:T(8,128)S(1)}, f32[256,128]{1,0:T(8,128)S(1)}, u32[]{:S(2)}, u32[]{:S(2)}) %collective-permute-start.38) | collective-permute-done | bytes 131104 | tf_op jit(solution)/shard_map/ppermute | solution.py:406
  139.1 1.6 %collective-permute-start.44 = (f32[256,128]{1,0:T(8,128)S(1)}, f32[256,128]{1,0:T(8,128)S(1)}, u32[]{:S(2)}, u32[]{:S(2)}) collective-permute-start(f32[256,128]{1,0:T(8,128)S(1)} %add.64.refs_5_), channel_id=1, source_target_pairs={{0,4},{2,6},{4,0},{6,2},{1,5},{3,7},{5,1},{7,3},{8,12},{10,14},{12... | collective-permute-start | bytes 393224 | tf_op jit(solution)/shard_map/ppermute | solution.py:402
  142.0 4.3 %shard_map.46 = (f32[512,1024]{1,0:T(8,128)S(1)}, f32[8,128]{1,0:T(8,128)S(1)}) custom-call(s32[4]{0:T(128)S(1)} %pad_add_fusion.flags_ref, f32[256,128]{1,0:T(8,128)S(1)} %broadcast_select_fusion.3.refs_0_, f32[256,128]{1,0:T(8,128)S(1)} %collective-permute-done.26.refs_1_, f32[256,128]{1,0:T(8,128)S(1)} %collective-permute-done.27.refs_2_, ...), custom_call_target="tpu_custom_call" | custom-call | tf_op jit(solution)/shard_map/pallas_call | solution.py:230
  146.3 1.9 %collective-permute-done.44.refs_7_ = f32[256,128]{1,0:T(8,128)S(1)} collective-permute-done((f32[256,128]{1,0:T(8,128)S(1)}, f32[256,128]{1,0:T(8,128)S(1)}, u32[]{:S(2)}, u32[]{:S(2)}) %collective-permute-start.44) | collective-permute-done | bytes 131104 | tf_op jit(solution)/shard_map/ppermute | solution.py:402
  150.5 1.7 %collective-permute-start.49 = (f32[8,128]{1,0:T(8,128)S(1)}, f32[8,128]{1,0:T(8,128)S(1)}, u32[]{:S(2)}, u32[]{:S(2)}) collective-permute-start(f32[8,128]{1,0:T(8,128)S(1)} %add.65.refs_0_), channel_id=1, source_target_pairs={{0,8},{8,16},{16,24},{24,0},{1,9},{9,17},{17,25},{25,1},{2,10},{10... | collective-permute-start | bytes 12296 | tf_op jit(solution)/shard_map/ppermute | solution.py:453
  155.5 2.4 %shard_map.48.up_ref = f32[256,1024]{1,0:T(8,128)S(1)} custom-call(s32[4]{0:T(128)S(1)} %pad_add_fusion.flags_ref, f32[256,256]{1,0:T(8,128)S(1)} %get-tuple-element.147.refs_0_, f32[256,256]{1,0:T(8,128)S(1)} %get-tuple-element.148.refs_1_, f32[256,256]{1,0:T(8,128)S(1)} %get-tuple-element.149.refs_2_, f32[256,256]{1,0:T(8,128)S(1)} %get-tuple-element.150.refs_3_, ...), custom_call_target="tpu_custom_call" | custom-call | tf_op jit(solution)/shard_map/pallas_call | solution.py:114
  158.0 1.8 %shard_map.49 = f32[256,1024]{1,0:T(8,128)} custom-call(s32[4]{0:T(128)S(1)} %pad_add_fusion.flags_ref, f32[256,1024]{1,0:T(8,128)S(1)} %shard_map.48.up_ref, f32[512,1024]{1,0:T(8,128)S(1)} %get-tuple-element.151.refs_8_.prod_ref, f32[1,1]{1,0:T(1,128)} %bitcast.5.norm_ref, f32[8,128]{1,0:T(8,128)S(1)} %add.65.refs_0_, ...), custom_call_target="tpu_custom_call" | custom-call | tf_op jit(solution)/shard_map/pallas_call | solution.py:114
  (109 shorter events, 60.8 us)
Async XLA Ops:
  1.4 27.6 %collective-permute-start = (f32[256,1024]{1,0:T(8,128)S(1)}, f32[256,1024]{1,0:T(8,128)}, u32[]{:S(2)}, u32[]{:S(2)}) collective-permute-start(f32[256,1024]{1,0:T(8,128)S(1)} %constant_dynamic-slice_fusion.1.own_ref), channel_id=1, source_target_pairs={{0,8},{8,0},{16,24},{24,16},{1,9},{9,1},{17,25},{25,17},{2,10},{10... | collective-permute-start | bytes 3145736 | tf_op jit(solution)/shard_map/ppermute | solution.py:377
  4.5 24.5 %collective-permute-start.1 = (f32[256,1024]{1,0:T(8,128)S(1)}, f32[256,1024]{1,0:T(8,128)}, u32[]{:S(2)}, u32[]{:S(2)}) collective-permute-start(f32[256,1024]{1,0:T(8,128)S(1)} %constant_dynamic-slice_fusion.1.own_ref), channel_id=1, source_target_pairs={{8,16},{16,8},{9,17},{17,9},{10,18},{18,10},{11,19},{19,11},{12,20... | collective-permute-start | bytes 3145736 | tf_op jit(solution)/shard_map/ppermute | solution.py:377
  8.6 8.1 %collective-permute-start.2 = (f32[256,256]{1,0:T(8,128)}, f32[256,256]{1,0:T(8,128)}, u32[]{:S(2)}, u32[]{:S(2)}) collective-permute-start(f32[256,256]{1,0:T(8,128)} %get-tuple-element.79), channel_id=1, source_target_pairs={{0,2},{2,0},{4,6},{6,4},{1,3},{3,1},{5,7},{7,5},{8,10},{10,8},{12,... | collective-permute-start | bytes 786440 | tf_op jit(solution)/shard_map/ppermute | solution.py:383
  10.0 9.2 %collective-permute-start.4 = (f32[256,256]{1,0:T(8,128)S(1)}, f32[256,256]{1,0:T(8,128)}, u32[]{:S(2)}, u32[]{:S(2)}) collective-permute-start(f32[256,256]{1,0:T(8,128)S(1)} %get-tuple-element.80), channel_id=1, source_target_pairs={{0,4},{2,6},{4,0},{6,2},{1,5},{3,7},{5,1},{7,3},{8,12},{10,14},{12... | collective-permute-start | bytes 786440 | tf_op jit(solution)/shard_map/ppermute | solution.py:384
  17.7 11.3 %collective-permute-start.3 = (f32[256,256]{1,0:T(8,128)S(1)}, f32[256,256]{1,0:T(8,128)S(1)}, u32[]{:S(2)}, u32[]{:S(2)}) collective-permute-start(f32[256,256]{1,0:T(8,128)S(1)} %add.53.refs_4_), channel_id=1, source_target_pairs={{0,4},{2,6},{4,0},{6,2},{1,5},{3,7},{5,1},{7,3},{8,12},{10,14},{12... | collective-permute-start | bytes 786440 | tf_op jit(solution)/shard_map/ppermute | solution.py:390
  20.3 8.8 %collective-permute-start.5 = (f32[256,256]{1,0:T(8,128)S(1)}, f32[256,256]{1,0:T(8,128)S(1)}, u32[]{:S(2)}, u32[]{:S(2)}) collective-permute-start(f32[256,256]{1,0:T(8,128)S(1)} %add.54.refs_6_), channel_id=1, source_target_pairs={{0,2},{2,0},{4,6},{6,4},{1,3},{3,1},{5,7},{7,5},{8,10},{10,8},{12,... | collective-permute-start | bytes 786440 | tf_op jit(solution)/shard_map/ppermute | solution.py:392
  29.0 12.1 %collective-permute-start.10 = (f32[256,1024]{1,0:T(8,128)}, f32[256,1024]{1,0:T(8,128)S(1)}, u32[]{:S(2)}, u32[]{:S(2)}) collective-permute-start(f32[256,1024]{1,0:T(8,128)} %collective-permute-done.first_ref.refs_13_.refs_17_), channel_id=1, source_target_pairs={{0,1},{1,0},{2,3},{3,2},{4,5},{5,4},{6,7},{7,6},{8,9},{9,8},{10,11... | collective-permute-start | bytes 3145736 | tf_op jit(solution)/shard_map/ppermute | solution.py:380
  29.3 32.0 %collective-permute-start.8 = (f32[256,1024]{1,0:T(8,128)}, f32[256,1024]{1,0:T(8,128)S(1)}, u32[]{:S(2)}, u32[]{:S(2)}) collective-permute-start(f32[256,1024]{1,0:T(8,128)} %collective-permute-done.first_ref.refs_13_.refs_17_), channel_id=1, source_target_pairs={{8,16},{16,8},{9,17},{17,9},{10,18},{18,10},{11,19},{19,11},{12,20... | collective-permute-start | bytes 3145736 | tf_op jit(solution)/shard_map/ppermute | solution.py:377
  30.0 31.3 %collective-permute-start.7 = (f32[256,1024]{1,0:T(8,128)}, f32[256,1024]{1,0:T(8,128)S(1)}, u32[]{:S(2)}, u32[]{:S(2)}) collective-permute-start(f32[256,1024]{1,0:T(8,128)} %collective-permute-done.1), channel_id=1, source_target_pairs={{8,0},{16,24},{9,1},{17,25},{10,2},{18,26},{11,3},{19,27},{12,4},{... | collective-permute-start | bytes 3145736 | tf_op jit(solution)/shard_map/ppermute | solution.py:377
  31.3 31.0 %collective-permute-start.9 = (f32[128,2048]{1,0:T(8,128)S(1)}, f32[128,2048]{1,0:T(8,128)S(1)}, u32[]{:S(2)}, u32[]{:S(2)}) collective-permute-start(f32[128,2048]{1,0:T(8,128)S(1)} %constant_dynamic-slice_fusion.refs_1_), channel_id=1, source_target_pairs={{0,8},{24,16},{1,9},{25,17},{2,10},{26,18},{3,11},{27,19},{4,12},{... | collective-permute-start | bytes 3145736 | tf_op jit(solution)/shard_map/ppermute | solution.py:377
  43.4 7.9 %collective-permute-start.11 = (f32[256,256]{1,0:T(8,128)S(1)}, f32[256,256]{1,0:T(8,128)S(1)}, u32[]{:S(2)}, u32[]{:S(2)}) collective-permute-start(f32[256,256]{1,0:T(8,128)S(1)} %get-tuple-element.90), channel_id=1, source_target_pairs={{0,2},{2,0},{4,6},{6,4},{1,3},{3,1},{5,7},{7,5},{8,10},{10,8},{12,... | collective-permute-start | bytes 786440 | tf_op jit(solution)/shard_map/ppermute | solution.py:383
  45.0 7.9 %collective-permute-start.12 = (f32[256,256]{1,0:T(8,128)S(1)}, f32[256,256]{1,0:T(8,128)S(1)}, u32[]{:S(2)}, u32[]{:S(2)}) collective-permute-start(f32[256,256]{1,0:T(8,128)S(1)} %get-tuple-element.91), channel_id=1, source_target_pairs={{0,4},{2,6},{4,0},{6,2},{1,5},{3,7},{5,1},{7,3},{8,12},{10,14},{12... | collective-permute-start | bytes 786440 | tf_op jit(solution)/shard_map/ppermute | solution.py:384
  62.5 33.5 %collective-permute-start.16 = (f32[128,2048]{1,0:T(8,128)S(1)}, f32[128,2048]{1,0:T(8,128)S(1)}, u32[]{:S(2)}, u32[]{:S(2)}) collective-permute-start(f32[128,2048]{1,0:T(8,128)S(1)} %collective-permute-done.9.refs_2_), channel_id=1, source_target_pairs={{8,16},{16,8},{9,17},{17,9},{10,18},{18,10},{11,19},{19,11},{12,20... | collective-permute-start | bytes 3145736 | tf_op jit(solution)/shard_map/ppermute | solution.py:377
  63.2 32.8 %collective-permute-start.30 = (f32[256,1024]{1,0:T(8,128)S(1)}, f32[256,1024]{1,0:T(8,128)S(1)}, u32[]{:S(2)}, u32[]{:S(2)}) collective-permute-start(f32[256,1024]{1,0:T(8,128)S(1)} %collective-permute-done.8), channel_id=1, source_target_pairs={{8,0},{16,24},{9,1},{17,25},{10,2},{18,26},{11,3},{19,27},{12,4},{... | collective-permute-start | bytes 3145736 | tf_op jit(solution)/shard_map/ppermute | solution.py:377
  66.8 8.4 %collective-permute-start.20 = (f32[256,256]{1,0:T(8,128)S(1)}, f32[256,256]{1,0:T(8,128)S(1)}, u32[]{:S(2)}, u32[]{:S(2)}) collective-permute-start(f32[256,256]{1,0:T(8,128)S(1)} %get-tuple-element.100), channel_id=1, source_target_pairs={{0,2},{2,0},{4,6},{6,4},{1,3},{3,1},{5,7},{7,5},{8,10},{10,8},{12,... | collective-permute-start | bytes 786440 | tf_op jit(solution)/shard_map/ppermute | solution.py:383
  68.3 9.2 %collective-permute-start.22 = (f32[256,256]{1,0:T(8,128)S(1)}, f32[256,256]{1,0:T(8,128)S(1)}, u32[]{:S(2)}, u32[]{:S(2)}) collective-permute-start(f32[256,256]{1,0:T(8,128)S(1)} %get-tuple-element.101), channel_id=1, source_target_pairs={{0,4},{2,6},{4,0},{6,2},{1,5},{3,7},{5,1},{7,3},{8,12},{10,14},{12... | collective-permute-start | bytes 786440 | tf_op jit(solution)/shard_map/ppermute | solution.py:384
  69.8 12.5 %collective-permute-start.24 = (f32[256,256]{1,0:T(8,128)S(1)}, f32[256,256]{1,0:T(8,128)S(1)}, u32[]{:S(2)}, u32[]{:S(2)}) collective-permute-start(f32[256,256]{1,0:T(8,128)S(1)} %add.56.refs_8_.refs_5_), channel_id=1, source_target_pairs={{0,4},{2,6},{4,0},{6,2},{1,5},{3,7},{5,1},{7,3},{8,12},{10,14},{12... | collective-permute-start | bytes 786440 | tf_op jit(solution)/shard_map/ppermute | solution.py:390
  78.9 17.2 %collective-permute-start.21 = (f32[256,256]{1,0:T(8,128)S(1)}, f32[256,256]{1,0:T(8,128)S(1)}, u32[]{:S(2)}, u32[]{:S(2)}) collective-permute-start(f32[256,256]{1,0:T(8,128)S(1)} %add.59.refs_9_), channel_id=1, source_target_pairs={{0,4},{2,6},{4,0},{6,2},{1,5},{3,7},{5,1},{7,3},{8,12},{10,14},{12... | collective-permute-start | bytes 786440 | tf_op jit(solution)/shard_map/ppermute | solution.py:390
  82.3 13.7 %collective-permute-start.23 = (f32[256,256]{1,0:T(8,128)S(1)}, f32[256,256]{1,0:T(8,128)S(1)}, u32[]{:S(2)}, u32[]{:S(2)}) collective-permute-start(f32[256,256]{1,0:T(8,128)S(1)} %add.60.refs_11_), channel_id=1, source_target_pairs={{0,2},{2,0},{4,6},{6,4},{1,3},{3,1},{5,7},{7,5},{8,10},{10,8},{12,... | collective-permute-start | bytes 786440 | tf_op jit(solution)/shard_map/ppermute | solution.py:392
  82.9 13.1 %collective-permute-start.19 = (f32[256,128]{1,0:T(8,128)S(1)}, f32[256,128]{1,0:T(8,128)S(1)}, u32[]{:S(2)}, u32[]{:S(2)}) collective-permute-start(f32[256,128]{1,0:T(8,128)S(1)} %add.58), channel_id=1, source_target_pairs={{8,0},{16,24},{9,1},{17,25},{10,2},{18,26},{11,3},{19,27},{12,4},{... | collective-permute-start | bytes 393224 | tf_op jit(solution)/shard_map/ppermute | solution.py:377
  96.3 30.8 %collective-permute-start.36 = (f32[128,2048]{1,0:T(8,128)S(1)}, f32[128,2048]{1,0:T(8,128)S(1)}, u32[]{:S(2)}, u32[]{:S(2)}) collective-permute-start(f32[128,2048]{1,0:T(8,128)S(1)} %collective-permute-done.16.refs_2_), channel_id=1, source_target_pairs={{8,0},{16,24},{9,1},{17,25},{10,2},{18,26},{11,3},{19,27},{12,4},{... | collective-permute-start | bytes 3145736 | tf_op jit(solution)/shard_map/ppermute | solution.py:377
  97.6 29.5 %collective-permute-start.37 = (f32[128,2048]{1,0:T(8,128)S(1)}, f32[128,2048]{1,0:T(8,128)S(1)}, u32[]{:S(2)}, u32[]{:S(2)}) collective-permute-start(f32[128,2048]{1,0:T(8,128)S(1)} %constant_dynamic-slice_fusion.refs_1_), channel_id=1, source_target_pairs={{8,16},{16,8},{9,17},{17,9},{10,18},{18,10},{11,19},{19,11},{12,20... | collective-permute-start | bytes 3145736 | tf_op jit(solution)/shard_map/ppermute | solution.py:377
  100.5 11.9 %collective-permute-start.32 = (f32[256,256]{1,0:T(8,128)S(1)}, f32[256,256]{1,0:T(8,128)S(1)}, u32[]{:S(2)}, u32[]{:S(2)}) collective-permute-start(f32[256,256]{1,0:T(8,128)S(1)} %get-tuple-element.119), channel_id=1, source_target_pairs={{0,2},{2,0},{4,6},{6,4},{1,3},{3,1},{5,7},{7,5},{8,10},{10,8},{12,... | collective-permute-start | bytes 786440 | tf_op jit(solution)/shard_map/ppermute | solution.py:383
  102.1 11.4 %collective-permute-start.33 = (f32[256,256]{1,0:T(8,128)S(1)}, f32[256,256]{1,0:T(8,128)S(1)}, u32[]{:S(2)}, u32[]{:S(2)}) collective-permute-start(f32[256,256]{1,0:T(8,128)S(1)} %get-tuple-element.120), channel_id=1, source_target_pairs={{0,4},{2,6},{4,0},{6,2},{1,5},{3,7},{5,1},{7,3},{8,12},{10,14},{12... | collective-permute-start | bytes 786440 | tf_op jit(solution)/shard_map/ppermute | solution.py:384
  103.6 8.1 %collective-permute-start.26 = (f32[256,128]{1,0:T(8,128)S(1)}, f32[256,128]{1,0:T(8,128)S(1)}, u32[]{:S(2)}, u32[]{:S(2)}) collective-permute-start(f32[256,128]{1,0:T(8,128)S(1)} %broadcast_select_fusion.3.refs_0_), channel_id=1, source_target_pairs={{2,0},{6,1},{0,2},{4,3},{3,4},{7,5},{1,6},{5,7},{10,8},{11,9},{8,1... | collective-permute-start | bytes 393224 | tf_op jit(solution)/shard_map/ppermute | solution.py:406
  123.5 9.1 %collective-permute-start.35 = (f32[256,128]{1,0:T(8,128)S(1)}, f32[256,128]{1,0:T(8,128)S(1)}, u32[]{:S(2)}, u32[]{:S(2)}) collective-permute-start(f32[256,128]{1,0:T(8,128)S(1)} %add.63), channel_id=1, source_target_pairs={{16,0},{8,24},{17,1},{9,25},{18,2},{10,26},{19,3},{11,27},{20,4},{... | collective-permute-start | bytes 393224 | tf_op jit(solution)/shard_map/ppermute | solution.py:377
  124.8 10.1 %collective-permute-start.46 = (f32[256,256]{1,0:T(8,128)S(1)}, f32[256,256]{1,0:T(8,128)S(1)}, u32[]{:S(2)}, u32[]{:S(2)}) collective-permute-start(f32[256,256]{1,0:T(8,128)S(1)} %add.61.refs_13_), channel_id=1, source_target_pairs={{0,4},{2,6},{4,0},{6,2},{1,5},{3,7},{5,1},{7,3},{8,12},{10,14},{12... | collective-permute-start | bytes 786440 | tf_op jit(solution)/shard_map/ppermute | solution.py:390
  126.3 9.3 %collective-permute-start.47 = (f32[256,256]{1,0:T(8,128)S(1)}, f32[256,256]{1,0:T(8,128)S(1)}, u32[]{:S(2)}, u32[]{:S(2)}) collective-permute-start(f32[256,256]{1,0:T(8,128)S(1)} %add.62.refs_15_), channel_id=1, source_target_pairs={{0,2},{2,0},{4,6},{6,4},{1,3},{3,1},{5,7},{7,5},{8,10},{10,8},{12,... | collective-permute-start | bytes 786440 | tf_op jit(solution)/shard_map/ppermute | solution.py:392
  134.9 11.4 %collective-permute-start.40 = (f32[256,128]{1,0:T(8,128)S(1)}, f32[256,128]{1,0:T(8,128)S(1)}, u32[]{:S(2)}, u32[]{:S(2)}) collective-permute-start(f32[256,128]{1,0:T(8,128)S(1)} %broadcast_select_fusion.2.refs_0_), channel_id=1, source_target_pairs={{3,0},{7,1},{1,2},{5,3},{2,4},{6,5},{0,6},{4,7},{14,8},{15,9},{12,... | collective-permute-start | bytes 393224 | tf_op jit(solution)/shard_map/ppermute | solution.py:406
  134.9 11.4 %collective-permute-start.41 = (f32[256,128]{1,0:T(8,128)S(1)}, f32[256,128]{1,0:T(8,128)S(1)}, u32[]{:S(2)}, u32[]{:S(2)}) collective-permute-start(f32[256,128]{1,0:T(8,128)S(1)} %broadcast_select_fusion.2.refs_0_), channel_id=1, source_target_pairs={{0,0},{4,1},{2,2},{6,3},{1,4},{5,5},{3,6},{7,7},{24,24},{28,25},{2... | collective-permute-start | bytes 393224 | tf_op jit(solution)/shard_map/ppermute | solution.py:406
  135.6 10.7 %collective-permute-start.43 = (f32[256,128]{1,0:T(8,128)S(1)}, f32[256,128]{1,0:T(8,128)S(1)}, u32[]{:S(2)}, u32[]{:S(2)}) collective-permute-start(f32[256,128]{1,0:T(8,128)S(1)} %add.64.refs_5_), channel_id=1, source_target_pairs={{0,2},{2,0},{4,6},{6,4},{1,3},{3,1},{5,7},{7,5},{8,10},{10,8},{12,... | collective-permute-start | bytes 393224 | tf_op jit(solution)/shard_map/ppermute | solution.py:402
  139.1 9.1 %collective-permute-start.44 = (f32[256,128]{1,0:T(8,128)S(1)}, f32[256,128]{1,0:T(8,128)S(1)}, u32[]{:S(2)}, u32[]{:S(2)}) collective-permute-start(f32[256,128]{1,0:T(8,128)S(1)} %add.64.refs_5_), channel_id=1, source_target_pairs={{0,4},{2,6},{4,0},{6,2},{1,5},{3,7},{5,1},{7,3},{8,12},{10,14},{12... | collective-permute-start | bytes 393224 | tf_op jit(solution)/shard_map/ppermute | solution.py:402
  (22 other events, 106.0 us)

commit v3 on v2

--- a/solution.py
+++ b/solution.py
@@ -438,11 +438,11 @@
     pieces_first = mixed(jnp.where(edge, back_in, first))
     s_c = both_halves(jnp.where(edge, last_edge, far_mid))
     part_c = sum_x_y(*gram_part(flags, s_half, s_c))
-    pieces_first, part_c, t_cross = step((pieces_first, part_c, t_cross))
+    part_c, t_cross = step((part_c, t_cross))
     cross = swap_rows(*teacher_parts(flags, t_split, [t_cross]))
     back_cross = send(cross, FAR)
     ks_c = terms_y_x(*part_c)
-    t_edge, t_mid, cross = step((t_edge, t_mid, cross))
+    t_edge, t_mid, cross, pieces_first = step((t_edge, t_mid, cross, pieces_first))
 
     pieces_third = same_plane(swap_rows(*teacher_parts(flags, t_split, [(t_edge, t_mid)])))
     pieces_second = mixed(jnp.where(edge, back_cross, cross))

time: 160 us -> 158 us (0.988)
    ppermute x8, waiting for transfers between devices: 13.2 us -> 5.48 us  [mixed(): lax.ppermute(piece, PLANE, piece_shift(hi, lo))]
    ppermute x4, waiting for transfers between devices: 12.9 us -> 18.5 us  [sum_x_y(): left = left + lax.ppermute(left, 'scol', chip_shift(1))]
    ppermute x4, starting transfers between devices: 2.77 us -> 0.48 us  [swap_rows(): return kept + lax.ppermute(away, 'tcol', CORES)]
    ppermute x11, waiting for transfers between devices: 14.7 us -> 16.5 us  [send(): return lax.ppermute(x, 'tok', perm)]
  transfers between devices with their start and end apart: 52 -> 52, of which waited for: 22 -> 23; matrix products, arithmetic and copies ran while one was open for 2% -> 2% of each run, Pallas kernels for 16% -> 16%
where the time goes in v3:
time: 158 us
  starting transfers between devices  65.1 us (41%)
  waiting for transfers between devices  55 us (35%)
  Pallas kernels  28.8 us (18%)
  local copies, waits for them, and re-layouts  4.94 us (3%)
  other arithmetic  2.75 us (2%)
    ppermute x11, starting transfers between devices, send(): return lax.ppermute(x, 'tok', perm)  21.8 us
    ppermute x4, waiting for transfers between devices, sum_x_y(): left = left + lax.ppermute(left, 'scol', chip_shift(1))  18.5 us
    ppermute x11, waiting for transfers between devices, send(): return lax.ppermute(x, 'tok', perm)  16.5 us
    pallas_call x7, Pallas kernels, call(): pl.pallas_call(kernel, out_shape=outs, in_specs=[FLAGS] + [whole] * len(a...  13 us
    ppermute x6, starting transfers between devices, same_plane(): lax.ppermute(piece, 'scol', chip_shift(s))  8.84 us
    pallas_call x2, Pallas kernels, products_call(): pl.pallas_call(kernel, out_shape=outs, in_specs=[FLAGS] + [whole] * len(a...  8.17 us
    pallas_call x4, Pallas kernels, teacher_parts(): pl.pallas_call(kernel, out_shape=outs, in_specs=[FLAGS] + [whole] * (len(...  7.7 us
    ppermute x8, starting transfers between devices, mixed(): lax.ppermute(piece, PLANE, piece_shift(hi, lo))  7.1 us
  transfers between devices with their start and end apart: 52, of which 23 were waited for; matrix products, arithmetic and copies ran while one was open for 2% of the time, Pallas kernels for 16%

profile of v3, /device:TPU:0, one launch (start us, length us, event | category | flops | bytes accessed | tf_op | source)
XLA Modules:
  0.0 157.8 jit_solution(14185576021299598010)
XLA Ops:
  1.4 3.1 %collective-permute-start = (f32[256,1024]{1,0:T(8,128)S(1)}, f32[256,1024]{1,0:T(8,128)}, u32[]{:S(2)}, u32[]{:S(2)}) collective-permute-start(f32[256,1024]{1,0:T(8,128)S(1)} %constant_dynamic-slice_fusion.1.own_ref), channel_id=1, source_target_pairs={{0,8},{8,0},{16,24},{24,16},{1,9},{9,1},{17,25},{25,17},{2,10},{10... | collective-permute-start | bytes 3145736 | tf_op jit(solution)/shard_map/ppermute | solution.py:377
  4.5 1.7 %collective-permute-start.1 = (f32[256,1024]{1,0:T(8,128)S(1)}, f32[256,1024]{1,0:T(8,128)}, u32[]{:S(2)}, u32[]{:S(2)}) collective-permute-start(f32[256,1024]{1,0:T(8,128)S(1)} %constant_dynamic-slice_fusion.1.own_ref), channel_id=1, source_target_pairs={{8,16},{16,8},{9,17},{17,9},{10,18},{18,10},{11,19},{19,11},{12,20... | collective-permute-start | bytes 3145736 | tf_op jit(solution)/shard_map/ppermute | solution.py:377
  6.3 2.3 %shard_map.37 = (f32[256,256]{1,0:T(8,128)}, f32[256,256]{1,0:T(8,128)S(1)}) custom-call(s32[4]{0:T(128)S(1)} %pad_add_fusion.flags_ref, f32[512,1024]{1,0:T(8,128)S(1)} %copy-done), custom_call_target="tpu_custom_call" | custom-call | tf_op jit(solution)/shard_map/pallas_call | solution.py:114
  11.6 5.1 %collective-permute-done.2 = f32[256,256]{1,0:T(8,128)} collective-permute-done((f32[256,256]{1,0:T(8,128)}, f32[256,256]{1,0:T(8,128)}, u32[]{:S(2)}, u32[]{:S(2)}) %collective-permute-start.2) | collective-permute-done | bytes 262176 | tf_op jit(solution)/shard_map/ppermute | solution.py:383
  23.2 2.2 %copy-done.1 = f32[512,2048]{1,0:T(8,128)S(1)} copy-done((f32[512,2048]{1,0:T(8,128)S(1)}, f32[512,2048]{1,0:T(8,128)}, u32[]{:S(2)}) %copy-start.1) | copy-done | bytes 4194328
  25.3 2.2 %shard_map.38 = (f32[256,128]{1,0:T(8,128)S(1)}, f32[256,128]{1,0:T(8,128)S(1)}, bf16[512,2048]{1,0:T(8,128)(2,1)S(1)}, bf16[512,2048]{1,0:T(8,128)(2,1)S(1)}) custom-call(s32[4]{0:T(128)S(1)} %pad_add_fusion.flags_ref, f32[512,2048]{1,0:T(8,128)S(1)} %copy-done.1, f32[128,2048]{1,0:T(8,128)S(1)} %constant_dynamic-slice_fusion.refs_1_), custom_call_target="tpu_custom_call" | custom-call | tf_op jit(solution)/shard_map/pallas_call | solution.py:197
  31.3 8.3 %collective-permute-start.9 = (f32[128,2048]{1,0:T(8,128)S(1)}, f32[128,2048]{1,0:T(8,128)S(1)}, u32[]{:S(2)}, u32[]{:S(2)}) collective-permute-start(f32[128,2048]{1,0:T(8,128)S(1)} %constant_dynamic-slice_fusion.refs_1_), channel_id=1, source_target_pairs={{0,8},{24,16},{1,9},{25,17},{2,10},{26,18},{3,11},{27,19},{4,12},{... | collective-permute-start | bytes 3145736 | tf_op jit(solution)/shard_map/ppermute | solution.py:377
  41.1 2.3 %shard_map.39 = (f32[256,256]{1,0:T(8,128)S(1)}, f32[256,256]{1,0:T(8,128)S(1)}) custom-call(s32[4]{0:T(128)S(1)} %pad_add_fusion.flags_ref, f32[256,1024]{1,0:T(8,128)S(1)} %constant_dynamic-slice_fusion.1.own_ref, f32[256,1024]{1,0:T(8,128)} %collective-permute-done.first_ref.refs_13_.refs_17_, ...), custom_call_target="tpu_custom_call" | custom-call | tf_op jit(solution)/shard_map/pallas_call | solution.py:114
  46.5 4.9 %collective-permute-done.11 = f32[256,256]{1,0:T(8,128)S(1)} collective-permute-done((f32[256,256]{1,0:T(8,128)S(1)}, f32[256,256]{1,0:T(8,128)S(1)}, u32[]{:S(2)}, u32[]{:S(2)}) %collective-permute-start.11) | collective-permute-done | bytes 262176 | tf_op jit(solution)/shard_map/ppermute | solution.py:383
  52.9 1.9 %collective-permute-start.15 = (f32[256,128]{1,0:T(8,128)S(1)}, f32[256,128]{1,0:T(8,128)S(1)}, u32[]{:S(2)}, u32[]{:S(2)}) collective-permute-start(f32[256,128]{1,0:T(8,128)S(1)} %add.55.refs_0_), channel_id=1, source_target_pairs={{0,6},{2,4},{4,2},{6,0},{1,7},{3,5},{5,3},{7,1},{8,14},{10,12},{12... | collective-permute-start | bytes 393224 | tf_op jit(solution)/shard_map/ppermute | solution.py:402
  54.9 4.2 %collective-permute-done.14.refs_2_ = f32[256,128]{1,0:T(8,128)S(1)} collective-permute-done((f32[256,128]{1,0:T(8,128)S(1)}, f32[256,128]{1,0:T(8,128)S(1)}, u32[]{:S(2)}, u32[]{:S(2)}) %collective-permute-start.14) | collective-permute-done | bytes 131104 | tf_op jit(solution)/shard_map/ppermute | solution.py:402
  59.1 2.2 %collective-permute-done.7 = f32[256,1024]{1,0:T(8,128)S(1)} collective-permute-done((f32[256,1024]{1,0:T(8,128)}, f32[256,1024]{1,0:T(8,128)S(1)}, u32[]{:S(2)}, u32[]{:S(2)}) %collective-permute-start.7) | collective-permute-done | bytes 1048608 | tf_op jit(solution)/shard_map/ppermute | solution.py:377
  70.3 1.8 %shard_map.40 = (f32[256,128]{1,0:T(8,128)S(1)}, f32[256,128]{1,0:T(8,128)S(1)}) custom-call(s32[4]{0:T(128)S(1)} %pad_add_fusion.flags_ref, bf16[512,2048]{1,0:T(8,128)(2,1)S(1)} %get-tuple-element.85.refs_0_, bf16[512,2048]{1,0:T(8,128)(2,1)S(1)} %get-tuple-element.86.refs_1_, f32[128,2048]{1,0:T(8,128)S(1)} %collective-permute-done.9.refs_2_), custom_call_target="tpu_custom_call" | custom-call | tf_op jit(solution)/shard_map/pallas_call | solution.py:197
  72.2 3.0 %collective-permute-done.21 = f32[256,256]{1,0:T(8,128)S(1)} collective-permute-done((f32[256,256]{1,0:T(8,128)S(1)}, f32[256,256]{1,0:T(8,128)S(1)}, u32[]{:S(2)}, u32[]{:S(2)}) %collective-permute-start.21) | collective-permute-done | bytes 262176 | tf_op jit(solution)/shard_map/ppermute | solution.py:383
  80.4 2.0 %collective-permute-done.25.refs_9_.refs_6_ = f32[256,256]{1,0:T(8,128)S(1)} collective-permute-done((f32[256,256]{1,0:T(8,128)S(1)}, f32[256,256]{1,0:T(8,128)S(1)}, u32[]{:S(2)}, u32[]{:S(2)}) %collective-permute-start.25) | collective-permute-done | bytes 262176 | tf_op jit(solution)/shard_map/ppermute | solution.py:390
  84.2 3.9 %shard_map.42 = (f32[512,1024]{1,0:T(8,128)S(1)}, f32[8,128]{1,0:T(8,128)S(1)}) custom-call(s32[4]{0:T(128)S(1)} %pad_add_fusion.flags_ref, f32[256,128]{1,0:T(8,128)S(1)} %add.55.refs_0_, f32[256,128]{1,0:T(8,128)S(1)} %collective-permute-done.13.refs_1_, f32[256,128]{1,0:T(8,128)S(1)} %collective-permute-done.14.refs_2_, ...), custom_call_target="tpu_custom_call" | custom-call | tf_op jit(solution)/shard_map/pallas_call | solution.py:230
  88.1 7.9 %collective-permute-done.20 = f32[256,128]{1,0:T(8,128)S(1)} collective-permute-done((f32[256,128]{1,0:T(8,128)S(1)}, f32[256,128]{1,0:T(8,128)S(1)}, u32[]{:S(2)}, u32[]{:S(2)}) %collective-permute-start.20) | collective-permute-done | bytes 131104 | tf_op jit(solution)/shard_map/ppermute | solution.py:377
  104.2 5.5 %collective-permute-done.28 = f32[256,256]{1,0:T(8,128)S(1)} collective-permute-done((f32[256,256]{1,0:T(8,128)S(1)}, f32[256,256]{1,0:T(8,128)S(1)}, u32[]{:S(2)}, u32[]{:S(2)}) %collective-permute-start.28) | collective-permute-done | bytes 262176 | tf_op jit(solution)/shard_map/ppermute | solution.py:383
  110.6 1.8 %shard_map.44 = (f32[256,128]{1,0:T(8,128)S(1)}, f32[256,128]{1,0:T(8,128)S(1)}) custom-call(s32[4]{0:T(128)S(1)} %pad_add_fusion.flags_ref, bf16[512,2048]{1,0:T(8,128)(2,1)S(1)} %get-tuple-element.85.refs_0_, bf16[512,2048]{1,0:T(8,128)(2,1)S(1)} %get-tuple-element.86.refs_1_, f32[128,2048]{1,0:T(8,128)S(1)} %collective-permute-done.17.refs_2_), custom_call_target="tpu_custom_call" | custom-call | tf_op jit(solution)/shard_map/pallas_call | solution.py:197
  112.5 2.5 %collective-permute-start.35 = (f32[256,128]{1,0:T(8,128)S(1)}, f32[256,128]{1,0:T(8,128)S(1)}, u32[]{:S(2)}, u32[]{:S(2)}) collective-permute-start(f32[256,128]{1,0:T(8,128)S(1)} %broadcast_select_fusion.3.refs_0_), channel_id=1, source_target_pairs={{1,0},{5,1},{3,2},{7,3},{0,4},{4,5},{2,6},{6,7},{12,8},{13,9},{14,... | collective-permute-start | bytes 393224 | tf_op jit(solution)/shard_map/ppermute | solution.py:406
  115.9 1.7 %collective-permute-done.35.refs_2_ = f32[256,128]{1,0:T(8,128)S(1)} collective-permute-done((f32[256,128]{1,0:T(8,128)S(1)}, f32[256,128]{1,0:T(8,128)S(1)}, u32[]{:S(2)}, u32[]{:S(2)}) %collective-permute-start.35) | collective-permute-done | bytes 131104 | tf_op jit(solution)/shard_map/ppermute | solution.py:406
  118.9 1.6 %collective-permute-done.36.refs_3_ = f32[256,128]{1,0:T(8,128)S(1)} collective-permute-done((f32[256,128]{1,0:T(8,128)S(1)}, f32[256,128]{1,0:T(8,128)S(1)}, u32[]{:S(2)}, u32[]{:S(2)}) %collective-permute-start.36) | collective-permute-done | bytes 131104 | tf_op jit(solution)/shard_map/ppermute | solution.py:406
  120.5 1.9 %collective-permute-start.46 = (f32[256,256]{1,0:T(8,128)S(1)}, f32[256,256]{1,0:T(8,128)S(1)}, u32[]{:S(2)}, u32[]{:S(2)}) collective-permute-start(f32[256,256]{1,0:T(8,128)S(1)} %add.61.refs_13_), channel_id=1, source_target_pairs={{0,4},{2,6},{4,0},{6,2},{1,5},{3,7},{5,1},{7,3},{8,12},{10,14},{12... | collective-permute-start | bytes 786440 | tf_op jit(solution)/shard_map/ppermute | solution.py:390
  123.8 1.8 %shard_map.45 = (f32[256,128]{1,0:T(8,128)S(1)}, f32[256,128]{1,0:T(8,128)S(1)}) custom-call(s32[4]{0:T(128)S(1)} %pad_add_fusion.flags_ref, bf16[512,2048]{1,0:T(8,128)(2,1)S(1)} %get-tuple-element.85.refs_0_, bf16[512,2048]{1,0:T(8,128)(2,1)S(1)} %get-tuple-element.86.refs_1_, f32[128,2048]{1,0:T(8,128)S(1)} %collective-permute-done.32.refs_2_, ...), custom_call_target="tpu_custom_call" | custom-call | tf_op jit(solution)/shard_map/pallas_call | solution.py:197
  125.9 4.2 %collective-permute-done.31 = f32[256,128]{1,0:T(8,128)S(1)} collective-permute-done((f32[256,128]{1,0:T(8,128)S(1)}, f32[256,128]{1,0:T(8,128)S(1)}, u32[]{:S(2)}, u32[]{:S(2)}) %collective-permute-start.31) | collective-permute-done | bytes 131104 | tf_op jit(solution)/shard_map/ppermute | solution.py:377
  134.1 2.1 %collective-permute-done.38.refs_1_ = f32[256,128]{1,0:T(8,128)S(1)} collective-permute-done((f32[256,128]{1,0:T(8,128)S(1)}, f32[256,128]{1,0:T(8,128)S(1)}, u32[]{:S(2)}, u32[]{:S(2)}) %collective-permute-start.38) | collective-permute-done | bytes 131104 | tf_op jit(solution)/shard_map/ppermute | solution.py:406
  136.3 2.1 %collective-permute-start.44 = (f32[256,128]{1,0:T(8,128)S(1)}, f32[256,128]{1,0:T(8,128)S(1)}, u32[]{:S(2)}, u32[]{:S(2)}) collective-permute-start(f32[256,128]{1,0:T(8,128)S(1)} %add.64.refs_5_), channel_id=1, source_target_pairs={{0,4},{2,6},{4,0},{6,2},{1,5},{3,7},{5,1},{7,3},{8,12},{10,14},{12... | collective-permute-start | bytes 393224 | tf_op jit(solution)/shard_map/ppermute | solution.py:402
  139.4 4.3 %shard_map.46 = (f32[512,1024]{1,0:T(8,128)S(1)}, f32[8,128]{1,0:T(8,128)S(1)}) custom-call(s32[4]{0:T(128)S(1)} %pad_add_fusion.flags_ref, f32[256,128]{1,0:T(8,128)S(1)} %broadcast_select_fusion.3.refs_0_, f32[256,128]{1,0:T(8,128)S(1)} %collective-permute-done.34.refs_1_, f32[256,128]{1,0:T(8,128)S(1)} %collective-permute-done.35.refs_2_, ...), custom_call_target="tpu_custom_call" | custom-call | tf_op jit(solution)/shard_map/pallas_call | solution.py:230
  147.3 2.9 %collective-permute-start.49 = (f32[8,128]{1,0:T(8,128)S(1)}, f32[8,128]{1,0:T(8,128)S(1)}, u32[]{:S(2)}, u32[]{:S(2)}) collective-permute-start(f32[8,128]{1,0:T(8,128)S(1)} %add.65.refs_0_), channel_id=1, source_target_pairs={{0,8},{8,16},{16,24},{24,0},{1,9},{9,17},{17,25},{25,1},{2,10},{10... | collective-permute-start | bytes 12296 | tf_op jit(solution)/shard_map/ppermute | solution.py:453
  150.5 2.4 %collective-permute-start.51 = (f32[8,128]{1,0:T(8,128)S(1)}, f32[8,128]{1,0:T(8,128)S(1)}, u32[]{:S(2)}, u32[]{:S(2)}) collective-permute-start(f32[8,128]{1,0:T(8,128)S(1)} %add.65.refs_0_), channel_id=1, source_target_pairs={{0,24},{8,0},{16,8},{24,16},{1,25},{9,1},{17,9},{25,17},{2,26},{10... | collective-permute-start | bytes 12296 | tf_op jit(solution)/shard_map/ppermute | solution.py:453
  153.5 2.4 %shard_map.48.up_ref = f32[256,1024]{1,0:T(8,128)S(1)} custom-call(s32[4]{0:T(128)S(1)} %pad_add_fusion.flags_ref, f32[256,256]{1,0:T(8,128)S(1)} %get-tuple-element.147.refs_0_, f32[256,256]{1,0:T(8,128)S(1)} %get-tuple-element.148.refs_1_, f32[256,256]{1,0:T(8,128)S(1)} %get-tuple-element.149.refs_2_, f32[256,256]{1,0:T(8,128)S(1)} %get-tuple-element.150.refs_3_, ...), custom_call_target="tpu_custom_call" | custom-call | tf_op jit(solution)/shard_map/pallas_call | solution.py:114
  156.0 1.8 %shard_map.49 = f32[256,1024]{1,0:T(8,128)} custom-call(s32[4]{0:T(128)S(1)} %pad_add_fusion.flags_ref, f32[256,1024]{1,0:T(8,128)S(1)} %shard_map.48.up_ref, f32[512,1024]{1,0:T(8,128)S(1)} %get-tuple-element.151.refs_8_.prod_ref, f32[1,1]{1,0:T(1,128)} %bitcast.5.norm_ref, f32[8,128]{1,0:T(8,128)S(1)} %add.65.refs_0_, ...), custom_call_target="tpu_custom_call" | custom-call | tf_op jit(solution)/shard_map/pallas_call | solution.py:114
  (109 shorter events, 58.8 us)
Async XLA Ops:
  1.4 27.6 %collective-permute-start = (f32[256,1024]{1,0:T(8,128)S(1)}, f32[256,1024]{1,0:T(8,128)}, u32[]{:S(2)}, u32[]{:S(2)}) collective-permute-start(f32[256,1024]{1,0:T(8,128)S(1)} %constant_dynamic-slice_fusion.1.own_ref), channel_id=1, source_target_pairs={{0,8},{8,0},{16,24},{24,16},{1,9},{9,1},{17,25},{25,17},{2,10},{10... | collective-permute-start | bytes 3145736 | tf_op jit(solution)/shard_map/ppermute | solution.py:377
  4.5 24.5 %collective-permute-start.1 = (f32[256,1024]{1,0:T(8,128)S(1)}, f32[256,1024]{1,0:T(8,128)}, u32[]{:S(2)}, u32[]{:S(2)}) collective-permute-start(f32[256,1024]{1,0:T(8,128)S(1)} %constant_dynamic-slice_fusion.1.own_ref), channel_id=1, source_target_pairs={{8,16},{16,8},{9,17},{17,9},{10,18},{18,10},{11,19},{19,11},{12,20... | collective-permute-start | bytes 3145736 | tf_op jit(solution)/shard_map/ppermute | solution.py:377
  8.6 8.1 %collective-permute-start.2 = (f32[256,256]{1,0:T(8,128)}, f32[256,256]{1,0:T(8,128)}, u32[]{:S(2)}, u32[]{:S(2)}) collective-permute-start(f32[256,256]{1,0:T(8,128)} %get-tuple-element.79), channel_id=1, source_target_pairs={{0,2},{2,0},{4,6},{6,4},{1,3},{3,1},{5,7},{7,5},{8,10},{10,8},{12,... | collective-permute-start | bytes 786440 | tf_op jit(solution)/shard_map/ppermute | solution.py:383
  10.0 9.2 %collective-permute-start.4 = (f32[256,256]{1,0:T(8,128)S(1)}, f32[256,256]{1,0:T(8,128)}, u32[]{:S(2)}, u32[]{:S(2)}) collective-permute-start(f32[256,256]{1,0:T(8,128)S(1)} %get-tuple-element.80), channel_id=1, source_target_pairs={{0,4},{2,6},{4,0},{6,2},{1,5},{3,7},{5,1},{7,3},{8,12},{10,14},{12... | collective-permute-start | bytes 786440 | tf_op jit(solution)/shard_map/ppermute | solution.py:384
  17.7 11.3 %collective-permute-start.3 = (f32[256,256]{1,0:T(8,128)S(1)}, f32[256,256]{1,0:T(8,128)S(1)}, u32[]{:S(2)}, u32[]{:S(2)}) collective-permute-start(f32[256,256]{1,0:T(8,128)S(1)} %add.53.refs_4_), channel_id=1, source_target_pairs={{0,4},{2,6},{4,0},{6,2},{1,5},{3,7},{5,1},{7,3},{8,12},{10,14},{12... | collective-permute-start | bytes 786440 | tf_op jit(solution)/shard_map/ppermute | solution.py:390
  20.3 8.8 %collective-permute-start.5 = (f32[256,256]{1,0:T(8,128)S(1)}, f32[256,256]{1,0:T(8,128)S(1)}, u32[]{:S(2)}, u32[]{:S(2)}) collective-permute-start(f32[256,256]{1,0:T(8,128)S(1)} %add.54.refs_6_), channel_id=1, source_target_pairs={{0,2},{2,0},{4,6},{6,4},{1,3},{3,1},{5,7},{7,5},{8,10},{10,8},{12,... | collective-permute-start | bytes 786440 | tf_op jit(solution)/shard_map/ppermute | solution.py:392
  29.0 12.1 %collective-permute-start.10 = (f32[256,1024]{1,0:T(8,128)}, f32[256,1024]{1,0:T(8,128)S(1)}, u32[]{:S(2)}, u32[]{:S(2)}) collective-permute-start(f32[256,1024]{1,0:T(8,128)} %collective-permute-done.first_ref.refs_13_.refs_17_), channel_id=1, source_target_pairs={{0,1},{1,0},{2,3},{3,2},{4,5},{5,4},{6,7},{7,6},{8,9},{9,8},{10,11... | collective-permute-start | bytes 3145736 | tf_op jit(solution)/shard_map/ppermute | solution.py:380
  29.3 32.0 %collective-permute-start.8 = (f32[256,1024]{1,0:T(8,128)}, f32[256,1024]{1,0:T(8,128)S(1)}, u32[]{:S(2)}, u32[]{:S(2)}) collective-permute-start(f32[256,1024]{1,0:T(8,128)} %collective-permute-done.first_ref.refs_13_.refs_17_), channel_id=1, source_target_pairs={{8,16},{16,8},{9,17},{17,9},{10,18},{18,10},{11,19},{19,11},{12,20... | collective-permute-start | bytes 3145736 | tf_op jit(solution)/shard_map/ppermute | solution.py:377
  30.0 31.3 %collective-permute-start.7 = (f32[256,1024]{1,0:T(8,128)}, f32[256,1024]{1,0:T(8,128)S(1)}, u32[]{:S(2)}, u32[]{:S(2)}) collective-permute-start(f32[256,1024]{1,0:T(8,128)} %collective-permute-done.1), channel_id=1, source_target_pairs={{8,0},{16,24},{9,1},{17,25},{10,2},{18,26},{11,3},{19,27},{12,4},{... | collective-permute-start | bytes 3145736 | tf_op jit(solution)/shard_map/ppermute | solution.py:377
  31.3 31.0 %collective-permute-start.9 = (f32[128,2048]{1,0:T(8,128)S(1)}, f32[128,2048]{1,0:T(8,128)S(1)}, u32[]{:S(2)}, u32[]{:S(2)}) collective-permute-start(f32[128,2048]{1,0:T(8,128)S(1)} %constant_dynamic-slice_fusion.refs_1_), channel_id=1, source_target_pairs={{0,8},{24,16},{1,9},{25,17},{2,10},{26,18},{3,11},{27,19},{4,12},{... | collective-permute-start | bytes 3145736 | tf_op jit(solution)/shard_map/ppermute | solution.py:377
  43.4 7.9 %collective-permute-start.11 = (f32[256,256]{1,0:T(8,128)S(1)}, f32[256,256]{1,0:T(8,128)S(1)}, u32[]{:S(2)}, u32[]{:S(2)}) collective-permute-start(f32[256,256]{1,0:T(8,128)S(1)} %get-tuple-element.90), channel_id=1, source_target_pairs={{0,2},{2,0},{4,6},{6,4},{1,3},{3,1},{5,7},{7,5},{8,10},{10,8},{12,... | collective-permute-start | bytes 786440 | tf_op jit(solution)/shard_map/ppermute | solution.py:383
  62.5 33.5 %collective-permute-start.17 = (f32[128,2048]{1,0:T(8,128)S(1)}, f32[128,2048]{1,0:T(8,128)S(1)}, u32[]{:S(2)}, u32[]{:S(2)}) collective-permute-start(f32[128,2048]{1,0:T(8,128)S(1)} %collective-permute-done.9.refs_2_), channel_id=1, source_target_pairs={{8,16},{16,8},{9,17},{17,9},{10,18},{18,10},{11,19},{19,11},{12,20... | collective-permute-start | bytes 3145736 | tf_op jit(solution)/shard_map/ppermute | solution.py:377
  63.2 32.8 %collective-permute-start.16 = (f32[256,1024]{1,0:T(8,128)S(1)}, f32[256,1024]{1,0:T(8,128)S(1)}, u32[]{:S(2)}, u32[]{:S(2)}) collective-permute-start(f32[256,1024]{1,0:T(8,128)S(1)} %collective-permute-done.8), channel_id=1, source_target_pairs={{8,0},{16,24},{9,1},{17,25},{10,2},{18,26},{11,3},{19,27},{12,4},{... | collective-permute-start | bytes 3145736 | tf_op jit(solution)/shard_map/ppermute | solution.py:377
  66.8 8.4 %collective-permute-start.21 = (f32[256,256]{1,0:T(8,128)S(1)}, f32[256,256]{1,0:T(8,128)S(1)}, u32[]{:S(2)}, u32[]{:S(2)}) collective-permute-start(f32[256,256]{1,0:T(8,128)S(1)} %get-tuple-element.100), channel_id=1, source_target_pairs={{0,2},{2,0},{4,6},{6,4},{1,3},{3,1},{5,7},{7,5},{8,10},{10,8},{12,... | collective-permute-start | bytes 786440 | tf_op jit(solution)/shard_map/ppermute | solution.py:383
  68.3 9.2 %collective-permute-start.23 = (f32[256,256]{1,0:T(8,128)S(1)}, f32[256,256]{1,0:T(8,128)S(1)}, u32[]{:S(2)}, u32[]{:S(2)}) collective-permute-start(f32[256,256]{1,0:T(8,128)S(1)} %get-tuple-element.101), channel_id=1, source_target_pairs={{0,4},{2,6},{4,0},{6,2},{1,5},{3,7},{5,1},{7,3},{8,12},{10,14},{12... | collective-permute-start | bytes 786440 | tf_op jit(solution)/shard_map/ppermute | solution.py:384
  69.8 12.5 %collective-permute-start.25 = (f32[256,256]{1,0:T(8,128)S(1)}, f32[256,256]{1,0:T(8,128)S(1)}, u32[]{:S(2)}, u32[]{:S(2)}) collective-permute-start(f32[256,256]{1,0:T(8,128)S(1)} %add.56.refs_8_.refs_5_), channel_id=1, source_target_pairs={{0,4},{2,6},{4,0},{6,2},{1,5},{3,7},{5,1},{7,3},{8,12},{10,14},{12... | collective-permute-start | bytes 786440 | tf_op jit(solution)/shard_map/ppermute | solution.py:390
  78.9 17.2 %collective-permute-start.22 = (f32[256,256]{1,0:T(8,128)S(1)}, f32[256,256]{1,0:T(8,128)S(1)}, u32[]{:S(2)}, u32[]{:S(2)}) collective-permute-start(f32[256,256]{1,0:T(8,128)S(1)} %add.59.refs_9_), channel_id=1, source_target_pairs={{0,4},{2,6},{4,0},{6,2},{1,5},{3,7},{5,1},{7,3},{8,12},{10,14},{12... | collective-permute-start | bytes 786440 | tf_op jit(solution)/shard_map/ppermute | solution.py:390
  82.3 13.7 %collective-permute-start.24 = (f32[256,256]{1,0:T(8,128)S(1)}, f32[256,256]{1,0:T(8,128)S(1)}, u32[]{:S(2)}, u32[]{:S(2)}) collective-permute-start(f32[256,256]{1,0:T(8,128)S(1)} %add.60.refs_11_), channel_id=1, source_target_pairs={{0,2},{2,0},{4,6},{6,4},{1,3},{3,1},{5,7},{7,5},{8,10},{10,8},{12,... | collective-permute-start | bytes 786440 | tf_op jit(solution)/shard_map/ppermute | solution.py:392
  82.9 13.1 %collective-permute-start.20 = (f32[256,128]{1,0:T(8,128)S(1)}, f32[256,128]{1,0:T(8,128)S(1)}, u32[]{:S(2)}, u32[]{:S(2)}) collective-permute-start(f32[256,128]{1,0:T(8,128)S(1)} %add.58), channel_id=1, source_target_pairs={{8,0},{16,24},{9,1},{17,25},{10,2},{18,26},{11,3},{19,27},{12,4},{... | collective-permute-start | bytes 393224 | tf_op jit(solution)/shard_map/ppermute | solution.py:377
  96.3 27.4 %collective-permute-start.32 = (f32[128,2048]{1,0:T(8,128)S(1)}, f32[128,2048]{1,0:T(8,128)S(1)}, u32[]{:S(2)}, u32[]{:S(2)}) collective-permute-start(f32[128,2048]{1,0:T(8,128)S(1)} %collective-permute-done.17.refs_2_), channel_id=1, source_target_pairs={{8,0},{16,24},{9,1},{17,25},{10,2},{18,26},{11,3},{19,27},{12,4},{... | collective-permute-start | bytes 3145736 | tf_op jit(solution)/shard_map/ppermute | solution.py:377
  97.6 26.1 %collective-permute-start.33 = (f32[128,2048]{1,0:T(8,128)S(1)}, f32[128,2048]{1,0:T(8,128)S(1)}, u32[]{:S(2)}, u32[]{:S(2)}) collective-permute-start(f32[128,2048]{1,0:T(8,128)S(1)} %constant_dynamic-slice_fusion.refs_1_), channel_id=1, source_target_pairs={{8,16},{16,8},{9,17},{17,9},{10,18},{18,10},{11,19},{19,11},{12,20... | collective-permute-start | bytes 3145736 | tf_op jit(solution)/shard_map/ppermute | solution.py:377
  100.5 9.2 %collective-permute-start.28 = (f32[256,256]{1,0:T(8,128)S(1)}, f32[256,256]{1,0:T(8,128)S(1)}, u32[]{:S(2)}, u32[]{:S(2)}) collective-permute-start(f32[256,256]{1,0:T(8,128)S(1)} %get-tuple-element.117), channel_id=1, source_target_pairs={{0,2},{2,0},{4,6},{6,4},{1,3},{3,1},{5,7},{7,5},{8,10},{10,8},{12,... | collective-permute-start | bytes 786440 | tf_op jit(solution)/shard_map/ppermute | solution.py:383
  102.1 8.5 %collective-permute-start.29 = (f32[256,256]{1,0:T(8,128)S(1)}, f32[256,256]{1,0:T(8,128)S(1)}, u32[]{:S(2)}, u32[]{:S(2)}) collective-permute-start(f32[256,256]{1,0:T(8,128)S(1)} %get-tuple-element.118), channel_id=1, source_target_pairs={{0,4},{2,6},{4,0},{6,2},{1,5},{3,7},{5,1},{7,3},{8,12},{10,14},{12... | collective-permute-start | bytes 786440 | tf_op jit(solution)/shard_map/ppermute | solution.py:384
  103.6 11.5 %collective-permute-start.34 = (f32[256,128]{1,0:T(8,128)S(1)}, f32[256,128]{1,0:T(8,128)S(1)}, u32[]{:S(2)}, u32[]{:S(2)}) collective-permute-start(f32[256,128]{1,0:T(8,128)S(1)} %broadcast_select_fusion.3.refs_0_), channel_id=1, source_target_pairs={{2,0},{6,1},{0,2},{4,3},{3,4},{7,5},{1,6},{5,7},{10,8},{11,9},{8,1... | collective-permute-start | bytes 393224 | tf_op jit(solution)/shard_map/ppermute | solution.py:406
  117.6 12.5 %collective-permute-start.31 = (f32[256,128]{1,0:T(8,128)S(1)}, f32[256,128]{1,0:T(8,128)S(1)}, u32[]{:S(2)}, u32[]{:S(2)}) collective-permute-start(f32[256,128]{1,0:T(8,128)S(1)} %add.63), channel_id=1, source_target_pairs={{16,0},{8,24},{17,1},{9,25},{18,2},{10,26},{19,3},{11,27},{20,4},{... | collective-permute-start | bytes 393224 | tf_op jit(solution)/shard_map/ppermute | solution.py:377
  120.5 12.2 %collective-permute-start.46 = (f32[256,256]{1,0:T(8,128)S(1)}, f32[256,256]{1,0:T(8,128)S(1)}, u32[]{:S(2)}, u32[]{:S(2)}) collective-permute-start(f32[256,256]{1,0:T(8,128)S(1)} %add.61.refs_13_), channel_id=1, source_target_pairs={{0,4},{2,6},{4,0},{6,2},{1,5},{3,7},{5,1},{7,3},{8,12},{10,14},{12... | collective-permute-start | bytes 786440 | tf_op jit(solution)/shard_map/ppermute | solution.py:390
  122.4 11.0 %collective-permute-start.47 = (f32[256,256]{1,0:T(8,128)S(1)}, f32[256,256]{1,0:T(8,128)S(1)}, u32[]{:S(2)}, u32[]{:S(2)}) collective-permute-start(f32[256,256]{1,0:T(8,128)S(1)} %add.62.refs_15_), channel_id=1, source_target_pairs={{0,2},{2,0},{4,6},{6,4},{1,3},{3,1},{5,7},{7,5},{8,10},{10,8},{12,... | collective-permute-start | bytes 786440 | tf_op jit(solution)/shard_map/ppermute | solution.py:392
  131.8 11.9 %collective-permute-start.40 = (f32[256,128]{1,0:T(8,128)S(1)}, f32[256,128]{1,0:T(8,128)S(1)}, u32[]{:S(2)}, u32[]{:S(2)}) collective-permute-start(f32[256,128]{1,0:T(8,128)S(1)} %broadcast_select_fusion.2.refs_0_), channel_id=1, source_target_pairs={{3,0},{7,1},{1,2},{5,3},{2,4},{6,5},{0,6},{4,7},{14,8},{15,9},{12,... | collective-permute-start | bytes 393224 | tf_op jit(solution)/shard_map/ppermute | solution.py:406
  132.7 11.0 %collective-permute-start.41 = (f32[256,128]{1,0:T(8,128)S(1)}, f32[256,128]{1,0:T(8,128)S(1)}, u32[]{:S(2)}, u32[]{:S(2)}) collective-permute-start(f32[256,128]{1,0:T(8,128)S(1)} %broadcast_select_fusion.2.refs_0_), channel_id=1, source_target_pairs={{0,0},{4,1},{2,2},{6,3},{1,4},{5,5},{3,6},{7,7},{24,24},{28,25},{2... | collective-permute-start | bytes 393224 | tf_op jit(solution)/shard_map/ppermute | solution.py:406
  133.4 10.3 %collective-permute-start.43 = (f32[256,128]{1,0:T(8,128)S(1)}, f32[256,128]{1,0:T(8,128)S(1)}, u32[]{:S(2)}, u32[]{:S(2)}) collective-permute-start(f32[256,128]{1,0:T(8,128)S(1)} %add.64.refs_5_), channel_id=1, source_target_pairs={{0,2},{2,0},{4,6},{6,4},{1,3},{3,1},{5,7},{7,5},{8,10},{10,8},{12,... | collective-permute-start | bytes 393224 | tf_op jit(solution)/shard_map/ppermute | solution.py:402
  136.3 8.7 %collective-permute-start.44 = (f32[256,128]{1,0:T(8,128)S(1)}, f32[256,128]{1,0:T(8,128)S(1)}, u32[]{:S(2)}, u32[]{:S(2)}) collective-permute-start(f32[256,128]{1,0:T(8,128)S(1)} %add.64.refs_5_), channel_id=1, source_target_pairs={{0,4},{2,6},{4,0},{6,2},{1,5},{3,7},{5,1},{7,3},{8,12},{10,14},{12... | collective-permute-start | bytes 393224 | tf_op jit(solution)/shard_map/ppermute | solution.py:402
  147.3 8.6 %collective-permute-start.49 = (f32[8,128]{1,0:T(8,128)S(1)}, f32[8,128]{1,0:T(8,128)S(1)}, u32[]{:S(2)}, u32[]{:S(2)}) collective-permute-start(f32[8,128]{1,0:T(8,128)S(1)} %add.65.refs_0_), channel_id=1, source_target_pairs={{0,8},{8,16},{16,24},{24,0},{1,9},{9,17},{17,25},{25,1},{2,10},{10... | collective-permute-start | bytes 12296 | tf_op jit(solution)/shard_map/ppermute | solution.py:453
  (22 other events, 110.2 us)

commit v4 on v3

--- a/solution.py
+++ b/solution.py
@@ -442,7 +442,7 @@
     cross = swap_rows(*teacher_parts(flags, t_split, [t_cross]))
     back_cross = send(cross, FAR)
     ks_c = terms_y_x(*part_c)
-    t_edge, t_mid, cross, pieces_first = step((t_edge, t_mid, cross, pieces_first))
+    t_edge, t_mid, cross = step((t_edge, t_mid, cross))
 
     pieces_third = same_plane(swap_rows(*teacher_parts(flags, t_split, [(t_edge, t_mid)])))
     pieces_second = mixed(jnp.where(edge, back_cross, cross))

time: 158 us -> 164 us (1.038)
  waiting for transfers between devices: 55 us -> 60.3 us
    ppermute x8, waiting for transfers between devices: 5.48 us -> 1.94 us  [mixed(): lax.ppermute(piece, PLANE, piece_shift(hi, lo))]
    ppermute x4, waiting for transfers between devices: 1.96 us -> 5.06 us  [terms_y_x(): lax.ppermute(left, 'scol', chip_shift(2))]
    ppermute x11, waiting for transfers between devices: 16.5 us -> 19.3 us  [send(): return lax.ppermute(x, 'tok', perm)]
    ppermute x8, starting transfers between devices: 7.1 us -> 9.1 us  [mixed(): lax.ppermute(piece, PLANE, piece_shift(hi, lo))]
    ppermute x4, waiting for transfers between devices: 0.01 us -> 1.68 us  [terms_y_x(): lax.ppermute(right, 'scol', chip_shift(1))]
  transfers between devices with their start and end apart: 52 -> 52, of which waited for: 23 -> 22; matrix products, arithmetic and copies ran while one was open for 2% -> 2% of each run, Pallas kernels for 16% -> 16%
where the time goes in v4:
time: 164 us; the launch traced here: 163 us
  starting transfers between devices  65 us (40%)
  waiting for transfers between devices  60.3 us (37%)
  Pallas kernels  28.8 us (18%)
  local copies, waits for them, and re-layouts  4.94 us (3%)
  other arithmetic  2.75 us (2%)
    ppermute x11, starting transfers between devices, send(): return lax.ppermute(x, 'tok', perm)  21.8 us
    ppermute x11, waiting for transfers between devices, send(): return lax.ppermute(x, 'tok', perm)  19.3 us
    ppermute x4, waiting for transfers between devices, sum_x_y(): left = left + lax.ppermute(left, 'scol', chip_shift(1))  18.3 us
    pallas_call x7, Pallas kernels, call(): pl.pallas_call(kernel, out_shape=outs, in_specs=[FLAGS] + [whole] * len(a...  13 us
    ppermute x8, starting transfers between devices, mixed(): lax.ppermute(piece, PLANE, piece_shift(hi, lo))  9.1 us
    pallas_call x2, Pallas kernels, products_call(): pl.pallas_call(kernel, out_shape=outs, in_specs=[FLAGS] + [whole] * len(a...  8.17 us
    pallas_call x4, Pallas kernels, teacher_parts(): pl.pallas_call(kernel, out_shape=outs, in_specs=[FLAGS] + [whole] * (len(...  7.7 us
    ppermute x6, starting transfers between devices, same_plane(): lax.ppermute(piece, 'scol', chip_shift(s))  7.67 us
  transfers between devices with their start and end apart: 52, of which 22 were waited for; matrix products, arithmetic and copies ran while one was open for 2% of the time, Pallas kernels for 16%

profile of v4, /device:TPU:0, one launch (start us, length us, event | category | flops | bytes accessed | tf_op | source)
XLA Modules:
  0.0 163.0 jit_solution(10924584574723898923)
XLA Ops:
  1.4 3.1 %collective-permute-start = (f32[256,1024]{1,0:T(8,128)S(1)}, f32[256,1024]{1,0:T(8,128)}, u32[]{:S(2)}, u32[]{:S(2)}) collective-permute-start(f32[256,1024]{1,0:T(8,128)S(1)} %constant_dynamic-slice_fusion.1.own_ref), channel_id=1, source_target_pairs={{0,8},{8,0},{16,24},{24,16},{1,9},{9,1},{17,25},{25,17},{2,10},{10... | collective-permute-start | bytes 3145736 | tf_op jit(solution)/shard_map/ppermute | solution.py:377
  4.5 1.7 %collective-permute-start.1 = (f32[256,1024]{1,0:T(8,128)S(1)}, f32[256,1024]{1,0:T(8,128)}, u32[]{:S(2)}, u32[]{:S(2)}) collective-permute-start(f32[256,1024]{1,0:T(8,128)S(1)} %constant_dynamic-slice_fusion.1.own_ref), channel_id=1, source_target_pairs={{8,16},{16,8},{9,17},{17,9},{10,18},{18,10},{11,19},{19,11},{12,20... | collective-permute-start | bytes 3145736 | tf_op jit(solution)/shard_map/ppermute | solution.py:377
  6.3 2.3 %shard_map.37 = (f32[256,256]{1,0:T(8,128)}, f32[256,256]{1,0:T(8,128)S(1)}) custom-call(s32[4]{0:T(128)S(1)} %pad_add_fusion.flags_ref, f32[512,1024]{1,0:T(8,128)S(1)} %copy-done), custom_call_target="tpu_custom_call" | custom-call | tf_op jit(solution)/shard_map/pallas_call | solution.py:114
  11.6 5.1 %collective-permute-done.2 = f32[256,256]{1,0:T(8,128)} collective-permute-done((f32[256,256]{1,0:T(8,128)}, f32[256,256]{1,0:T(8,128)}, u32[]{:S(2)}, u32[]{:S(2)}) %collective-permute-start.2) | collective-permute-done | bytes 262176 | tf_op jit(solution)/shard_map/ppermute | solution.py:383
  23.2 2.2 %copy-done.1 = f32[512,2048]{1,0:T(8,128)S(1)} copy-done((f32[512,2048]{1,0:T(8,128)S(1)}, f32[512,2048]{1,0:T(8,128)}, u32[]{:S(2)}) %copy-start.1) | copy-done | bytes 4194328
  25.3 2.2 %shard_map.38 = (f32[256,128]{1,0:T(8,128)S(1)}, f32[256,128]{1,0:T(8,128)S(1)}, bf16[512,2048]{1,0:T(8,128)(2,1)S(1)}, bf16[512,2048]{1,0:T(8,128)(2,1)S(1)}) custom-call(s32[4]{0:T(128)S(1)} %pad_add_fusion.flags_ref, f32[512,2048]{1,0:T(8,128)S(1)} %copy-done.1, f32[128,2048]{1,0:T(8,128)S(1)} %constant_dynamic-slice_fusion.refs_1_), custom_call_target="tpu_custom_call" | custom-call | tf_op jit(solution)/shard_map/pallas_call | solution.py:197
  31.3 8.3 %collective-permute-start.9 = (f32[128,2048]{1,0:T(8,128)S(1)}, f32[128,2048]{1,0:T(8,128)S(1)}, u32[]{:S(2)}, u32[]{:S(2)}) collective-permute-start(f32[128,2048]{1,0:T(8,128)S(1)} %constant_dynamic-slice_fusion.refs_1_), channel_id=1, source_target_pairs={{0,8},{24,16},{1,9},{25,17},{2,10},{26,18},{3,11},{27,19},{4,12},{... | collective-permute-start | bytes 3145736 | tf_op jit(solution)/shard_map/ppermute | solution.py:377
  41.1 2.3 %shard_map.39 = (f32[256,256]{1,0:T(8,128)S(1)}, f32[256,256]{1,0:T(8,128)S(1)}) custom-call(s32[4]{0:T(128)S(1)} %pad_add_fusion.flags_ref, f32[256,1024]{1,0:T(8,128)S(1)} %constant_dynamic-slice_fusion.1.own_ref, f32[256,1024]{1,0:T(8,128)} %collective-permute-done.first_ref.refs_13_.refs_17_, ...), custom_call_target="tpu_custom_call" | custom-call | tf_op jit(solution)/shard_map/pallas_call | solution.py:114
  46.5 4.9 %collective-permute-done.11 = f32[256,256]{1,0:T(8,128)S(1)} collective-permute-done((f32[256,256]{1,0:T(8,128)S(1)}, f32[256,256]{1,0:T(8,128)S(1)}, u32[]{:S(2)}, u32[]{:S(2)}) %collective-permute-start.11) | collective-permute-done | bytes 262176 | tf_op jit(solution)/shard_map/ppermute | solution.py:383
  52.9 1.9 %collective-permute-start.15 = (f32[256,128]{1,0:T(8,128)S(1)}, f32[256,128]{1,0:T(8,128)S(1)}, u32[]{:S(2)}, u32[]{:S(2)}) collective-permute-start(f32[256,128]{1,0:T(8,128)S(1)} %add.55.refs_0_), channel_id=1, source_target_pairs={{0,6},{2,4},{4,2},{6,0},{1,7},{3,5},{5,3},{7,1},{8,14},{10,12},{12... | collective-permute-start | bytes 393224 | tf_op jit(solution)/shard_map/ppermute | solution.py:402
  54.9 4.2 %collective-permute-done.14.refs_2_ = f32[256,128]{1,0:T(8,128)S(1)} collective-permute-done((f32[256,128]{1,0:T(8,128)S(1)}, f32[256,128]{1,0:T(8,128)S(1)}, u32[]{:S(2)}, u32[]{:S(2)}) %collective-permute-start.14) | collective-permute-done | bytes 131104 | tf_op jit(solution)/shard_map/ppermute | solution.py:402
  59.1 2.2 %collective-permute-done.7 = f32[256,1024]{1,0:T(8,128)S(1)} collective-permute-done((f32[256,1024]{1,0:T(8,128)}, f32[256,1024]{1,0:T(8,128)S(1)}, u32[]{:S(2)}, u32[]{:S(2)}) %collective-permute-start.7) | collective-permute-done | bytes 1048608 | tf_op jit(solution)/shard_map/ppermute | solution.py:377
  70.3 1.8 %shard_map.40 = (f32[256,128]{1,0:T(8,128)S(1)}, f32[256,128]{1,0:T(8,128)S(1)}) custom-call(s32[4]{0:T(128)S(1)} %pad_add_fusion.flags_ref, bf16[512,2048]{1,0:T(8,128)(2,1)S(1)} %get-tuple-element.80.refs_0_, bf16[512,2048]{1,0:T(8,128)(2,1)S(1)} %get-tuple-element.81.refs_1_, f32[128,2048]{1,0:T(8,128)S(1)} %collective-permute-done.9.refs_2_), custom_call_target="tpu_custom_call" | custom-call | tf_op jit(solution)/shard_map/pallas_call | solution.py:197
  72.2 3.0 %collective-permute-done.21 = f32[256,256]{1,0:T(8,128)S(1)} collective-permute-done((f32[256,256]{1,0:T(8,128)S(1)}, f32[256,256]{1,0:T(8,128)S(1)}, u32[]{:S(2)}, u32[]{:S(2)}) %collective-permute-start.21) | collective-permute-done | bytes 262176 | tf_op jit(solution)/shard_map/ppermute | solution.py:383
  80.4 2.0 %collective-permute-done.25.refs_9_.refs_6_ = f32[256,256]{1,0:T(8,128)S(1)} collective-permute-done((f32[256,256]{1,0:T(8,128)S(1)}, f32[256,256]{1,0:T(8,128)S(1)}, u32[]{:S(2)}, u32[]{:S(2)}) %collective-permute-start.25) | collective-permute-done | bytes 262176 | tf_op jit(solution)/shard_map/ppermute | solution.py:390
  84.2 3.9 %shard_map.42 = (f32[512,1024]{1,0:T(8,128)S(1)}, f32[8,128]{1,0:T(8,128)S(1)}) custom-call(s32[4]{0:T(128)S(1)} %pad_add_fusion.flags_ref, f32[256,128]{1,0:T(8,128)S(1)} %add.55.refs_0_, f32[256,128]{1,0:T(8,128)S(1)} %collective-permute-done.13.refs_1_, f32[256,128]{1,0:T(8,128)S(1)} %collective-permute-done.14.refs_2_, ...), custom_call_target="tpu_custom_call" | custom-call | tf_op jit(solution)/shard_map/pallas_call | solution.py:230
  88.1 7.9 %collective-permute-done.20 = f32[256,128]{1,0:T(8,128)S(1)} collective-permute-done((f32[256,128]{1,0:T(8,128)S(1)}, f32[256,128]{1,0:T(8,128)S(1)}, u32[]{:S(2)}, u32[]{:S(2)}) %collective-permute-start.20) | collective-permute-done | bytes 131104 | tf_op jit(solution)/shard_map/ppermute | solution.py:377
  103.6 5.3 %collective-permute-done.28 = f32[256,256]{1,0:T(8,128)S(1)} collective-permute-done((f32[256,256]{1,0:T(8,128)S(1)}, f32[256,256]{1,0:T(8,128)S(1)}, u32[]{:S(2)}, u32[]{:S(2)}) %collective-permute-start.28) | collective-permute-done | bytes 262176 | tf_op jit(solution)/shard_map/ppermute | solution.py:383
  110.2 1.8 %shard_map.44 = (f32[256,128]{1,0:T(8,128)S(1)}, f32[256,128]{1,0:T(8,128)S(1)}) custom-call(s32[4]{0:T(128)S(1)} %pad_add_fusion.flags_ref, bf16[512,2048]{1,0:T(8,128)(2,1)S(1)} %get-tuple-element.80.refs_0_, bf16[512,2048]{1,0:T(8,128)(2,1)S(1)} %get-tuple-element.81.refs_1_, f32[128,2048]{1,0:T(8,128)S(1)} %collective-permute-done.17.refs_2_), custom_call_target="tpu_custom_call" | custom-call | tf_op jit(solution)/shard_map/pallas_call | solution.py:197
  115.6 8.2 %collective-permute-done.32.refs_2_ = f32[128,2048]{1,0:T(8,128)S(1)} collective-permute-done((f32[128,2048]{1,0:T(8,128)S(1)}, f32[128,2048]{1,0:T(8,128)S(1)}, u32[]{:S(2)}, u32[]{:S(2)}) %collective-permute-start.32) | collective-permute-done | bytes 1048608 | tf_op jit(solution)/shard_map/ppermute | solution.py:377
  123.8 2.4 %collective-permute-start.46 = (f32[256,128]{1,0:T(8,128)S(1)}, f32[256,128]{1,0:T(8,128)S(1)}, u32[]{:S(2)}, u32[]{:S(2)}) collective-permute-start(f32[256,128]{1,0:T(8,128)S(1)} %broadcast_select_fusion.2.refs_0_), channel_id=1, source_target_pairs={{3,0},{7,1},{1,2},{5,3},{2,4},{6,5},{0,6},{4,7},{14,8},{15,9},{12,... | collective-permute-start | bytes 393224 | tf_op jit(solution)/shard_map/ppermute | solution.py:406
  126.9 1.8 %shard_map.45 = (f32[256,128]{1,0:T(8,128)S(1)}, f32[256,128]{1,0:T(8,128)S(1)}) custom-call(s32[4]{0:T(128)S(1)} %pad_add_fusion.flags_ref, bf16[512,2048]{1,0:T(8,128)(2,1)S(1)} %get-tuple-element.80.refs_0_, bf16[512,2048]{1,0:T(8,128)(2,1)S(1)} %get-tuple-element.81.refs_1_, f32[128,2048]{1,0:T(8,128)S(1)} %collective-permute-done.32.refs_2_, ...), custom_call_target="tpu_custom_call" | custom-call | tf_op jit(solution)/shard_map/pallas_call | solution.py:197
  128.7 2.1 %collective-permute-start.42 = (f32[256,256]{1,0:T(8,128)S(1)}, f32[256,256]{1,0:T(8,128)S(1)}, u32[]{:S(2)}, u32[]{:S(2)}) collective-permute-start(f32[256,256]{1,0:T(8,128)S(1)} %add.61.refs_13_), channel_id=1, source_target_pairs={{0,4},{2,6},{4,0},{6,2},{1,5},{3,7},{5,1},{7,3},{8,12},{10,14},{12... | collective-permute-start | bytes 786440 | tf_op jit(solution)/shard_map/ppermute | solution.py:390
  134.6 3.1 %collective-permute-done.42.refs_14_ = f32[256,256]{1,0:T(8,128)S(1)} collective-permute-done((f32[256,256]{1,0:T(8,128)S(1)}, f32[256,256]{1,0:T(8,128)S(1)}, u32[]{:S(2)}, u32[]{:S(2)}) %collective-permute-start.42) | collective-permute-done | bytes 262176 | tf_op jit(solution)/shard_map/ppermute | solution.py:390
  138.4 1.7 %collective-permute-done.43.refs_16_ = f32[256,256]{1,0:T(8,128)S(1)} collective-permute-done((f32[256,256]{1,0:T(8,128)S(1)}, f32[256,256]{1,0:T(8,128)S(1)}, u32[]{:S(2)}, u32[]{:S(2)}) %collective-permute-start.43) | collective-permute-done | bytes 262176 | tf_op jit(solution)/shard_map/ppermute | solution.py:392
  140.6 1.9 %collective-permute-done.34.refs_1_ = f32[256,128]{1,0:T(8,128)S(1)} collective-permute-done((f32[256,128]{1,0:T(8,128)S(1)}, f32[256,128]{1,0:T(8,128)S(1)}, u32[]{:S(2)}, u32[]{:S(2)}) %collective-permute-start.34) | collective-permute-done | bytes 131104 | tf_op jit(solution)/shard_map/ppermute | solution.py:406
  142.5 2.2 %collective-permute-start.41 = (f32[256,128]{1,0:T(8,128)S(1)}, f32[256,128]{1,0:T(8,128)S(1)}, u32[]{:S(2)}, u32[]{:S(2)}) collective-permute-start(f32[256,128]{1,0:T(8,128)S(1)} %add.64.refs_5_), channel_id=1, source_target_pairs={{0,6},{2,4},{4,2},{6,0},{1,7},{3,5},{5,3},{7,1},{8,14},{10,12},{12... | collective-permute-start | bytes 393224 | tf_op jit(solution)/shard_map/ppermute | solution.py:402
  144.7 4.3 %shard_map.46 = (f32[512,1024]{1,0:T(8,128)S(1)}, f32[8,128]{1,0:T(8,128)S(1)}) custom-call(s32[4]{0:T(128)S(1)} %pad_add_fusion.flags_ref, f32[256,128]{1,0:T(8,128)S(1)} %broadcast_select_fusion.2.refs_0_, f32[256,128]{1,0:T(8,128)S(1)} %collective-permute-done.44.refs_1_, f32[256,128]{1,0:T(8,128)S(1)} %collective-permute-done.45.refs_2_, ...), custom_call_target="tpu_custom_call" | custom-call | tf_op jit(solution)/shard_map/pallas_call | solution.py:230
  149.0 2.1 %collective-permute-done.40.refs_7_ = f32[256,128]{1,0:T(8,128)S(1)} collective-permute-done((f32[256,128]{1,0:T(8,128)S(1)}, f32[256,128]{1,0:T(8,128)S(1)}, u32[]{:S(2)}, u32[]{:S(2)}) %collective-permute-start.40) | collective-permute-done | bytes 131104 | tf_op jit(solution)/shard_map/ppermute | solution.py:402
  153.9 2.6 %collective-permute-start.50 = (f32[8,128]{1,0:T(8,128)S(1)}, f32[8,128]{1,0:T(8,128)S(1)}, u32[]{:S(2)}, u32[]{:S(2)}) collective-permute-start(f32[8,128]{1,0:T(8,128)S(1)} %add.65.refs_0_), channel_id=1, source_target_pairs={{0,16},{8,24},{16,0},{24,8},{1,17},{9,25},{17,1},{25,9},{2,18},{10... | collective-permute-start | bytes 12296 | tf_op jit(solution)/shard_map/ppermute | solution.py:453
  158.7 2.4 %shard_map.48.up_ref = f32[256,1024]{1,0:T(8,128)S(1)} custom-call(s32[4]{0:T(128)S(1)} %pad_add_fusion.flags_ref, f32[256,256]{1,0:T(8,128)S(1)} %get-tuple-element.137.refs_0_, f32[256,256]{1,0:T(8,128)S(1)} %get-tuple-element.138.refs_1_, f32[256,256]{1,0:T(8,128)S(1)} %get-tuple-element.139.refs_2_, f32[256,256]{1,0:T(8,128)S(1)} %get-tuple-element.140.refs_3_, ...), custom_call_target="tpu_custom_call" | custom-call | tf_op jit(solution)/shard_map/pallas_call | solution.py:114
  161.1 1.8 %shard_map.49 = f32[256,1024]{1,0:T(8,128)} custom-call(s32[4]{0:T(128)S(1)} %pad_add_fusion.flags_ref, f32[256,1024]{1,0:T(8,128)S(1)} %shard_map.48.up_ref, f32[512,1024]{1,0:T(8,128)S(1)} %get-tuple-element.141.refs_8_.prod_ref, f32[1,1]{1,0:T(1,128)} %bitcast.5.norm_ref, f32[8,128]{1,0:T(8,128)S(1)} %add.65.refs_0_, ...), custom_call_target="tpu_custom_call" | custom-call | tf_op jit(solution)/shard_map/pallas_call | solution.py:114
  (109 shorter events, 59.4 us)
Async XLA Ops:
  1.4 27.6 %collective-permute-start = (f32[256,1024]{1,0:T(8,128)S(1)}, f32[256,1024]{1,0:T(8,128)}, u32[]{:S(2)}, u32[]{:S(2)}) collective-permute-start(f32[256,1024]{1,0:T(8,128)S(1)} %constant_dynamic-slice_fusion.1.own_ref), channel_id=1, source_target_pairs={{0,8},{8,0},{16,24},{24,16},{1,9},{9,1},{17,25},{25,17},{2,10},{10... | collective-permute-start | bytes 3145736 | tf_op jit(solution)/shard_map/ppermute | solution.py:377
  4.5 24.5 %collective-permute-start.1 = (f32[256,1024]{1,0:T(8,128)S(1)}, f32[256,1024]{1,0:T(8,128)}, u32[]{:S(2)}, u32[]{:S(2)}) collective-permute-start(f32[256,1024]{1,0:T(8,128)S(1)} %constant_dynamic-slice_fusion.1.own_ref), channel_id=1, source_target_pairs={{8,16},{16,8},{9,17},{17,9},{10,18},{18,10},{11,19},{19,11},{12,20... | collective-permute-start | bytes 3145736 | tf_op jit(solution)/shard_map/ppermute | solution.py:377
  10.0 9.2 %collective-permute-start.4 = (f32[256,256]{1,0:T(8,128)S(1)}, f32[256,256]{1,0:T(8,128)}, u32[]{:S(2)}, u32[]{:S(2)}) collective-permute-start(f32[256,256]{1,0:T(8,128)S(1)} %get-tuple-element.75), channel_id=1, source_target_pairs={{0,4},{2,6},{4,0},{6,2},{1,5},{3,7},{5,1},{7,3},{8,12},{10,14},{12... | collective-permute-start | bytes 786440 | tf_op jit(solution)/shard_map/ppermute | solution.py:384
  17.7 11.3 %collective-permute-start.3 = (f32[256,256]{1,0:T(8,128)S(1)}, f32[256,256]{1,0:T(8,128)S(1)}, u32[]{:S(2)}, u32[]{:S(2)}) collective-permute-start(f32[256,256]{1,0:T(8,128)S(1)} %add.53.refs_4_), channel_id=1, source_target_pairs={{0,4},{2,6},{4,0},{6,2},{1,5},{3,7},{5,1},{7,3},{8,12},{10,14},{12... | collective-permute-start | bytes 786440 | tf_op jit(solution)/shard_map/ppermute | solution.py:390
  20.3 8.8 %collective-permute-start.5 = (f32[256,256]{1,0:T(8,128)S(1)}, f32[256,256]{1,0:T(8,128)S(1)}, u32[]{:S(2)}, u32[]{:S(2)}) collective-permute-start(f32[256,256]{1,0:T(8,128)S(1)} %add.54.refs_6_), channel_id=1, source_target_pairs={{0,2},{2,0},{4,6},{6,4},{1,3},{3,1},{5,7},{7,5},{8,10},{10,8},{12,... | collective-permute-start | bytes 786440 | tf_op jit(solution)/shard_map/ppermute | solution.py:392
  29.0 12.1 %collective-permute-start.10 = (f32[256,1024]{1,0:T(8,128)}, f32[256,1024]{1,0:T(8,128)S(1)}, u32[]{:S(2)}, u32[]{:S(2)}) collective-permute-start(f32[256,1024]{1,0:T(8,128)} %collective-permute-done.first_ref.refs_13_.refs_17_), channel_id=1, source_target_pairs={{0,1},{1,0},{2,3},{3,2},{4,5},{5,4},{6,7},{7,6},{8,9},{9,8},{10,11... | collective-permute-start | bytes 3145736 | tf_op jit(solution)/shard_map/ppermute | solution.py:380
  29.3 32.0 %collective-permute-start.8 = (f32[256,1024]{1,0:T(8,128)}, f32[256,1024]{1,0:T(8,128)S(1)}, u32[]{:S(2)}, u32[]{:S(2)}) collective-permute-start(f32[256,1024]{1,0:T(8,128)} %collective-permute-done.first_ref.refs_13_.refs_17_), channel_id=1, source_target_pairs={{8,16},{16,8},{9,17},{17,9},{10,18},{18,10},{11,19},{19,11},{12,20... | collective-permute-start | bytes 3145736 | tf_op jit(solution)/shard_map/ppermute | solution.py:377
  30.0 31.3 %collective-permute-start.7 = (f32[256,1024]{1,0:T(8,128)}, f32[256,1024]{1,0:T(8,128)S(1)}, u32[]{:S(2)}, u32[]{:S(2)}) collective-permute-start(f32[256,1024]{1,0:T(8,128)} %collective-permute-done.1), channel_id=1, source_target_pairs={{8,0},{16,24},{9,1},{17,25},{10,2},{18,26},{11,3},{19,27},{12,4},{... | collective-permute-start | bytes 3145736 | tf_op jit(solution)/shard_map/ppermute | solution.py:377
  31.3 31.0 %collective-permute-start.9 = (f32[128,2048]{1,0:T(8,128)S(1)}, f32[128,2048]{1,0:T(8,128)S(1)}, u32[]{:S(2)}, u32[]{:S(2)}) collective-permute-start(f32[128,2048]{1,0:T(8,128)S(1)} %constant_dynamic-slice_fusion.refs_1_), channel_id=1, source_target_pairs={{0,8},{24,16},{1,9},{25,17},{2,10},{26,18},{3,11},{27,19},{4,12},{... | collective-permute-start | bytes 3145736 | tf_op jit(solution)/shard_map/ppermute | solution.py:377
  62.5 33.5 %collective-permute-start.17 = (f32[128,2048]{1,0:T(8,128)S(1)}, f32[128,2048]{1,0:T(8,128)S(1)}, u32[]{:S(2)}, u32[]{:S(2)}) collective-permute-start(f32[128,2048]{1,0:T(8,128)S(1)} %collective-permute-done.9.refs_2_), channel_id=1, source_target_pairs={{8,16},{16,8},{9,17},{17,9},{10,18},{18,10},{11,19},{19,11},{12,20... | collective-permute-start | bytes 3145736 | tf_op jit(solution)/shard_map/ppermute | solution.py:377
  63.2 32.8 %collective-permute-start.16 = (f32[256,1024]{1,0:T(8,128)S(1)}, f32[256,1024]{1,0:T(8,128)S(1)}, u32[]{:S(2)}, u32[]{:S(2)}) collective-permute-start(f32[256,1024]{1,0:T(8,128)S(1)} %collective-permute-done.8), channel_id=1, source_target_pairs={{8,0},{16,24},{9,1},{17,25},{10,2},{18,26},{11,3},{19,27},{12,4},{... | collective-permute-start | bytes 3145736 | tf_op jit(solution)/shard_map/ppermute | solution.py:377
  66.8 8.4 %collective-permute-start.21 = (f32[256,256]{1,0:T(8,128)S(1)}, f32[256,256]{1,0:T(8,128)S(1)}, u32[]{:S(2)}, u32[]{:S(2)}) collective-permute-start(f32[256,256]{1,0:T(8,128)S(1)} %get-tuple-element.95), channel_id=1, source_target_pairs={{0,2},{2,0},{4,6},{6,4},{1,3},{3,1},{5,7},{7,5},{8,10},{10,8},{12,... | collective-permute-start | bytes 786440 | tf_op jit(solution)/shard_map/ppermute | solution.py:383
  68.3 9.2 %collective-permute-start.23 = (f32[256,256]{1,0:T(8,128)S(1)}, f32[256,256]{1,0:T(8,128)S(1)}, u32[]{:S(2)}, u32[]{:S(2)}) collective-permute-start(f32[256,256]{1,0:T(8,128)S(1)} %get-tuple-element.96), channel_id=1, source_target_pairs={{0,4},{2,6},{4,0},{6,2},{1,5},{3,7},{5,1},{7,3},{8,12},{10,14},{12... | collective-permute-start | bytes 786440 | tf_op jit(solution)/shard_map/ppermute | solution.py:384
  69.8 12.5 %collective-permute-start.25 = (f32[256,256]{1,0:T(8,128)S(1)}, f32[256,256]{1,0:T(8,128)S(1)}, u32[]{:S(2)}, u32[]{:S(2)}) collective-permute-start(f32[256,256]{1,0:T(8,128)S(1)} %add.56.refs_8_.refs_5_), channel_id=1, source_target_pairs={{0,4},{2,6},{4,0},{6,2},{1,5},{3,7},{5,1},{7,3},{8,12},{10,14},{12... | collective-permute-start | bytes 786440 | tf_op jit(solution)/shard_map/ppermute | solution.py:390
  78.9 17.2 %collective-permute-start.22 = (f32[256,256]{1,0:T(8,128)S(1)}, f32[256,256]{1,0:T(8,128)S(1)}, u32[]{:S(2)}, u32[]{:S(2)}) collective-permute-start(f32[256,256]{1,0:T(8,128)S(1)} %add.59.refs_9_), channel_id=1, source_target_pairs={{0,4},{2,6},{4,0},{6,2},{1,5},{3,7},{5,1},{7,3},{8,12},{10,14},{12... | collective-permute-start | bytes 786440 | tf_op jit(solution)/shard_map/ppermute | solution.py:390
  82.3 13.7 %collective-permute-start.24 = (f32[256,256]{1,0:T(8,128)S(1)}, f32[256,256]{1,0:T(8,128)S(1)}, u32[]{:S(2)}, u32[]{:S(2)}) collective-permute-start(f32[256,256]{1,0:T(8,128)S(1)} %add.60.refs_11_), channel_id=1, source_target_pairs={{0,2},{2,0},{4,6},{6,4},{1,3},{3,1},{5,7},{7,5},{8,10},{10,8},{12,... | collective-permute-start | bytes 786440 | tf_op jit(solution)/shard_map/ppermute | solution.py:392
  82.9 13.1 %collective-permute-start.20 = (f32[256,128]{1,0:T(8,128)S(1)}, f32[256,128]{1,0:T(8,128)S(1)}, u32[]{:S(2)}, u32[]{:S(2)}) collective-permute-start(f32[256,128]{1,0:T(8,128)S(1)} %add.58), channel_id=1, source_target_pairs={{8,0},{16,24},{9,1},{17,25},{10,2},{18,26},{11,3},{19,27},{12,4},{... | collective-permute-start | bytes 393224 | tf_op jit(solution)/shard_map/ppermute | solution.py:377
  96.3 27.4 %collective-permute-start.32 = (f32[128,2048]{1,0:T(8,128)S(1)}, f32[128,2048]{1,0:T(8,128)S(1)}, u32[]{:S(2)}, u32[]{:S(2)}) collective-permute-start(f32[128,2048]{1,0:T(8,128)S(1)} %collective-permute-done.17.refs_2_), channel_id=1, source_target_pairs={{8,0},{16,24},{9,1},{17,25},{10,2},{18,26},{11,3},{19,27},{12,4},{... | collective-permute-start | bytes 3145736 | tf_op jit(solution)/shard_map/ppermute | solution.py:377
  97.6 28.6 %collective-permute-start.33 = (f32[128,2048]{1,0:T(8,128)S(1)}, f32[128,2048]{1,0:T(8,128)S(1)}, u32[]{:S(2)}, u32[]{:S(2)}) collective-permute-start(f32[128,2048]{1,0:T(8,128)S(1)} %constant_dynamic-slice_fusion.refs_1_), channel_id=1, source_target_pairs={{8,16},{16,8},{9,17},{17,9},{10,18},{18,10},{11,19},{19,11},{12,20... | collective-permute-start | bytes 3145736 | tf_op jit(solution)/shard_map/ppermute | solution.py:377
  100.5 8.4 %collective-permute-start.28 = (f32[256,256]{1,0:T(8,128)S(1)}, f32[256,256]{1,0:T(8,128)S(1)}, u32[]{:S(2)}, u32[]{:S(2)}) collective-permute-start(f32[256,256]{1,0:T(8,128)S(1)} %get-tuple-element.112), channel_id=1, source_target_pairs={{0,2},{2,0},{4,6},{6,4},{1,3},{3,1},{5,7},{7,5},{8,10},{10,8},{12,... | collective-permute-start | bytes 786440 | tf_op jit(solution)/shard_map/ppermute | solution.py:383
  112.1 16.6 %collective-permute-start.44 = (f32[256,128]{1,0:T(8,128)S(1)}, f32[256,128]{1,0:T(8,128)S(1)}, u32[]{:S(2)}, u32[]{:S(2)}) collective-permute-start(f32[256,128]{1,0:T(8,128)S(1)} %broadcast_select_fusion.2.refs_0_), channel_id=1, source_target_pairs={{2,0},{6,1},{0,2},{4,3},{3,4},{7,5},{1,6},{5,7},{10,8},{11,9},{8,1... | collective-permute-start | bytes 393224 | tf_op jit(solution)/shard_map/ppermute | solution.py:406
  112.7 18.1 %collective-permute-start.45 = (f32[256,128]{1,0:T(8,128)S(1)}, f32[256,128]{1,0:T(8,128)S(1)}, u32[]{:S(2)}, u32[]{:S(2)}) collective-permute-start(f32[256,128]{1,0:T(8,128)S(1)} %broadcast_select_fusion.2.refs_0_), channel_id=1, source_target_pairs={{1,0},{5,1},{3,2},{7,3},{0,4},{4,5},{2,6},{6,7},{12,8},{13,9},{14,... | collective-permute-start | bytes 393224 | tf_op jit(solution)/shard_map/ppermute | solution.py:406
  114.3 17.1 %collective-permute-start.31 = (f32[256,128]{1,0:T(8,128)S(1)}, f32[256,128]{1,0:T(8,128)S(1)}, u32[]{:S(2)}, u32[]{:S(2)}) collective-permute-start(f32[256,128]{1,0:T(8,128)S(1)} %add.63), channel_id=1, source_target_pairs={{16,0},{8,24},{17,1},{9,25},{18,2},{10,26},{19,3},{11,27},{20,4},{... | collective-permute-start | bytes 393224 | tf_op jit(solution)/shard_map/ppermute | solution.py:377
  128.7 9.0 %collective-permute-start.42 = (f32[256,256]{1,0:T(8,128)S(1)}, f32[256,256]{1,0:T(8,128)S(1)}, u32[]{:S(2)}, u32[]{:S(2)}) collective-permute-start(f32[256,256]{1,0:T(8,128)S(1)} %add.61.refs_13_), channel_id=1, source_target_pairs={{0,4},{2,6},{4,0},{6,2},{1,5},{3,7},{5,1},{7,3},{8,12},{10,14},{12... | collective-permute-start | bytes 786440 | tf_op jit(solution)/shard_map/ppermute | solution.py:390
  130.8 9.2 %collective-permute-start.43 = (f32[256,256]{1,0:T(8,128)S(1)}, f32[256,256]{1,0:T(8,128)S(1)}, u32[]{:S(2)}, u32[]{:S(2)}) collective-permute-start(f32[256,256]{1,0:T(8,128)S(1)} %add.62.refs_15_), channel_id=1, source_target_pairs={{0,2},{2,0},{4,6},{6,4},{1,3},{3,1},{5,7},{7,5},{8,10},{10,8},{12,... | collective-permute-start | bytes 786440 | tf_op jit(solution)/shard_map/ppermute | solution.py:392
  131.4 11.1 %collective-permute-start.34 = (f32[256,128]{1,0:T(8,128)S(1)}, f32[256,128]{1,0:T(8,128)S(1)}, u32[]{:S(2)}, u32[]{:S(2)}) collective-permute-start(f32[256,128]{1,0:T(8,128)S(1)} %broadcast_select_fusion.3.refs_0_), channel_id=1, source_target_pairs={{2,0},{6,1},{0,2},{4,3},{3,4},{7,5},{1,6},{5,7},{10,8},{11,9},{8,1... | collective-permute-start | bytes 393224 | tf_op jit(solution)/shard_map/ppermute | solution.py:406
  133.0 9.6 %collective-permute-start.35 = (f32[256,128]{1,0:T(8,128)S(1)}, f32[256,128]{1,0:T(8,128)S(1)}, u32[]{:S(2)}, u32[]{:S(2)}) collective-permute-start(f32[256,128]{1,0:T(8,128)S(1)} %broadcast_select_fusion.3.refs_0_), channel_id=1, source_target_pairs={{1,0},{5,1},{3,2},{7,3},{0,4},{4,5},{2,6},{6,7},{12,8},{13,9},{14,... | collective-permute-start | bytes 393224 | tf_op jit(solution)/shard_map/ppermute | solution.py:406
  134.6 14.4 %collective-permute-start.36 = (f32[256,128]{1,0:T(8,128)S(1)}, f32[256,128]{1,0:T(8,128)S(1)}, u32[]{:S(2)}, u32[]{:S(2)}) collective-permute-start(f32[256,128]{1,0:T(8,128)S(1)} %broadcast_select_fusion.3.refs_0_), channel_id=1, source_target_pairs={{3,0},{7,1},{1,2},{5,3},{2,4},{6,5},{0,6},{4,7},{14,8},{15,9},{12,... | collective-permute-start | bytes 393224 | tf_op jit(solution)/shard_map/ppermute | solution.py:406
  137.7 11.2 %collective-permute-start.37 = (f32[256,128]{1,0:T(8,128)S(1)}, f32[256,128]{1,0:T(8,128)S(1)}, u32[]{:S(2)}, u32[]{:S(2)}) collective-permute-start(f32[256,128]{1,0:T(8,128)S(1)} %broadcast_select_fusion.3.refs_0_), channel_id=1, source_target_pairs={{0,0},{4,1},{2,2},{6,3},{1,4},{5,5},{3,6},{7,7},{24,24},{28,25},{2... | collective-permute-start | bytes 393224 | tf_op jit(solution)/shard_map/ppermute | solution.py:406
  140.1 8.9 %collective-permute-start.39 = (f32[256,128]{1,0:T(8,128)S(1)}, f32[256,128]{1,0:T(8,128)S(1)}, u32[]{:S(2)}, u32[]{:S(2)}) collective-permute-start(f32[256,128]{1,0:T(8,128)S(1)} %add.64.refs_5_), channel_id=1, source_target_pairs={{0,2},{2,0},{4,6},{6,4},{1,3},{3,1},{5,7},{7,5},{8,10},{10,8},{12,... | collective-permute-start | bytes 393224 | tf_op jit(solution)/shard_map/ppermute | solution.py:402
  142.5 8.5 %collective-permute-start.40 = (f32[256,128]{1,0:T(8,128)S(1)}, f32[256,128]{1,0:T(8,128)S(1)}, u32[]{:S(2)}, u32[]{:S(2)}) collective-permute-start(f32[256,128]{1,0:T(8,128)S(1)} %add.64.refs_5_), channel_id=1, source_target_pairs={{0,4},{2,6},{4,0},{6,2},{1,5},{3,7},{5,1},{7,3},{8,12},{10,14},{12... | collective-permute-start | bytes 393224 | tf_op jit(solution)/shard_map/ppermute | solution.py:402
  142.5 8.5 %collective-permute-start.41 = (f32[256,128]{1,0:T(8,128)S(1)}, f32[256,128]{1,0:T(8,128)S(1)}, u32[]{:S(2)}, u32[]{:S(2)}) collective-permute-start(f32[256,128]{1,0:T(8,128)S(1)} %add.64.refs_5_), channel_id=1, source_target_pairs={{0,6},{2,4},{4,2},{6,0},{1,7},{3,5},{5,3},{7,1},{8,14},{10,12},{12... | collective-permute-start | bytes 393224 | tf_op jit(solution)/shard_map/ppermute | solution.py:402
  (22 other events, 116.4 us)
